TPU v7x, 32 devices: a whole 2x2x4 slice. The times are simulated.
32 devices in a mesh: dp: 16 (over z, x, core), tensor: 2 (over y).
Axes of the slice: x: 2, y: 2, z: 4, core: 2. Of those that a mesh axis runs over, the one named last changes fastest.
Arguments:
- tokens: bfloat16 [16384, 1024], P('dp'), may hold values from -6 to 6
- doc_ids: int32 [16384], replicated, may hold values from 0 to 39, as said below
- routes: int32 [16384, 8], P('dp'), may hold values from 0 to 31, all different within a row; in each aligned block of 1024 rows (0 to 1023, 1024 to 2047, ...) at most 384 rows name the same one
- attention_gain: bfloat16 [1024], replicated, may hold values from 0.5 to 1.5
- w_query: bfloat16 [1024, 1024], P(None, 'tensor'), may hold values from -0.75 to 0.75
- w_key: bfloat16 [512, 1024], P('tensor'), may hold values from -0.75 to 0.75
- w_value: bfloat16 [512, 1024], P('tensor'), may hold values from -0.1875 to 0.1875
- w_out: bfloat16 [1024, 1024], P('tensor'), may hold values from -4 to 4
- mixture_gain: bfloat16 [1024], replicated, may hold values from 0.5 to 1.5
- w_router: bfloat16 [1024, 32], replicated, may hold values from -0.09375 to 0.09375
- expert_gate_up: bfloat16 [32, 2, 512, 1024], P(None, None, 'tensor'), may hold values from -0.1875 to 0.1875
- expert_down: bfloat16 [32, 512, 1024], P(None, 'tensor'), may hold values from -4 to 4
- out_cotangent: bfloat16 [16384, 1024], P('dp'), may hold values from -6 to 6
Outputs:
- mixed: bfloat16 [16384, 1024], P('dp')
- tokens_gradient: bfloat16 [16384, 1024], P('dp')
- attention_gain_gradient: float32 [1024], replicated
- w_query_gradient: float32 [1024, 1024], P(None, 'tensor')
- w_key_gradient: float32 [512, 1024], P('tensor')
- w_value_gradient: float32 [512, 1024], P('tensor')
- w_out_gradient: float32 [1024, 1024], P('tensor')
- mixture_gain_gradient: float32 [1024], replicated
- w_router_gradient: float32 [1024, 32], replicated
- expert_gate_up_gradient: float32 [32, 2, 512, 1024], P('dp', None, 'tensor')
- expert_down_gradient: float32 [32, 512, 1024], P('dp', 'tensor')
Inputs may be any that keep to these rules, and one draw needn't show every extreme that they name: doc_ids never fall along the tokens; every sequence of 2048 tokens begins with a new number and holds exactly five documents. `routes`: each token names 8 different experts; in each aligned block of 1024 tokens no expert is named by more than 384 tokens.
All inputs are finite; a program needn't handle non-finite values.
Results may differ from a plain program's by a relative error of at most 0.025.
Values may be sent and summed in bfloat16 or wider, within the bound.
No kernel may reach another device: no remote copies, remote signals or barrier semaphores. Data moves between devices by JAX's collectives and lax.ppermute only.
A program may use at most 448 MiB of HBM per device.

v0:
```python
import jax
import jax.numpy as jnp
from jax import lax
from jax.sharding import PartitionSpec as P

HEAD_DIM = 64
EXPERTS = 32
TOP = 8
SEQ_LEN = 2048
CAP = 384


epsilon = 1e-06
score_scale = 0.015625
residual_scale = 0.22
rope_base = 10000.0
masked_value = -1e30
highest = lax.Precision.HIGHEST


def passed_along(shard, axis, by):
    peers = lax.axis_size(axis)
    pairs = [(i, i + by) for i in range(peers) if 0 <= i + by < peers]
    return lax.ppermute(shard, axis, pairs)


def norm_rows(values, gain):
    return values * lax.rsqrt(jnp.mean(values * values, axis=-1, keepdims=True) + epsilon) * gain


def rotate(values, position):
    width = values.shape[-1]
    half = width // 2
    inverse = rope_base ** (-2.0 * jnp.arange(half, dtype=jnp.float32) / width)
    angle = position.astype(jnp.float32)[:, None] * inverse[None, :]
    cosine = jnp.concatenate([jnp.cos(angle), jnp.cos(angle)], axis=-1)[:, None, :]
    sine = jnp.concatenate([jnp.sin(angle), jnp.sin(angle)], axis=-1)[:, None, :]
    turned = jnp.concatenate([-values[..., half:], values[..., :half]], axis=-1)
    return values * cosine + turned * sine


def slot_tables(routes):
    pairs = routes.shape[0] * routes.shape[1]
    flat = routes.reshape(-1)
    one_hot = (flat[:, None] == jnp.arange(EXPERTS, dtype=jnp.int32)[None, :]).astype(jnp.int32)
    earlier = jnp.sum((jnp.cumsum(one_hot, axis=0) - one_hot) * one_hot, axis=1)
    place = flat * CAP + earlier
    source = (
        jnp.full((EXPERTS * CAP,), pairs, jnp.int32)
        .at[place]
        .set(jnp.arange(pairs, dtype=jnp.int32))
    )
    return (place, source)


def inner_rows(left, right):
    return lax.dot_general(
        left, right, (((0,), (0,)), ((), ())), preferred_element_type=jnp.float32
    )


def times_transposed(left, right):
    return lax.dot_general(
        left, right, (((1,), (1,)), ((), ())), preferred_element_type=jnp.float32
    )


def expert_terms(rows_in, gate_up_in, slot_in, active_in):
    first_part = jnp.einsum(
        "ecjf,ecd->ejfd", gate_up_in, rows_in, preferred_element_type=jnp.float32
    )
    second_part = jnp.einsum("ecf,ecd->efd", active_in, slot_in, preferred_element_type=jnp.float32)
    return jnp.concatenate([first_part, second_part[:, None]], axis=1)


def on_device(
    tokens,
    doc_ids,
    routes,
    attention_gain,
    w_query,
    w_key,
    w_value,
    w_out,
    mixture_gain,
    w_router,
    expert_gate_up,
    expert_down,
    out_cotangent,
):
    rows = tokens.shape[0]
    width = tokens.shape[1]
    heads_here = w_query.shape[1] // HEAD_DIM
    pair_heads = w_key.shape[0] // HEAD_DIM
    group = heads_here // pair_heads
    split = pair_heads * HEAD_DIM
    span = SEQ_LEN // rows
    block = min(512, rows)
    count = rows // block
    device = lax.axis_index("dp")
    first = device * rows
    query_place = first + jnp.arange(rows, dtype=jnp.int32)
    position = query_place % SEQ_LEN
    query_doc = lax.dynamic_slice_in_dim(doc_ids, first, rows)
    inputs = tokens.astype(jnp.float32)
    normed_attention, pull_first_norm = jax.vjp(
        norm_rows, inputs, attention_gain.astype(jnp.float32)
    )
    normed_attention = normed_attention.astype(jnp.bfloat16)
    query_lin = jnp.dot(normed_attention, w_query, preferred_element_type=jnp.float32).reshape(
        rows, heads_here, HEAD_DIM
    )
    key_lin = times_transposed(normed_attention, w_key).reshape(rows, pair_heads, HEAD_DIM)
    value_lin = times_transposed(normed_attention, w_value)
    query_rot, pull_query = jax.vjp(lambda values: rotate(values, position), query_lin)
    key_rot, pull_key = jax.vjp(lambda values: rotate(values, position), key_lin)
    query_low = query_rot.astype(jnp.bfloat16)
    pair_low = jnp.concatenate([key_rot.reshape(rows, split), value_lin], axis=1).astype(
        jnp.bfloat16
    )
    blocks = [pair_low]
    offset = 1
    blocks.append(passed_along(pair_low, "dp", offset))
    pair_all = jnp.concatenate(blocks, axis=0)
    key_all = pair_all[:, :split].reshape(span * rows, pair_heads, HEAD_DIM)
    value_all = pair_all[:, split:].reshape(span * rows, pair_heads, HEAD_DIM)
    key_place = jnp.concatenate(
        [(device - offset) * rows + jnp.arange(rows, dtype=jnp.int32) for offset in range(span)]
    )
    key_doc = jnp.concatenate(
        [
            lax.dynamic_slice_in_dim(doc_ids, jnp.maximum(device - offset, 0) * rows, rows)
            for offset in range(span)
        ]
    )

    def scores_of(query_block, place_block, doc_block):
        grouped = query_block.reshape(block, pair_heads, group, HEAD_DIM)
        raw = (
            jnp.einsum("qhgd,khd->hgqk", grouped, key_all, preferred_element_type=jnp.float32)
            * score_scale
        )
        allowed = (
            (key_place[None, :] <= place_block[:, None])
            & (key_place[None, :] >= 0)
            & (key_doc[None, :] == doc_block[:, None])
        )
        return (jnp.where(allowed[None, None], raw, masked_value), grouped)

    query_blocks = query_low.reshape(count, block, heads_here, HEAD_DIM)
    place_blocks = query_place.reshape(count, block)
    doc_blocks = query_doc.reshape(count, block)

    def forward_block(item):
        scores, grouped = scores_of(item[0], item[1], item[2])
        peak = jnp.max(scores, axis=-1, keepdims=True)
        total = jnp.sum(jnp.exp(scores - peak), axis=-1, keepdims=True)
        log_total = peak + jnp.log(total)
        probs = jnp.exp(scores - log_total).astype(jnp.bfloat16)
        context = jnp.einsum("hgqk,khd->qhgd", probs, value_all, preferred_element_type=jnp.float32)
        return (context.reshape(block, heads_here * HEAD_DIM), log_total)

    context, log_totals = lax.map(forward_block, (query_blocks, place_blocks, doc_blocks))
    context = context.reshape(rows, heads_here * HEAD_DIM).astype(jnp.bfloat16)
    attention_part = jnp.dot(context, w_out, preferred_element_type=jnp.float32)
    attention_out = lax.psum(attention_part.astype(jnp.bfloat16), "tensor").astype(jnp.float32)
    hidden = inputs + residual_scale * attention_out
    normed_mixture, pull_second_norm = jax.vjp(norm_rows, hidden, mixture_gain.astype(jnp.float32))
    normed_mixture = normed_mixture.astype(jnp.bfloat16)
    logits = jnp.dot(normed_mixture, w_router, preferred_element_type=jnp.float32)
    chosen_mask = (
        routes[:, :, None] == jnp.arange(EXPERTS, dtype=jnp.int32)[None, None, :]
    ).astype(jnp.float32)

    def gate_values(logit_rows):
        return jax.nn.softmax(jnp.sum(chosen_mask * logit_rows[:, None, :], axis=-1), axis=-1)

    gates, pull_gates = jax.vjp(gate_values, logits)
    place, source = slot_tables(routes)
    token_of = source // TOP
    padded = jnp.concatenate([normed_mixture, jnp.zeros((1, width), jnp.bfloat16)], axis=0)
    expert_rows = padded[token_of].reshape(EXPERTS, CAP, width)
    gate_up = jnp.einsum(
        "ecd,ejfd->ecjf", expert_rows, expert_gate_up, preferred_element_type=jnp.float32
    )

    def activate(values):
        return jax.nn.silu(values[:, :, 0]) * values[:, :, 1]

    active, pull_active = jax.vjp(activate, gate_up)
    active_low = active.astype(jnp.bfloat16)
    expert_out = jnp.einsum(
        "ecf,efd->ecd", active_low, expert_down, preferred_element_type=jnp.float32
    ).reshape(EXPERTS * CAP, width)
    picked = expert_out[place].reshape(rows, TOP, width)
    mixture_part = jnp.sum(gates[:, :, None] * picked, axis=1)
    mixture_out = lax.psum(mixture_part.astype(jnp.bfloat16), "tensor").astype(jnp.float32)
    mixed = (hidden + residual_scale * mixture_out).astype(jnp.bfloat16)
    upstream = out_cotangent.astype(jnp.float32)
    mixture_upstream = residual_scale * upstream
    gates_gradient = jnp.sum(picked * mixture_upstream[:, None, :], axis=-1)
    gate_padded = jnp.concatenate([gates.reshape(-1), jnp.zeros((1,), jnp.float32)])
    upstream_padded = jnp.concatenate(
        [mixture_upstream, jnp.zeros((1, width), jnp.float32)], axis=0
    )
    slot_gradient = (
        (upstream_padded[token_of] * gate_padded[source][:, None])
        .reshape(EXPERTS, CAP, width)
        .astype(jnp.bfloat16)
    )
    active_gradient = jnp.einsum(
        "ecd,efd->ecf", slot_gradient, expert_down, preferred_element_type=jnp.float32
    )
    gate_up_gradient = pull_active(active_gradient)[0].astype(jnp.bfloat16)
    rows_gradient = jnp.einsum(
        "ecjf,ejfd->ecd", gate_up_gradient, expert_gate_up, preferred_element_type=jnp.float32
    )
    normed_gradient = (
        jnp.zeros((rows + 1, width), jnp.float32)
        .at[token_of]
        .add(rows_gradient.reshape(-1, width))[:rows]
    )
    logits_gradient = pull_gates(gates_gradient)[0]
    router_float = w_router.astype(jnp.float32)
    normed_gradient = normed_gradient + lax.dot_general(
        logits_gradient, router_float, (((1,), (1,)), ((), ())), precision=highest
    )
    router_gradient = lax.dot_general(
        normed_mixture.astype(jnp.float32),
        logits_gradient,
        (((0,), (0,)), ((), ())),
        precision=highest,
    )
    hidden_part, second_gain_part = pull_second_norm(normed_gradient)
    branch_total, second_gain_total, router_total = (
        lax.psum(hidden_part.astype(jnp.bfloat16), "tensor").astype(jnp.float32),
        lax.psum(second_gain_part.astype(jnp.bfloat16), "tensor").astype(jnp.float32),
        lax.psum(router_gradient.astype(jnp.bfloat16), "tensor").astype(jnp.float32),
    )
    hidden_gradient = upstream + branch_total
    shares = lax.psum_scatter(
        expert_terms(expert_rows, gate_up_gradient, slot_gradient, active_low).astype(jnp.bfloat16),
        "dp",
        scatter_dimension=0,
        tiled=True,
    ).astype(jnp.float32)
    attention_gradient = (residual_scale * hidden_gradient).astype(jnp.bfloat16)
    w_out_gradient = inner_rows(context, attention_gradient)
    context_gradient = (
        times_transposed(attention_gradient, w_out)
        .astype(jnp.bfloat16)
        .reshape(count, block, heads_here, HEAD_DIM)
    )

    def backward_block(carry, item):
        key_sum, value_sum = carry
        scores, grouped = scores_of(item[0], item[1], item[2])
        probs = jnp.exp(scores - item[3])
        grouped_gradient = item[4].reshape(block, pair_heads, group, HEAD_DIM)
        probs_gradient = jnp.einsum(
            "qhgd,khd->hgqk", grouped_gradient, value_all, preferred_element_type=jnp.float32
        )
        spread = jnp.sum(probs * probs_gradient, axis=-1, keepdims=True)
        scores_gradient = (probs * (probs_gradient - spread)).astype(jnp.bfloat16)
        query_gradient = (
            jnp.einsum(
                "hgqk,khd->qhgd", scores_gradient, key_all, preferred_element_type=jnp.float32
            )
            * score_scale
        )
        key_sum = (
            key_sum
            + jnp.einsum(
                "hgqk,qhgd->khd", scores_gradient, grouped, preferred_element_type=jnp.float32
            )
            * score_scale
        )
        value_sum = value_sum + jnp.einsum(
            "hgqk,qhgd->khd",
            probs.astype(jnp.bfloat16),
            grouped_gradient,
            preferred_element_type=jnp.float32,
        )
        return ((key_sum, value_sum), query_gradient.reshape(block, heads_here, HEAD_DIM))

    zero_pairs = jnp.zeros((span * rows, pair_heads, HEAD_DIM), jnp.float32)
    (key_sum, value_sum), query_gradient = lax.scan(
        backward_block,
        (zero_pairs, zero_pairs),
        (query_blocks, place_blocks, doc_blocks, log_totals, context_gradient),
    )
    pair_gradients = jnp.concatenate(
        [key_sum.reshape(span * rows, split), value_sum.reshape(span * rows, split)], axis=1
    ).reshape(span, rows, 2 * split)
    pair_gradient = pair_gradients[0]
    offset = 1
    pair_gradient = pair_gradient + passed_along(
        pair_gradients[offset].astype(jnp.bfloat16), "dp", -offset
    ).astype(jnp.float32)
    key_lin_gradient = (
        pull_key(pair_gradient[:, :split].reshape(rows, pair_heads, HEAD_DIM))[0]
        .reshape(rows, split)
        .astype(jnp.bfloat16)
    )
    value_lin_gradient = pair_gradient[:, split:].astype(jnp.bfloat16)
    query_lin_gradient = (
        pull_query(query_gradient.reshape(rows, heads_here, HEAD_DIM))[0]
        .reshape(rows, heads_here * HEAD_DIM)
        .astype(jnp.bfloat16)
    )
    w_query_gradient = inner_rows(normed_attention, query_lin_gradient)
    w_key_gradient = inner_rows(key_lin_gradient, normed_attention)
    w_value_gradient = inner_rows(value_lin_gradient, normed_attention)
    normed_attention_gradient = (
        times_transposed(query_lin_gradient, w_query)
        + jnp.dot(key_lin_gradient, w_key, preferred_element_type=jnp.float32)
        + jnp.dot(value_lin_gradient, w_value, preferred_element_type=jnp.float32)
    )
    input_part, first_gain_part = pull_first_norm(normed_attention_gradient)
    input_total, first_gain_total = (
        lax.psum(input_part.astype(jnp.bfloat16), "tensor").astype(jnp.float32),
        lax.psum(first_gain_part.astype(jnp.bfloat16), "tensor").astype(jnp.float32),
    )
    tokens_gradient = (hidden_gradient + input_total).astype(jnp.bfloat16)
    summed = (
        lax.psum(first_gain_total.astype(jnp.bfloat16), "dp").astype(jnp.float32),
        lax.psum(w_query_gradient.astype(jnp.bfloat16), "dp").astype(jnp.float32),
        lax.psum(w_key_gradient.astype(jnp.bfloat16), "dp").astype(jnp.float32),
        lax.psum(w_value_gradient.astype(jnp.bfloat16), "dp").astype(jnp.float32),
        lax.psum(w_out_gradient.astype(jnp.bfloat16), "dp").astype(jnp.float32),
        lax.psum(second_gain_total.astype(jnp.bfloat16), "dp").astype(jnp.float32),
        lax.psum(router_total.astype(jnp.bfloat16), "dp").astype(jnp.float32),
    )
    return (
        mixed,
        tokens_gradient,
        summed[0],
        summed[1],
        summed[2],
        summed[3],
        summed[4],
        summed[5],
        summed[6],
        shares[:, :2],
        shares[:, 2],
    )


def solution(mesh):
    placed = (
        P("dp", None),
        P(),
        P("dp", None),
        P(),
        P(None, "tensor"),
        P("tensor", None),
        P("tensor", None),
        P("tensor", None),
        P(),
        P(),
        P(None, None, "tensor", None),
        P(None, "tensor", None),
        P("dp", None),
    )
    return jax.shard_map(
        on_device,
        mesh=mesh,
        in_specs=placed,
        out_specs=(
            P("dp", None),
            P("dp", None),
            P(),
            P(None, "tensor"),
            P("tensor", None),
            P("tensor", None),
            P("tensor", None),
            P(),
            P(),
            P("dp", None, "tensor", None),
            P("dp", "tensor", None),
        ),
        check_vma=False,
    )
```

profile of v0, /device:TPU:0, one launch (start us, length us, event | category | flops | bytes accessed | tf_op | source)
XLA Modules:
  0.0 1801.3 jit_solution(10208344725264198869)
XLA Ops:
  11.5 2.7 convolution_convert_fusion.7
  17.3 3.9 collective-permute-start
  34.0 18.8 %reduce-window.6 = s32[32,64,128]{2,1,0:T(8,128)} reduce-window(s32[32,64,128]{2,1,0:T(8,128)} %fusion.65, s32[]{:T(128)} %constant.75.clone.1), window={size=1x1x128 pad=0_0x0_0x127_0}, to_apply=%region_10.11 | reduce-window | flops 33292288 | bytes 2097156 | tf_op jit(solution)/shard_map/reduce-window
  55.1 4.0 fusion.87
  59.1 4.1 reshape.518
  64.7 3.2 concatenate.57
  67.9 3.1 concatenate.58
  71.0 2.9 fusion.60
  83.6 97.5 %while.27 = (s32[]{:T(128)}, bf16[2,512,512]{2,1,0:T(8,128)(2,1)}, f32[2,4,2,512,1]{3,2,1,4,0:T(2,128)S(1)}, s32[2048]{0:T(1024)S(1)}, s32[2,512]{1,0:T(2,128)S(...) while((s32[]{:T(128)}, bf16[2,512,512]{2,1,0:T(8,128)(2,1)}, ...), condition=%wide.region_4.5_spmd, body=%wide.region_1.4_spmd.sunk | while | flops 2243950592 | bytes 111321216 | solution.py:163
  86.1 13.7 bitcast_reduce_fusion.2
  99.9 15.0 fusion.159
  114.9 15.5 fusion.160
  134.8 13.7 bitcast_reduce_fusion.2
  148.6 15.0 fusion.159
  163.6 15.5 fusion.160
  181.2 4.2 convolution_convert_fusion.1
  185.6 30.5 %scatter_custom_fusion = s32[12288]{0:T(1024)S(1)} fusion(s32[8192]{0:T(1024)S(1)} %bitcast.330, s32[8192]{0:T(1024)S(1)} %iota.56, s32[]{:T(128)} %constant.136.clone.1), kind=kCustom, calls=%fused_computation.180 | custom fusion | bytes 49156 | tf_op jit(solution)/shard_map/scatter | solution.py:51
  216.8 67.5 %gather_fusion.2 = f32[12288,1024]{1,0:T(8,128)} fusion(f32[1025,1024]{1,0:T(8,128)} %concatenate.67, s32[12288]{0:T(1024)S(1)} %get-tuple-element.328), kind=kCustom, calls=%fused_computation.2 | custom fusion | bytes 100712448 | tf_op jit(solution)/shard_map/gather | solution.py:207
  284.9 2.6 multiply_reduce_fusion.2
  292.7 68.0 %gather_fusion.3 = f32[12288]{0:T(1024)S(1)} fusion(f32[8193]{0:T(1024)S(1)} %pad_maximum_fusion.8, s32[12288]{0:T(1024)S(1)} %get-tuple-element.356), kind=kCustom, calls=%fused_computation.3 | custom fusion | bytes 147456 | tf_op jit(solution)/shard_map/gather | solution.py:207
  362.6 52.6 %gather_fusion = bf16[12288,1024]{1,0:T(8,128)(2,1)} fusion(bf16[1025,1024]{1,0:T(8,128)(2,1)S(1)} %concatenate.66, s32[12288]{0:T(1024)S(1)} %get-tuple-element.328), kind=kCustom, calls=%fused_computation | custom fusion | bytes 50380800 | tf_op jit(solution)/shard_map/gather | solution.py:182
  415.2 28.9 %fusion.94 = f32[32,384,2,256]{3,1,2,0:T(8,128)} fusion(bf16[32,384,1024,1]{2,1,3,0:T(8,128)(2,1)} %bitcast.303, bf16[32,2,256,1024]{3,2,1,0:T(8,128)(2,1)} %param.27), kind=kOutput, calls=%fused_computation.218 | convolution fusion | flops 12884901888 | bytes 83886080 | tf_op jit(solution)/shard_map/ecd,ejfd->ecjf/dot_general | solution.py:183
  444.1 41.4 %multiply_bitcast_fusion = (f32[32,384,1,256]{3,1,0,2:T(8,128)}, f32[32,384,1,256]{3,1,0,2:T(8,128)}, bf16[32,384,256]{2,1,0:T(8,128)(2,1)}) fusion(f32[32,384,2,256]{3,1,2,0:T(8,128)} %fusion.94, bf16[32,256,1024]{2,1,0:T(8,128)(2,1)} %param.28, f32[32,384,1024]{2,1,0:T(8,128)} %bitcast.298, f32[32,384]{1,0:T(8,128)S(1)} %mul.414), kind=kOutput, calls=%fused_computation.78 | convolution fusion | flops 6511656960 | bytes 123781120 | tf_op jit(solution)/shard_map/ecd,efd->ecf/dot_general | solution.py:211
  485.5 25.6 %fusion.95 = f32[32,384,1024]{2,1,0:T(8,128)} fusion(bf16[32,384,256]{2,1,0:T(8,128)(2,1)} %get-tuple-element.342, bf16[32,256,1024]{2,1,0:T(8,128)(2,1)} %param.28), kind=kOutput, calls=%fused_computation.219 | convolution fusion | flops 6442450944 | bytes 73400320 | tf_op jit(solution)/shard_map/ecf,efd->ecd/dot_general | solution.py:192
  511.1 59.0 %gather_fusion.1 = f32[8192,1024]{1,0:T(8,128)} fusion(f32[12288,1024]{1,0:T(8,128)} %bitcast.297, s32[8192]{0:T(1024)S(1)} %copy-done.67), kind=kCustom, calls=%fused_computation.1 | custom fusion | bytes 67141632 | tf_op jit(solution)/shard_map/gather | solution.py:195
  570.1 17.3 fusion.37
  590.6 40.0 %fusion.38 = f32[32,384,1024,1]{2,1,0,3:T(8,128)} fusion(bf16[32,2,256,1024]{3,2,1,0:T(8,128)(2,1)} %param.27, f32[32,384,1,256]{3,1,0,2:T(8,128)} %get-tuple-element.341, f32[32,384,1,256]{3,1,0,2:T(8,128)} %get-tuple-element.340), kind=kOutput, calls=%fused_computation.66 | convolution fusion | flops 12897484800 | bytes 109051904 | tf_op jit(solution)/shard_map/ecjf,ejfd->ecd/dot_general | solution.py:215
  630.6 108.1 %scatter_custom_fusion.1 = f32[1025,1024]{1,0:T(8,128)} fusion(s32[12288]{0:T(1024)} %get-tuple-element.329, f32[12288,1024]{1,0:T(8,128)} %bitcast.308, f32[]{:T(128)} %constant.76.clone.1), kind=kCustom, calls=%fused_computation.111 | custom fusion | flops 12582912 | bytes 4198912 | tf_op jit(solution)/shard_map/scatter-add | solution.py:221
  738.8 6.2 multiply_reduce_fusion
  745.1 2.6 fusion.50
  747.7 25.8 %convert_bitcast_fusion = bf16[32,1,256,1024]{3,2,1,0:T(8,128)(2,1)} fusion(bf16[32,384,256]{2,1,0:T(8,128)(2,1)} %get-tuple-element.342, f32[32,384,1024]{2,1,0:T(8,128)} %bitcast.299, f32[32,384]{1,0:T(8,128)S(1)} %copy-done.58), kind=kOutput, calls=%fused_computation.71 | convolution fusion | flops 6476005376 | bytes 73449472 | tf_op jit(solution)/shard_map/ecf,ecd->efd/dot_general | solution.py:72
  773.5 38.6 %all-reduce.19.cloned.1.call-done = bf16[1024,1024]{1,0:T(8,128)(2,1)} async-done(((bf16[1024,1024]{1,0:T(8,128)(2,1)}), bf16[1024,1024]{1,0:T(8,128)(2,1)}) %all-reduce.19.cloned.1.call-update) | async-done | bytes 2097168 | tf_op jit(solution)/shard_map/psum | solution.py:236
  812.2 3.9 convolution_convert_fusion.4
  816.1 4.0 reshape.595
  820.0 3.3 copy.77
  823.4 241.8 %while.28 = (s32[]{:T(128)}, f32[2048,4,64]{0,2,1:T(8,128)}, f32[2048,4,64]{0,2,1:T(8,128)}, f32[2,512,8,64]{1,0,3,2:T(2,128)}, bf16[2,512,8,64]{1,3,2,0:T(8,128...) while((s32[]{:T(128)}, f32[2048,4,64]{0,2,1:T(8,128)}, ...), condition=%wide.region_24.25_spmd.clone, body=%wide.region_22.24_spmd.clone.sunk | while | flops 5501614080 | bytes 348283136 | solution.py:287
  826.2 13.2 fusion.170
  839.4 15.7 fusion.174
  855.1 24.4 %fusion.171 = (f32[4,2,512]{2,1,0:T(2,128)S(1)}, f32[4,512,2,2048]{3,1,2,0:T(8,128)}) fusion(f32[4,512,2,2048]{3,1,2,0:T(8,128)} %fusion.170, f32[4,2,512]{2,1,0:T(2,128)S(1)} %dynamic-slice_bitcast_fusion.2, pred[512,2048]{1,0:T(8,128)(4,1)S(1)} %compare_and_fusion.5, bf16[512,4,2,64]{0,3,2,1:T(8,128)(2,1)S(1)} %bitcast.310, ...), kind=kOutput, calls=%fused_computation.31.clone.1 | convolution fusion | flops 1115680768 | bytes 69763072 | tf_op jit(solution)/shard_map/while/body/eval_jaxpr/qhgd,khd->hgqk/dot_general | solution.py:260
  879.4 27.8 %fusion.172 = bf16[4,2,512,2048]{3,2,1,0:T(8,128)(2,1)} fusion(f32[4,512,2,2048]{3,1,2,0:T(8,128)} %get-tuple-element.529, f32[4,512,2,2048]{3,1,2,0:T(8,128)} %fusion.170, f32[4,2,512]{2,1,0:T(2,128)S(1)} %get-tuple-element.530, f32[4,2,512]{2,1,0:T(2,128)S(1)} %dynamic-slice_bitcast_fusion.2, pred[512,2048]{1,0:T(8,128)(4,1)S(1)} %compare_and_fusion.5), kind=kLoop, calls=%fused_computation.33.clone.1 | loop fusion | flops 50331648 | bytes 84967424 | tf_op jit(solution)/shard_map/while/body/eval_jaxpr/convert_element_type | solution.py:264
  907.2 10.8 convolution_multiply_fusion.2
  918.0 4.4 fusion.173
  923.5 19.6 %dynamic_update_slice.20 = f32[2,512,8,64]{1,0,3,2:T(2,128)} dynamic-update-slice(f32[2,512,8,64]{1,0,3,2:T(2,128)} %get-tuple-element.582, f32[1,512,8,64]{1,0,3,2:T(1,128)S(1)} %copy.128, s32[]{:T(128)S(6)} %copy.147, s32[]{:T(128)} %constant.75.clone.1..sunk, s32[]{:T(128)} %constant.75.clone.1..sunk, s32[]{:T(128)} %constant.75.clone.1..sunk) | dynamic-update-slice | bytes 2097156 | tf_op jit(solution)/shard_map/while/body/jit(dynamic_update_index_in_dim)/dynamic_update_slice | solution.py:287
  945.7 13.2 fusion.170
  958.8 16.3 fusion.174
  975.1 24.4 %fusion.171 = (f32[4,2,512]{2,1,0:T(2,128)S(1)}, f32[4,512,2,2048]{3,1,2,0:T(8,128)}) fusion(f32[4,512,2,2048]{3,1,2,0:T(8,128)} %fusion.170, f32[4,2,512]{2,1,0:T(2,128)S(1)} %dynamic-slice_bitcast_fusion.2, pred[512,2048]{1,0:T(8,128)(4,1)S(1)} %compare_and_fusion.5, bf16[512,4,2,64]{0,3,2,1:T(8,128)(2,1)S(1)} %bitcast.310, ...), kind=kOutput, calls=%fused_computation.31.clone.1 | convolution fusion | flops 1115680768 | bytes 69763072 | tf_op jit(solution)/shard_map/while/body/eval_jaxpr/qhgd,khd->hgqk/dot_general | solution.py:260
  999.5 27.8 %fusion.172 = bf16[4,2,512,2048]{3,2,1,0:T(8,128)(2,1)} fusion(f32[4,512,2,2048]{3,1,2,0:T(8,128)} %get-tuple-element.529, f32[4,512,2,2048]{3,1,2,0:T(8,128)} %fusion.170, f32[4,2,512]{2,1,0:T(2,128)S(1)} %get-tuple-element.530, f32[4,2,512]{2,1,0:T(2,128)S(1)} %dynamic-slice_bitcast_fusion.2, pred[512,2048]{1,0:T(8,128)(4,1)S(1)} %compare_and_fusion.5), kind=kLoop, calls=%fused_computation.33.clone.1 | loop fusion | flops 50331648 | bytes 84967424 | tf_op jit(solution)/shard_map/while/body/eval_jaxpr/convert_element_type | solution.py:264
  1027.3 10.8 convolution_multiply_fusion.2
  1038.1 6.0 fusion.173
  1045.2 19.6 %dynamic_update_slice.20 = f32[2,512,8,64]{1,0,3,2:T(2,128)} dynamic-update-slice(f32[2,512,8,64]{1,0,3,2:T(2,128)} %get-tuple-element.582, f32[1,512,8,64]{1,0,3,2:T(1,128)S(1)} %copy.128, s32[]{:T(128)S(6)} %copy.147, s32[]{:T(128)} %constant.75.clone.1..sunk, s32[]{:T(128)} %constant.75.clone.1..sunk, s32[]{:T(128)} %constant.75.clone.1..sunk) | dynamic-update-slice | bytes 2097156 | tf_op jit(solution)/shard_map/while/body/jit(dynamic_update_index_in_dim)/dynamic_update_slice | solution.py:287
  1065.2 4.2 reshape.529
  1083.2 38.3 %convolution_convert_fusion = bf16[32,2,256,1024]{3,2,1,0:T(8,128)(2,1)} fusion(bf16[32,384,1024,1]{2,1,3,0:T(8,128)(2,1)} %bitcast.304, f32[32,384,1,256]{3,1,0,2:T(8,128)} %get-tuple-element.341, f32[32,384,1,256]{3,1,0,2:T(8,128)} %get-tuple-element.340), kind=kOutput, calls=%fused_computation.69 | convolution fusion | flops 12914262016 | bytes 83886080 | tf_op jit(solution)/shard_map/ecjf,ecd->ejfd/dot_general | solution.py:69
  1121.6 2.5 convolution_convert_fusion.3
  1129.7 74.5 %all-reduce.23.cloned.1.call-done = (bf16[1024,1024]{1,0:T(8,128)(2,1)}, bf16[1024,1024]{1,0:T(8,128)(2,1)}, bf16[1024,32]{0,1:T(8,128)(2,1)}) async-done(((bf16[1024,1024]{1,0:T(8,128)(2,1)}, bf16[1024,1024]{1,0:T(8,128)(2,1)}, bf16[1024,32]{0,1:T(8,128)(2,1)}), (bf16[1024,1024]{1,0:T(8,128)(2,1)}, bf16[1024,1024]{1,0:T(8,128)(2,1)}, bf16[1024,32]{0,1:T(8,128)(2,1)})) %all-reduce.23.cloned.1.call-update) | async-done | bytes 4259856 | tf_op jit(solution)/shard_map/psum | solution.py:197
  1204.3 33.6 %pad_maximum_fusion = bf16[32,3,256,1024]{3,2,1,0:T(8,128)(2,1)} fusion(bf16[32,1,256,1024]{3,2,1,0:T(8,128)(2,1)} %convert_bitcast_fusion, bf16[32,2,256,1024]{3,2,1,0:T(8,128)(2,1)} %convolution_convert_fusion), kind=kLoop, calls=%fused_computation.60 | loop fusion | flops 25165824 | bytes 100663296 | tf_op jit(solution)/shard_map/concatenate | solution.py:73
  1238.6 4.9 all-reduce.10
  1243.5 33.0 %all-reduce.8 = (bf16[1024]{0:T(1024)(128)(2,1)S(1)}, bf16[1024]{0:T(1024)(128)(2,1)S(1)}) all-reduce(bf16[1024]{0:T(1024)(128)(2,1)S(1)} %get-tuple-element.321, bf16[1024]{0:T(1024)(128)(2,1)S(1)} %get-tuple-element.322), channel_id=1, replica_groups=mesh['dp'=16,'tensor'=2] {'dp'}, use_global_device_ids=true, to_apply=%region_29.30 | all-reduce | flops 2048 | bytes 8192 | tf_op jit(solution)/shard_map/psum | solution.py:326
  1277.7 5.8 add_convert_fusion.1
  1283.5 2.9 add_convert_fusion.2
  1286.4 29.0 %all-reduce.21.cloned.1.call-done = (bf16[1024,512]{1,0:T(8,128)(2,1)}, bf16[256,1024]{1,0:T(8,128)(2,1)}, bf16[256,1024]{1,0:T(8,128)(2,1)}, bf16[512,1024]{1,0:T(8,128)(2,1)}, bf16[1024,32]{0,1:T(8,128)(2,1)}) async-done(((bf16[1024,512]{1,0:T(8,128)(2,1)}, bf16[256,1024]{1,0:T(8,128)(2,1)}, bf16[256,1024]{1,0:T(8,128)(2,1)}, bf16[512,1024]{1,0:T(8,128)(2,1)}, bf16[1024,32]{0,1:T(8,128)(2,1)}), ...) | async-done | bytes 3211280 | tf_op jit(solution)/shard_map/psum | solution.py:327
  1317.0 2.8 convert_element_type.209
  1324.7 462.0 %reduce-scatter.2.cloned.1.call-done = bf16[2,3,256,1024]{3,2,1,0:T(8,128)(2,1)} async-done(((bf16[32,3,256,1024]{3,2,1,0:T(8,128)(2,1)}), bf16[2,3,256,1024]{3,2,1,0:T(8,128)(2,1)}) %reduce-scatter.2.cloned.1.call-update) | async-done | bytes 3145744 | tf_op jit(solution)/shard_map/reduce_scatter | solution.py:241
  1786.7 2.6 convert_element_type.220
  1792.0 2.5 slice.95
  (325 shorter events, 91.3 us)
Async XLA Ops:
  7.2 174.0 %copy-start = (bf16[512,1024]{1,0:T(8,128)(2,1)S(1)}, bf16[512,1024]{1,0:T(8,128)(2,1)}, u32[]{:S(2)}) copy-start(bf16[512,1024]{1,0:T(8,128)(2,1)} %param.24) | copy-start | bytes 3145732
  7.2 277.7 %all-reduce.17.cloned.1.call-start = ((), (), s32[]{:S(2)}) async-start(), calls=%async_computation.1 | async-start | bytes 4194304 | tf_op jit(solution)/shard_map/psum | solution.py:166
  8.0 47.1 %copy-start.78 = (f32[1024]{0:T(1024)}, f32[1024]{0:T(1024)S(1)}, u32[]{:S(2)}) copy-start(f32[1024]{0:T(1024)S(1)} %convert_element_type.174) | copy-start | bytes 12292
  8.0 6.1 copy-start.3
  10.2 4.8 copy-start.82
  10.3 44.8 %copy-start.80 = (f32[1024]{0:T(1024)}, f32[1024]{0:T(1024)S(1)}, u32[]{:S(2)}) copy-start(f32[1024]{0:T(1024)S(1)} %fusion.77) | copy-start | bytes 12292
  10.3 3.9 copy-start.50
  11.5 3.8 copy-start.33
  11.5 3.6 copy-start.31
  15.1 6.2 copy-start.54
  15.1 9.7 copy-start.91
  17.3 63.6 %collective-permute-start = (bf16[1024,512]{0,1:T(8,128)(2,1)}, bf16[1024,512]{0,1:T(8,128)(2,1)}, u32[]{:S(2)}, u32[]{:S(2)}) collective-permute-start(bf16[1024,512]{0,1:T(8,128)(2,1)} %pad_maximum_fusion.3), channel_id=1, source_target_pairs={{0,2},{2,4},{4,6},{6,8},{8,10},{10,12},{12,14},{14,16},{16,18},{18... | collective-permute-start | bytes 3145736 | tf_op jit(solution)/shard_map/ppermute | solution.py:24
  59.1 4.1 copy-start.26
  64.7 6.3 copy-start.27
  71.0 4.1 copy-start.23
  75.7 5.2 copy-start.30
  75.7 5.2 copy-start.42
  181.2 4.2 copy-start.7
  181.2 4.2 copy-start.37
  181.2 4.2 copy-start.48
  181.2 4.3 copy-start.61
  181.2 4.3 copy-start.63
  181.2 4.3 copy-start.65
  181.2 4.3 copy-start.68
  181.2 4.3 copy-start.69
  185.5 626.7 %all-reduce.19.cloned.1.call-start = ((), (), s32[]{:S(2)}) async-start(), calls=%async_computation.2 | async-start | bytes 4194304 | tf_op jit(solution)/shard_map/psum | solution.py:236
  216.8 68.1 %copy-start.4 = (bf16[1024,1024]{1,0:T(8,128)(2,1)S(1)}, bf16[1024,1024]{1,0:T(8,128)(2,1)}, u32[]{:S(2)}) copy-start(bf16[1024,1024]{1,0:T(8,128)(2,1)} %param.17) | copy-start | bytes 6291460
  360.8 83.3 %copy-start.57 = (f32[32,384]{1,0:T(8,128)}, f32[32,384]{1,0:T(8,128)S(1)}, u32[]{:S(2)}) copy-start(f32[32,384]{1,0:T(8,128)S(1)} %mul.414) | copy-start | bytes 147460
  485.5 25.6 %copy-start.67 = (s32[8192]{0:T(1024)S(1)}, s32[8192]{0:T(1024)}, u32[]{:S(2)}) copy-start(s32[8192]{0:T(1024)} %broadcast_clamp_fusion.1) | copy-start | bytes 98308
  570.1 18.5 %copy-start.44 = (f32[1024,8]{0,1:T(8,128)S(1)}, f32[1024,8]{0,1:T(8,128)}, u32[]{:S(2)}) copy-start(f32[1024,8]{0,1:T(8,128)} %copy-done.43) | copy-start | bytes 98308
  570.1 18.5 %copy-start.71 = (f32[1024]{0:T(1024)S(1)}, f32[1024]{0:T(1024)}, u32[]{:S(2)}) copy-start(f32[1024]{0:T(1024)} %copy-done.70) | copy-start | bytes 12292
  570.1 18.5 %copy-start.86 = (f32[1024]{0:T(1024)S(1)}, f32[1024]{0:T(1024)}, u32[]{:S(2)}) copy-start(f32[1024]{0:T(1024)} %multiply_divide_fusion) | copy-start | bytes 12292
  570.1 18.6 %copy-start.77 = (f32[1024]{0:T(1024)S(1)}, f32[1024]{0:T(1024)}, u32[]{:S(2)}) copy-start(f32[1024]{0:T(1024)} %copy-done.76) | copy-start | bytes 12292
  570.1 18.6 %copy-start.56 = (s32[1024,8]{0,1:T(8,128)S(1)}, s32[1024,8]{0,1:T(8,128)}, u32[]{:S(2)}) copy-start(s32[1024,8]{0,1:T(8,128)} %param.19) | copy-start | bytes 98308
  570.1 18.7 %copy-start.16 = (bf16[1024,1024]{1,0:T(8,128)(2,1)S(1)}, bf16[1024,1024]{1,0:T(8,128)(2,1)}, u32[]{:S(2)}) copy-start(bf16[1024,1024]{1,0:T(8,128)(2,1)} %copy-done.15) | copy-start | bytes 6291460
  630.6 108.2 %copy-start.5 = (bf16[1024,1024]{1,0:T(8,128)(2,1)S(1)}, bf16[1024,1024]{1,0:T(8,128)(2,1)}, u32[]{:S(2)}) copy-start(bf16[1024,1024]{1,0:T(8,128)(2,1)} %param.17) | copy-start | bytes 6291460
  630.6 108.2 %copy-start.60 = (bf16[1024,32]{0,1:T(8,128)(2,1)S(1)}, bf16[1024,32]{0,1:T(8,128)(2,1)}, u32[]{:S(2)}) copy-start(bf16[1024,32]{0,1:T(8,128)(2,1)} %param.26) | copy-start | bytes 196612
  630.6 108.2 %copy-start.73 = (f32[1024]{0:T(1024)S(1)}, f32[1024]{0:T(1024)}, u32[]{:S(2)}) copy-start(f32[1024]{0:T(1024)} %convert_element_type.183) | copy-start | bytes 12292
  630.6 108.2 %copy-start.75 = (f32[1024]{0:T(1024)S(1)}, f32[1024]{0:T(1024)}, u32[]{:S(2)}) copy-start(f32[1024]{0:T(1024)} %copy-done.74) | copy-start | bytes 12292
  738.8 6.3 copy-start.85
  738.8 6.3 copy-start.11
  747.7 64.5 %copy-start.24 = (bf16[1024,1024]{1,0:T(8,128)(2,1)S(1)}, bf16[1024,1024]{1,0:T(8,128)(2,1)}, u32[]{:S(2)}) copy-start(bf16[1024,1024]{1,0:T(8,128)(2,1)} %param.29) | copy-start | bytes 6291460
  747.7 456.6 %all-reduce.23.cloned.1.call-start = ((), (), s32[]{:S(2)}) async-start(), calls=%async_computation.5 | async-start | bytes 8519680 | tf_op jit(solution)/shard_map/psum | solution.py:197
  816.0 7.3 copy-start.8
  816.0 7.3 copy-start.38
  816.0 7.3 copy-start.49
  816.0 7.3 copy-start.62
  816.0 7.3 copy-start.64
  816.0 7.3 copy-start.66
  839.4 15.7 copy-start.13
  907.2 10.8 copy-start.2
  958.8 16.3 copy-start.13
  1027.3 10.8 copy-start.2
  1065.2 4.2 copy-start.9
  1065.2 7.2 copy-start.32
  1070.9 4.7 collective-permute-start.1
  1083.1 38.4 %copy-start.47 = (bf16[1024,8,64]{0,2,1:T(8,128)(2,1)S(1)}, bf16[1024,8,64]{0,2,1:T(8,128)(2,1)}, u32[]{:S(2)}) copy-start(bf16[1024,8,64]{0,2,1:T(8,128)(2,1)} %copy-done.46) | copy-start | bytes 3145732
  1083.1 232.3 %all-reduce.21.cloned.1.call-start = ((), (), s32[]{:S(2)}) async-start(), calls=%async_computation.4 | async-start | bytes 6422528 | tf_op jit(solution)/shard_map/psum | solution.py:327
  1204.3 582.4 %reduce-scatter.2.cloned.1.call-start = ((), (), s32[]{:S(2)}) async-start(), calls=%async_computation.3 | async-start | bytes 53477376 | tf_op jit(solution)/shard_map/reduce_scatter | solution.py:241
  1277.7 5.8 copy-start.12
  1277.7 5.8 copy-start.40
  1315.4 6.6 copy-start.53
  1315.4 7.7 copy-start.45
  1789.4 5.1 copy-start.1
  (39 other events, 80.9 us)
Sparse Core Ops, SparseCore 0:
  185.6 64.4 all-reduce.16
  747.8 64.3 all-reduce.18
  1083.3 120.9 all-reduce.22
  1209.5 105.8 all-reduce.20
  1320.1 466.6 reduce-scatter.1
where the time goes:
time: 1810 us; the launch traced here: 1800 us
  waiting for transfers between devices  605 us (33%)
  matrix products  434 us (24%)
  local copies, waits for them, and re-layouts  381 us (21%)
  other arithmetic  323 us (18%)
  blocking collectives  37.9 us (2%)
    reduce_scatter x1, waiting for transfers between devices, on_device(): lax.psum_scatter(expert_terms(expert_rows, gate_up_gradient, slot_gradien...  462 us
    scatter-add x1, other arithmetic, on_device(): normed_gradient = jnp.zeros((rows + 1, width), jnp.float32).at[token_of]....  108 us
    psum x1, waiting for transfers between devices, on_device(): lax.psum(mixture_part.astype(jnp.bfloat16), 'tensor').astype(jnp.float32)  74.5 us
    gather x1, local copies, waits for them, and re-layouts, on_device(): gate_padded[source][:, None]  68 us
    gather x1, local copies, waits for them, and re-layouts, on_device(): upstream_padded[token_of] * gate_padded[source][:, None]  67.5 us
    gather x1, local copies, waits for them, and re-layouts, on_device(): picked = expert_out[place].reshape(rows, TOP, width)  59 us
    convert_element_type x2, other arithmetic, backward_block(): scores_gradient = (probs * (probs_gradient - spread)).astype(jnp.bfloat16)  55.6 us
    dot_general x4, matrix products, scores_of(): jnp.einsum('qhgd,khd->hgqk', grouped, key_all, preferred_element_type=jnp...  53.8 us
  transfers between devices with their start and end apart: 7, of which 5 were waited for; matrix products, arithmetic and copies ran while one was open for 16% of the time, Pallas kernels for 0%

commit v1 on v0

v1 whole, which is shorter than its diff:
```python
import functools

import jax
import jax.numpy as jnp
from jax import lax
from jax.experimental import pallas as pl
from jax.experimental.pallas import tpu as pltpu
from jax.sharding import PartitionSpec as P

HEAD_DIM = 64
EXPERTS = 32
SEQ_LEN = 2048
BLOCK = 256

epsilon = 1e-06
score_scale = 0.015625
residual_scale = 0.22
rope_base = 10000.0
masked_value = -1e30
vmem_bytes = 48 * 1024 * 1024
f32 = jnp.float32
bf16 = jnp.bfloat16


def dot(left, right, left_dim, right_dim):
    return lax.dot_general(
        left, right, (((left_dim,), (right_dim,)), ((), ())), preferred_element_type=f32
    )


def mm(left, right):
    return jnp.dot(left, right, preferred_element_type=f32)


def block_mask(lo, hi, start, lanes):
    place = start + lax.broadcasted_iota(jnp.int32, (BLOCK, lanes), 0)
    return (place >= lo) & (place <= hi)


def window_of(lo_ref, block, before, group):
    cut = pl.ds(block * BLOCK, BLOCK)
    lo = lo_ref[:, cut]
    hi = before + block * BLOCK + lax.broadcasted_iota(jnp.int32, (1, BLOCK), 1)
    return (
        jnp.concatenate([lo] * group, axis=1),
        jnp.concatenate([hi] * group, axis=1),
    )


def heads_side_by_side(ref, block, group):
    cut = pl.ds(block * BLOCK, BLOCK)
    return jnp.concatenate(
        [ref[h * HEAD_DIM : (h + 1) * HEAD_DIM, cut] for h in range(group)], axis=1
    )


def heads_one_above(ref, block, group):
    cut = pl.ds(block * BLOCK, BLOCK)
    return jnp.concatenate([ref[0, h, cut, :] for h in range(group)], axis=0)


def attend_kernel(
    group, first_ref, lo_ref, qt_ref, k_ref, vt_ref, old_k_ref, old_vt_ref, out_ref, log_ref
):
    lanes = group * BLOCK
    before = old_k_ref.shape[1]
    passed = before // BLOCK
    for block in range(qt_ref.shape[1] // BLOCK):
        lo, hi = window_of(lo_ref, block, before, group)
        query = heads_side_by_side(qt_ref, block, group)

        def step(keys_ref, values_ref, offset, number, carry):
            peak, total, acc = carry
            start = pl.multiple_of(number * BLOCK, BLOCK)
            scores = mm(keys_ref[0, pl.ds(start, BLOCK), :], query)
            scores = jnp.where(block_mask(lo, hi, offset + start, lanes), scores, masked_value)
            top = jnp.maximum(peak, jnp.max(scores, axis=0, keepdims=True))
            weights = jnp.exp(scores - top)
            fade = jnp.exp(peak - top)
            total = total * fade + jnp.sum(weights, axis=0, keepdims=True)
            acc = acc * fade + mm(values_ref[:, pl.ds(start, BLOCK)], weights.astype(bf16))
            return (top, total, acc)

        first = first_ref[block]
        carry = (
            jnp.full((1, lanes), masked_value, f32),
            jnp.zeros((1, lanes), f32),
            jnp.zeros((HEAD_DIM, lanes), f32),
        )
        carry = lax.fori_loop(
            first, passed, functools.partial(step, old_k_ref, old_vt_ref, 0), carry
        )
        peak, total, acc = lax.fori_loop(
            jnp.maximum(first - passed, 0),
            block + 1,
            functools.partial(step, k_ref, vt_ref, before),
            carry,
        )
        result = (acc / total).astype(bf16)
        logs = peak + jnp.log(total)
        cut = pl.ds(block * BLOCK, BLOCK)
        for h in range(group):
            side = slice(h * BLOCK, (h + 1) * BLOCK)
            out_ref[h * HEAD_DIM : (h + 1) * HEAD_DIM, cut] = result[:, side]
            log_ref[0, h : h + 1, cut] = logs[:, side]


def attend(first, lo, q_t, k, v_t, old_k, old_v_t, group):
    pair_heads, rows, _ = k.shape
    before = old_k.shape[1]
    tall = group * HEAD_DIM
    by_head = lambda h, s: (h, 0, 0)
    return pl.pallas_call(
        functools.partial(attend_kernel, group),
        grid_spec=pltpu.PrefetchScalarGridSpec(
            num_scalar_prefetch=1,
            grid=(pair_heads,),
            in_specs=[
                pl.BlockSpec((1, rows), lambda h, s: (0, 0)),
                pl.BlockSpec((tall, rows), lambda h, s: (h, 0)),
                pl.BlockSpec((1, rows, HEAD_DIM), by_head),
                pl.BlockSpec((HEAD_DIM, rows), lambda h, s: (h, 0)),
                pl.BlockSpec((1, before, HEAD_DIM), by_head),
                pl.BlockSpec((HEAD_DIM, before), lambda h, s: (h, 0)),
            ],
            out_specs=[
                pl.BlockSpec((tall, rows), lambda h, s: (h, 0)),
                pl.BlockSpec((1, group, rows), by_head),
            ],
        ),
        out_shape=[
            jax.ShapeDtypeStruct((pair_heads * tall, rows), bf16),
            jax.ShapeDtypeStruct((pair_heads, group, rows), f32),
        ],
        compiler_params=pltpu.CompilerParams(vmem_limit_bytes=vmem_bytes),
        cost_estimate=pl.CostEstimate(
            flops=pair_heads * group * rows * (rows + before) * 512,
            bytes_accessed=8 * 1024 * 1024,
            transcendentals=pair_heads * group * rows * (rows + before),
        ),
        name="attend",
    )(first, lo, q_t, k, v_t, old_k, old_v_t)


def attend_back_kernel(
    group, earlier, before,
    first_ref, lo_ref, log_ref, spread_ref, qt_ref, dt_ref, q_ref, d_ref, k_ref, kt_ref, v_ref,
    sum_ref, dq_ref, dk_ref, dv_ref, pair_ref,
):
    lanes = group * BLOCK
    passed = before // BLOCK
    pair_ref[...] = jnp.zeros_like(pair_ref)
    for block in range(qt_ref.shape[1] // BLOCK):
        cut = pl.ds(block * BLOCK, BLOCK)
        lo, hi = window_of(lo_ref, block, before, group)
        query = heads_side_by_side(qt_ref, block, group)
        upstream = heads_side_by_side(dt_ref, block, group)
        query_rows = heads_one_above(q_ref, block, group)
        upstream_rows = heads_one_above(d_ref, block, group)
        nothing = jnp.zeros_like(query_rows)
        both_rows = jnp.concatenate(
            [
                jnp.concatenate([query_rows, nothing], axis=1),
                jnp.concatenate([nothing, upstream_rows], axis=1),
            ],
            axis=0,
        )
        logs = jnp.concatenate([log_ref[0, h : h + 1, cut] for h in range(group)], axis=1)
        spread = jnp.concatenate([spread_ref[0, h : h + 1, cut] for h in range(group)], axis=1)

        def step(number, acc):
            start = pl.multiple_of(number * BLOCK, BLOCK)
            here = pl.ds(start, BLOCK)
            scores = mm(k_ref[0, here, :], query)
            mask = block_mask(lo, hi, start + (0 if earlier else before), lanes)
            probs = jnp.exp(jnp.where(mask, scores - logs, masked_value))
            change = mm(v_ref[0, here, :], upstream)
            scores_change = (probs * (change - spread)).astype(bf16)
            pair_ref[here, :] += mm(
                jnp.concatenate([scores_change, probs.astype(bf16)], axis=1), both_rows
            )
            return acc + mm(kt_ref[:, here], scores_change)

        first = first_ref[block]
        bounds = (first, passed) if earlier else (jnp.maximum(first - passed, 0), block + 1)
        acc = lax.fori_loop(*bounds, step, jnp.zeros((HEAD_DIM, lanes), f32))
        for h in range(group):
            side = slice(h * HEAD_DIM, (h + 1) * HEAD_DIM)
            dq_ref[side, cut] = sum_ref[side, cut] + (
                acc[:, h * BLOCK : (h + 1) * BLOCK] * score_scale
            )
    pair_t = pair_ref[...].T
    dk_ref[...] = pair_t[:HEAD_DIM].astype(dk_ref.dtype)
    dv_ref[...] = pair_t[HEAD_DIM:].astype(dv_ref.dtype)


def attend_back(
    first, lo, logs, spread, q_t, d_t, q_rows, d_rows, k, k_t, v, dq_sum, before, earlier
):
    pair_heads, keys, _ = k.shape
    group, rows = q_rows.shape[1:3]
    tall = group * HEAD_DIM
    by_head = lambda h, s: (h, 0, 0)
    flat = lambda h, s: (h, 0)
    pair_type = bf16 if earlier else f32
    return pl.pallas_call(
        functools.partial(attend_back_kernel, group, earlier, before),
        grid_spec=pltpu.PrefetchScalarGridSpec(
            num_scalar_prefetch=1,
            grid=(pair_heads,),
            in_specs=[
                pl.BlockSpec((1, rows), lambda h, s: (0, 0)),
                pl.BlockSpec((1, group, rows), by_head),
                pl.BlockSpec((1, group, rows), by_head),
                pl.BlockSpec((tall, rows), flat),
                pl.BlockSpec((tall, rows), flat),
                pl.BlockSpec((1, group, rows, HEAD_DIM), lambda h, s: (h, 0, 0, 0)),
                pl.BlockSpec((1, group, rows, HEAD_DIM), lambda h, s: (h, 0, 0, 0)),
                pl.BlockSpec((1, keys, HEAD_DIM), by_head),
                pl.BlockSpec((HEAD_DIM, keys), flat),
                pl.BlockSpec((1, keys, HEAD_DIM), by_head),
                pl.BlockSpec((tall, rows), flat),
            ],
            out_specs=[
                pl.BlockSpec((tall, rows), flat),
                pl.BlockSpec((HEAD_DIM, keys), flat),
                pl.BlockSpec((HEAD_DIM, keys), flat),
            ],
            scratch_shapes=[pltpu.VMEM((keys, 2 * HEAD_DIM), f32)],
        ),
        out_shape=[
            jax.ShapeDtypeStruct((pair_heads * tall, rows), f32),
            jax.ShapeDtypeStruct((pair_heads * HEAD_DIM, keys), pair_type),
            jax.ShapeDtypeStruct((pair_heads * HEAD_DIM, keys), pair_type),
        ],
        compiler_params=pltpu.CompilerParams(vmem_limit_bytes=vmem_bytes),
        cost_estimate=pl.CostEstimate(
            flops=pair_heads * group * rows * keys * 1280,
            bytes_accessed=10 * 1024 * 1024,
            transcendentals=pair_heads * group * rows * keys,
        ),
        name="attend_back",
    )(first, lo, logs, spread, q_t, d_t, q_rows, d_rows, k, k_t, v, dq_sum)


def turn(tall, cosine, sine):
    half = HEAD_DIM // 2
    parts = []
    for start in range(0, tall.shape[0], HEAD_DIM):
        a, b = tall[start : start + half], tall[start + half : start + HEAD_DIM]
        parts += [a * cosine - b * sine, b * cosine + a * sine]
    return jnp.concatenate(parts, axis=0)


def put_heads(ref, rows_of_heads):
    for h in range(ref.shape[0]):
        ref[h] = rows_of_heads[:, h * HEAD_DIM : (h + 1) * HEAD_DIM]


def project_kernel(
    x_ref, gain_ref, cos_ref, sin_ref, wq_ref, wk_ref, wv_ref,
    normed_ref, qt_ref, q_ref, kt_ref, k_ref, vt_ref, v_ref,
):
    x = x_ref[...].astype(f32)
    normed = (x * scale_of(x) * gain_ref[...].astype(f32)).astype(bf16)
    normed_ref[...] = normed
    cosine, sine = cos_ref[...], sin_ref[...]
    q_t = turn(mm(normed, wq_ref[...]).T, cosine, sine).astype(bf16).astype(f32) * score_scale
    qt_ref[...] = q_t.astype(bf16)
    put_heads(q_ref, q_t.T.astype(bf16))
    k_t = turn(dot(wk_ref[...], normed, 1, 1), cosine, sine)
    kt_ref[...] = k_t.astype(bf16)
    put_heads(k_ref, k_t.T.astype(bf16))
    v_t = dot(wv_ref[...], normed, 1, 1)
    vt_ref[...] = v_t.astype(bf16)
    put_heads(v_ref, v_t.T.astype(bf16))


def project(tokens, gain, cosine, sine, w_query, w_key, w_value):
    rows, width = tokens.shape
    tall, split = w_query.shape[1], w_key.shape[0]
    heads, pair_heads = tall // HEAD_DIM, split // HEAD_DIM
    whole = lambda shape: pl.BlockSpec(shape, lambda t: (0,) * len(shape))
    down = lambda wide: pl.BlockSpec((BLOCK, wide), lambda t: (t, 0))
    across = lambda high: pl.BlockSpec((high, BLOCK), lambda t: (0, t))
    stacked = lambda count: pl.BlockSpec((count, BLOCK, HEAD_DIM), lambda t: (0, t, 0))
    return pl.pallas_call(
        project_kernel,
        grid=(rows // BLOCK,),
        in_specs=[
            down(width), whole((1, width)), across(HEAD_DIM // 2), across(HEAD_DIM // 2),
            whole((width, tall)), whole((split, width)), whole((split, width)),
        ],
        out_specs=[
            down(width), across(tall), stacked(heads), across(split), stacked(pair_heads),
            across(split), stacked(pair_heads),
        ],
        out_shape=[
            jax.ShapeDtypeStruct((rows, width), bf16),
            jax.ShapeDtypeStruct((tall, rows), bf16),
            jax.ShapeDtypeStruct((heads, rows, HEAD_DIM), bf16),
            jax.ShapeDtypeStruct((split, rows), bf16),
            jax.ShapeDtypeStruct((pair_heads, rows, HEAD_DIM), bf16),
            jax.ShapeDtypeStruct((split, rows), bf16),
            jax.ShapeDtypeStruct((pair_heads, rows, HEAD_DIM), bf16),
        ],
        compiler_params=pltpu.CompilerParams(vmem_limit_bytes=vmem_bytes),
        cost_estimate=pl.CostEstimate(
            flops=2 * rows * width * (tall + 2 * split),
            bytes_accessed=12 * 1024 * 1024,
            transcendentals=0,
        ),
        name="project",
    )(tokens, gain, cosine, sine, w_query, w_key, w_value)


def enter_mixture_kernel(count, x_ref, gain_ref, router_ref, routes_ref, *refs):
    pieces, (hidden_ref, normed_ref, normed_t_ref, gates_ref) = refs[: 2 * count], refs[2 * count :]
    projected = 0.0
    for context_ref, w_ref in zip(pieces[:count], pieces[count:]):
        projected = projected + mm(context_ref[...].astype(f32).T.astype(bf16), w_ref[...])
    hidden = x_ref[...].astype(f32) + residual_scale * projected
    hidden_ref[...] = hidden
    normed = hidden * scale_of(hidden) * gain_ref[...].astype(f32)
    normed_t_ref[...] = normed.T.astype(bf16)
    normed = normed.astype(bf16)
    normed_ref[...] = normed
    logits = dot(router_ref[...], normed, 1, 1)
    expert = lax.broadcasted_iota(jnp.int32, logits.shape, 0)
    chosen = expert == routes_ref[0:1, :]
    for k in range(1, routes_ref.shape[0]):
        chosen = chosen | (expert == routes_ref[k : k + 1, :])
    logits = jnp.where(chosen, logits, masked_value)
    weights = jnp.exp(logits - jnp.max(logits, axis=0, keepdims=True))
    weights = jnp.where(chosen, weights, 0.0)
    gates_ref[...] = weights / jnp.sum(weights, axis=0, keepdims=True)


def enter_mixture(tokens, gain, router_t, routes_t, contexts, weights):
    rows, width = tokens.shape
    whole = lambda shape: pl.BlockSpec(shape, lambda t: (0,) * len(shape))
    down = lambda wide: pl.BlockSpec((BLOCK, wide), lambda t: (t, 0))
    across = lambda high: pl.BlockSpec((high, BLOCK), lambda t: (0, t))
    return pl.pallas_call(
        functools.partial(enter_mixture_kernel, len(contexts)),
        grid=(rows // BLOCK,),
        in_specs=[
            down(width), whole((1, width)), whole(router_t.shape), across(routes_t.shape[0]),
            *[across(context.shape[0]) for context in contexts],
            *[whole(weight.shape) for weight in weights],
        ],
        out_specs=[down(width), down(width), across(width), across(EXPERTS)],
        out_shape=[
            jax.ShapeDtypeStruct((rows, width), f32),
            jax.ShapeDtypeStruct((rows, width), bf16),
            jax.ShapeDtypeStruct((width, rows), bf16),
            jax.ShapeDtypeStruct((EXPERTS, rows), f32),
        ],
        compiler_params=pltpu.CompilerParams(vmem_limit_bytes=vmem_bytes),
        cost_estimate=pl.CostEstimate(
            flops=2 * rows * width * width, bytes_accessed=16 * 1024 * 1024, transcendentals=0
        ),
        name="enter_mixture",
    )(tokens, gain, router_t, routes_t, *contexts, *weights)


def enter_back_kernel(c_ref, own_ref, other_ref, wo_ref, ctx_ref, hidden_ref, dt_ref, d_ref, spread_ref, wo_grad_ref):
    hidden_gradient = c_ref[...].astype(f32) + (
        own_ref[...].astype(f32) + other_ref[...].astype(f32)
    )
    hidden_ref[...] = hidden_gradient
    attention_gradient = (residual_scale * hidden_gradient).astype(bf16)
    d_t = dot(wo_ref[...], attention_gradient, 1, 1)
    dt_ref[...] = d_t.astype(bf16)
    put_heads(d_ref, d_t.T.astype(bf16))
    context_t = ctx_ref[...]
    weighed = d_t.astype(bf16).astype(f32) * context_t.astype(f32)
    for h in range(spread_ref.shape[0]):
        spread_ref[h : h + 1, :] = jnp.sum(
            weighed[h * HEAD_DIM : (h + 1) * HEAD_DIM], axis=0, keepdims=True
        )

    @pl.when(pl.program_id(0) == 0)
    def start():
        wo_grad_ref[...] = jnp.zeros_like(wo_grad_ref)

    wo_grad_ref[...] += mm(context_t, attention_gradient)


def enter_back(cotangent, own, other, w_out, context_t):
    rows, width = cotangent.shape
    tall = w_out.shape[0]
    heads = tall // HEAD_DIM
    whole = lambda shape: pl.BlockSpec(shape, lambda t: (0,) * len(shape))
    down = lambda wide: pl.BlockSpec((BLOCK, wide), lambda t: (t, 0))
    across = lambda high: pl.BlockSpec((high, BLOCK), lambda t: (0, t))
    return pl.pallas_call(
        enter_back_kernel,
        grid=(rows // BLOCK,),
        in_specs=[down(width), down(width), down(width), whole((tall, width)), across(tall)],
        out_specs=[
            down(width), across(tall),
            pl.BlockSpec((heads, BLOCK, HEAD_DIM), lambda t: (0, t, 0)),
            across(heads), whole((tall, width)),
        ],
        out_shape=[
            jax.ShapeDtypeStruct((rows, width), f32),
            jax.ShapeDtypeStruct((tall, rows), bf16),
            jax.ShapeDtypeStruct((heads, rows, HEAD_DIM), bf16),
            jax.ShapeDtypeStruct((heads, rows), f32),
            jax.ShapeDtypeStruct((tall, width), f32),
        ],
        compiler_params=pltpu.CompilerParams(vmem_limit_bytes=vmem_bytes),
        cost_estimate=pl.CostEstimate(
            flops=4 * rows * width * tall, bytes_accessed=20 * 1024 * 1024, transcendentals=0
        ),
        name="enter_back",
    )(cotangent, own, other, w_out, context_t)


def leave_back_kernel(
    x_ref, gain_ref, cos_ref, sin_ref, wq_ref, wk_ref, wv_ref, normed_ref,
    dq_ref, dk_ref, dv_ref, more_dk_ref, more_dv_ref,
    part_ref, gain_grad_ref, w_grad_ref, w_sum_ref,
):
    step = pl.program_id(0)
    cosine, sine = cos_ref[...], -sin_ref[...]
    dq_t = turn(dq_ref[...], cosine, sine).astype(bf16)
    dk_t = turn(dk_ref[...] + more_dk_ref[...].astype(f32), cosine, sine).astype(bf16)
    dv_t = (dv_ref[...] + more_dv_ref[...].astype(f32)).astype(bf16)
    normed = normed_ref[...]

    @pl.when(step == 0)
    def start():
        w_sum_ref[...] = jnp.zeros_like(w_sum_ref)
        gain_grad_ref[...] = jnp.zeros_like(gain_grad_ref)

    w_sum_ref[...] += mm(jnp.concatenate([dq_t, dk_t, dv_t], axis=0), normed)
    rows_of = lambda tall: tall.astype(f32).T.astype(bf16)
    upstream = (
        dot(rows_of(dq_t), wq_ref[...], 1, 1)
        + mm(rows_of(dk_t), wk_ref[...])
        + mm(rows_of(dv_t), wv_ref[...])
    )
    x = x_ref[...].astype(f32)
    part, gain_part = norm_back(x, scale_of(x), gain_ref[...].astype(f32), upstream)
    part_ref[...] = part.astype(bf16)
    gain_grad_ref[...] += gain_part[None, :]

    @pl.when(step == pl.num_programs(0) - 1)
    def finish():
        w_grad_ref[...] = w_sum_ref[...].astype(bf16)


def leave_back(
    tokens, gain, cosine, sine, w_query, w_key, w_value, normed, dq_t, dk_t, dv_t, more_dk, more_dv
):
    rows, width = tokens.shape
    tall, split = w_query.shape[1], w_key.shape[0]
    whole = lambda shape: pl.BlockSpec(shape, lambda t: (0,) * len(shape))
    down = lambda wide: pl.BlockSpec((BLOCK, wide), lambda t: (t, 0))
    across = lambda high: pl.BlockSpec((high, BLOCK), lambda t: (0, t))
    return pl.pallas_call(
        leave_back_kernel,
        grid=(rows // BLOCK,),
        in_specs=[
            down(width), whole((1, width)), across(HEAD_DIM // 2), across(HEAD_DIM // 2),
            whole((width, tall)), whole((split, width)), whole((split, width)), down(width),
            across(tall), across(split), across(split), across(split), across(split),
        ],
        out_specs=[
            down(width), whole((1, width)), whole((tall + 2 * split, width)),
        ],
        out_shape=[
            jax.ShapeDtypeStruct((rows, width), bf16),
            jax.ShapeDtypeStruct((1, width), f32),
            jax.ShapeDtypeStruct((tall + 2 * split, width), bf16),
        ],
        scratch_shapes=[pltpu.VMEM((tall + 2 * split, width), f32)],
        compiler_params=pltpu.CompilerParams(vmem_limit_bytes=vmem_bytes),
        cost_estimate=pl.CostEstimate(
            flops=4 * rows * width * (tall + 2 * split),
            bytes_accessed=20 * 1024 * 1024,
            transcendentals=0,
        ),
        name="leave_back",
    )(
        tokens, gain, cosine, sine, w_query, w_key, w_value, normed, dq_t, dk_t, dv_t, more_dk,
        more_dv,
    )


def expert_kernel(
    adds, ids_ref, gates_ref, xt_ref, x_ref, ct_ref, c_ref, up_ref, down_ref, *refs
):
    if adds:
        more_ref, *refs = refs
    _, _, _, grad_ref, up_grad_ref, act_ref, gate_grad_ref = refs
    rows = x_ref.shape[0]
    chunk = min(BLOCK, rows)
    for part in range(rows // chunk):
        cut = pl.ds(part * chunk, chunk)
        xt = xt_ref[:, cut]
        gate = mm(up_ref[0, 0], xt)
        up = mm(up_ref[0, 1], xt)
        active_grad = mm(down_ref[0], ct_ref[:, cut])
        share = 1.0 / (1.0 + jnp.exp(-gate))
        silu = gate * share
        active = silu * up
        weight = gates_ref[0, :, cut] * residual_scale
        gate_grad_ref[0, :, cut] = residual_scale * jnp.sum(
            active * active_grad, axis=0, keepdims=True
        )
        active_grad = active_grad * weight
        act_ref[0, :, cut] = (active * weight).astype(bf16)
        up_grad_ref[0, 0, :, cut] = (
            active_grad * up * (share + silu * (1.0 - share))
        ).astype(bf16)
        up_grad_ref[0, 1, :, cut] = (active_grad * silu).astype(bf16)

    def put(place, total):
        if adds:
            total = total + more_ref[0, place].astype(f32)
        grad_ref[0, place] = total.astype(bf16)

    x = x_ref[...]
    put(0, mm(up_grad_ref[0, 0], x))
    put(1, mm(up_grad_ref[0, 1], x))
    put(2, mm(act_ref[0], c_ref[...]))


def expert_step(ids, gates, xt, x, ct, c, w_up, w_down, more, old):
    count = ids.shape[0]
    rows, width = x.shape
    units = w_down.shape[1]
    whole = lambda shape: pl.BlockSpec(shape, lambda e, s: (0,) * len(shape))
    fresh = old is None
    adds = more is not None
    each = pl.BlockSpec((1, 3, units, width), lambda e, s: (e, 0, 0, 0))
    if fresh:
        old = (jnp.zeros((8, 128), f32),) * 3
    return pl.pallas_call(
        functools.partial(expert_kernel, adds),
        grid_spec=pltpu.PrefetchScalarGridSpec(
            num_scalar_prefetch=1,
            grid=(count,),
            in_specs=[
                pl.BlockSpec((1, 1, rows), lambda e, s: (s[e], 0, 0)),
                whole((width, rows)),
                whole((rows, width)),
                whole((width, rows)),
                whole((rows, width)),
                pl.BlockSpec((1, 2, units, width), lambda e, s: (s[e], 0, 0, 0)),
                pl.BlockSpec((1, units, width), lambda e, s: (s[e], 0, 0)),
                *([each] if adds else []),
                pl.BlockSpec(memory_space=pl.ANY),
                pl.BlockSpec(memory_space=pl.ANY),
                pl.BlockSpec(memory_space=pl.ANY),
            ],
            out_specs=[
                each,
                pl.BlockSpec((1, 2, units, rows), lambda e, s: (s[e], 0, 0, 0)),
                pl.BlockSpec((1, units, rows), lambda e, s: (s[e], 0, 0)),
                pl.BlockSpec((1, 1, rows), lambda e, s: (s[e], 0, 0)),
            ],
        ),
        out_shape=[
            jax.ShapeDtypeStruct((count, 3, units, width), bf16),
            jax.ShapeDtypeStruct((EXPERTS, 2, units, rows), bf16),
            jax.ShapeDtypeStruct((EXPERTS, units, rows), bf16),
            jax.ShapeDtypeStruct((EXPERTS, 1, rows), f32),
        ],
        input_output_aliases={} if fresh else {8 + adds: 1, 9 + adds: 2, 10 + adds: 3},
        compiler_params=pltpu.CompilerParams(vmem_limit_bytes=vmem_bytes),
        cost_estimate=pl.CostEstimate(
            flops=count * 12 * rows * width * units,
            bytes_accessed=count * units * width * 12 + 8 * rows * width,
            transcendentals=count * units * rows,
        ),
        name="experts",
    )(ids, gates, xt, x, ct, c, w_up, w_down, *([more] if adds else []), *old)


def from_other_half(shard):
    return lax.ppermute(shard, "tensor", [(0, 1), (1, 0)])


def gathered(shard):
    if lax.axis_size("tensor") != 2:
        return [lax.all_gather(shard, "tensor", axis=0, tiled=True)]
    return [shard, from_other_half(shard)]


def both_parts(part):
    if lax.axis_size("tensor") != 2:
        return lax.psum(part, "tensor"), jnp.zeros_like(part)
    return part, from_other_half(part)


def summed_parts(part):
    low = part.astype(bf16)
    if lax.axis_size("tensor") != 2:
        return lax.psum(low, "tensor").astype(f32)
    return low.astype(f32) + from_other_half(low).astype(f32)


def chip_order(chips):
    there = [2 * z for z in range(chips // 2)]
    return there + [chip + 1 for chip in reversed(there)]


def chunk_experts(device, peers, number):
    order = jnp.array(chip_order(peers // 2), jnp.int32)
    each = EXPERTS // peers
    core = device % 2

    def owned(side):
        chips = jnp.where(side == 0, order, order[::-1])
        return (2 * chips + side) * each + number

    return owned(1 - core).astype(jnp.int32), owned(core).astype(jnp.int32)


def chip_rings():
    order = chip_order(lax.axis_size("dp") // 2)
    return [[2 * chip for chip in order], [2 * chip + 1 for chip in reversed(order)]]


def to_owner(chip_sum):
    return lax.psum_scatter(
        chip_sum, "dp", scatter_dimension=0, axis_index_groups=chip_rings(), tiled=True
    )


def summed_over_tokens(part):
    swap = [(i, i ^ 1) for i in range(lax.axis_size("dp"))]
    is_first = lax.axis_index("dp") % 2 == 0
    low, high = jnp.split(part, 2, axis=0)
    received = lax.ppermute(jnp.where(is_first, high, low), "dp", swap)
    half = (jnp.where(is_first, low, high).astype(f32) + received.astype(f32)).astype(bf16)
    half = lax.psum(half, "dp", axis_index_groups=chip_rings())
    other = lax.ppermute(half, "dp", swap)
    return jnp.concatenate(
        [jnp.where(is_first, half, other), jnp.where(is_first, other, half)], axis=0
    )


def angles(position):
    inverse = rope_base ** (-2.0 * jnp.arange(HEAD_DIM // 2, dtype=f32) / HEAD_DIM)
    angle = inverse[:, None] * position.astype(f32)[None, :]
    return jnp.cos(angle), jnp.sin(angle)


def scale_of(values):
    return lax.rsqrt(jnp.mean(values * values, axis=-1, keepdims=True) + epsilon)


def norm_back(values, scale, gain, upstream):
    pulled = gain * upstream
    slope = jnp.mean(pulled * values, axis=-1, keepdims=True)
    return (
        scale * pulled - values * (scale * scale * scale * slope),
        jnp.sum(upstream * values * scale, axis=0),
    )


def on_device(
    tokens, doc_ids, routes, attention_gain, w_query, w_key, w_value, w_out, mixture_gain,
    w_router, expert_gate_up, expert_down, out_cotangent,
):
    rows, width = tokens.shape
    peers = lax.axis_size("dp")
    device = lax.axis_index("dp")
    pair_heads = w_key.shape[0] // HEAD_DIM
    group = w_query.shape[1] // w_key.shape[0]
    first = device * rows
    chunks = EXPERTS // peers
    w_out_parts = gathered(w_out)

    docs = lax.dynamic_slice_in_dim(doc_ids, first, rows)
    docs_before = lax.dynamic_slice_in_dim(doc_ids, jnp.maximum(device - 1, 0) * rows, rows)
    docs_before = jnp.where(device > 0, docs_before, -1)
    docs_window = jnp.concatenate([docs_before, docs])
    lo = jnp.sum((docs_window[:, None] < docs[None, :]).astype(jnp.int32), axis=0)
    first_block = lo[::BLOCK] // BLOCK
    lo = lo[None, :]

    position = (first + jnp.arange(rows, dtype=jnp.int32)) % SEQ_LEN
    cosine, sine = angles(position)
    gain_one = attention_gain[None, :]
    normed_attention, q_t, q_rows, k_t, k_rows, v_t, v_rows = project(
        tokens, gain_one, cosine, sine, w_query, w_key, w_value
    )
    to_next = [(i, i + 1) for i in range(0, peers, 2)]
    before = SEQ_LEN - rows
    old_k_t = lax.ppermute(k_t, "dp", to_next)
    old_v_t = lax.ppermute(v_t, "dp", to_next)
    across = lambda tall: jnp.swapaxes(tall.reshape(pair_heads, HEAD_DIM, before), 1, 2)
    old_k_rows, old_v_rows = across(old_k_t), across(old_v_t)

    context_t, logs = attend(first_block, lo, q_t, k_rows, v_t, old_k_rows, old_v_t, group)
    hidden, normed_mixture, normed_t, gates = enter_mixture(
        tokens, mixture_gain[None, :], w_router.T, routes.T, gathered(context_t), w_out_parts
    )
    gain_two = mixture_gain.astype(f32)
    scale_two = scale_of(hidden)

    upstream_t = out_cotangent.T
    swap_cores = [(i, i ^ 1) for i in range(peers)]
    shares, old = [], None

    def run_experts(ids):
        return expert_step(
            ids, gates[:, None, :], normed_t, normed_mixture, upstream_t, out_cotangent,
            expert_gate_up, expert_down, None, old,
        )

    for number in range(chunks):
        other_ids, own_ids = chunk_experts(device, peers, number)
        send, *old = run_experts(other_ids)
        received = lax.ppermute(send, "dp", swap_cores)
        keep, *old = run_experts(own_ids)
        if number < chunks - 1:
            chip_sum = (keep.astype(f32) + received.astype(f32)).astype(bf16)
            chip_sum, *old = lax.optimization_barrier((chip_sum, *old))
            shares.append(to_owner(chip_sum))
    up_grad, act, gates_gradient = old
    gates_gradient = gates_gradient[:, 0]
    units = expert_down.shape[1]
    wide = EXPERTS * units

    logits_gradient = gates * (
        gates_gradient - jnp.sum(gates * gates_gradient, axis=0, keepdims=True)
    )
    logits_low = logits_gradient.astype(bf16)
    router_gradient = mm(logits_low, normed_mixture)
    up_grad = up_grad.reshape(2 * wide, rows)
    w_up = expert_gate_up.reshape(2 * wide, width)
    own_parts, other_parts, gain_parts = [], [], []
    for start in range(0, rows, rows // 2):
        cut = slice(start, start + rows // 2)
        if start > 0:
            up_grad, own_parts[0] = lax.optimization_barrier((up_grad, own_parts[0]))
        normed_gradient = dot(up_grad[:, cut], w_up, 0, 0) + dot(logits_low[:, cut], w_router, 0, 1)
        part, gain_part = norm_back(hidden[cut], scale_two[cut], gain_two, normed_gradient)
        part = part.astype(bf16)
        if start > 0:
            part, act, keep, received, other_parts[0] = lax.optimization_barrier(
                (part, act, keep, received, other_parts[0])
            )
        own, other = both_parts(part)
        own_parts.append(own)
        other_parts.append(other)
        gain_parts.append(gain_part)
    second_gain_part = gain_parts[0] + gain_parts[1]
    chip_sum = (keep.astype(f32) + received.astype(f32)).astype(bf16)
    shares.append(to_owner(chip_sum))

    mixture_part = dot(act.reshape(wide, rows), expert_down.reshape(wide, width), 0, 0)
    mixture_low = mixture_part.astype(bf16)
    own_part = jnp.concatenate(own_parts, axis=0)
    other_part = jnp.concatenate(other_parts, axis=0)
    own_part, other_part, mixture_low = lax.optimization_barrier(
        (own_part, other_part, mixture_low)
    )
    mixed = (hidden + summed_parts(mixture_low)).astype(bf16)

    hidden_gradient, d_t, d_rows, spread, w_out_gradient = enter_back(
        out_cotangent, own_part, other_part, w_out, context_t
    )
    by_group = lambda rows_of_heads: rows_of_heads.reshape(pair_heads, group, rows, HEAD_DIM)
    back = functools.partial(
        attend_back, first_block, lo, logs, spread.reshape(pair_heads, group, rows), q_t, d_t,
        by_group(q_rows), by_group(d_rows),
    )
    dq_t, old_dk, old_dv = back(
        old_k_rows, old_k_t, old_v_rows, jnp.zeros((q_t.shape[0], rows), f32), before, True
    )
    to_previous = [(i + 1, i) for i in range(0, peers, 2)]
    more_dk = lax.ppermute(old_dk, "dp", to_previous)
    more_dv = lax.ppermute(old_dv, "dp", to_previous)
    dq_t, dk_t, dv_t = back(k_rows, k_t, v_rows, dq_t, before, False)
    dq_t, mixed = lax.optimization_barrier((dq_t, mixed))
    if chunks > 1:
        dq_t, shares[0] = lax.optimization_barrier((dq_t, shares[0]))
    input_part, first_gain_part, w_gradients = leave_back(
        tokens, gain_one, cosine, sine, w_query, w_key, w_value, normed_attention, dq_t, dk_t, dv_t,
        more_dk, more_dv,
    )
    tokens_gradient = (hidden_gradient + summed_parts(input_part)).astype(bf16)
    small = jnp.concatenate([router_gradient, second_gain_part[None, :], first_gain_part], axis=0)
    small = summed_parts(small).astype(bf16)
    tall, split = w_query.shape[1], w_key.shape[0]
    ends = [tall, tall + split, tall + 2 * split, 2 * tall + 2 * split, 2 * tall + 2 * split + EXPERTS]
    filler = jnp.zeros((-(ends[-1] + 2) % 64, width), bf16)
    gradients = jnp.concatenate([w_gradients, w_out_gradient.astype(bf16), small, filler], axis=0)
    shares[-1], gradients, tokens_gradient = lax.optimization_barrier(
        (shares[-1], gradients, tokens_gradient)
    )
    gradients = summed_over_tokens(gradients).astype(f32)
    w_q, w_k, w_v, w_o, router, gains = jnp.split(gradients, ends, axis=0)
    experts_gradient = jnp.concatenate(shares, axis=0).astype(f32)
    return (
        mixed, tokens_gradient, gains[1], w_q.T, w_k, w_v, w_o, gains[0], router.T,
        experts_gradient[:, :2], experts_gradient[:, 2],
    )


def solution(mesh):
    placed = (
        P("dp", None),
        P(),
        P("dp", None),
        P(),
        P(None, "tensor"),
        P("tensor", None),
        P("tensor", None),
        P("tensor", None),
        P(),
        P(),
        P(None, None, "tensor", None),
        P(None, "tensor", None),
        P("dp", None),
    )
    return jax.shard_map(
        on_device,
        mesh=mesh,
        in_specs=placed,
        out_specs=(
            P("dp", None),
            P("dp", None),
            P(),
            P(None, "tensor"),
            P("tensor", None),
            P("tensor", None),
            P("tensor", None),
            P(),
            P(),
            P("dp", None, "tensor", None),
            P("dp", "tensor", None),
        ),
        check_vma=False,
    )
```

time: 1810 us -> 613 us (0.34)
  waiting for transfers between devices: 605 us -> 135 us
  matrix products: 434 us -> 76.4 us
  local copies, waits for them, and re-layouts: 381 us -> 55.6 us
  other arithmetic: 323 us -> 60.9 us
  Pallas kernels: 0 us -> 221 us
  starting transfers between devices: 5.51 us -> 45.1 us
  blocking collectives: 37.9 us -> 0 us
    reduce_scatter x1 -> x2, waiting for transfers between devices: 462 us -> 0.01 us  [to_owner(): lax.psum_scatter(chip_sum, 'dp', scatter_dimension=0, axis_index_groups=c...]
    dot_general x35 -> x6, matrix products: 434 us -> 76.4 us  [the longest x5 75.9 us: dot(): lax.dot_general(left, right, (((left_dim,), (right_dim,)), ((), ())), pre...]
    gather x4 -> x0, local copies, waits for them, and re-layouts: 247 us -> none  [the longest x1 68 us: on_device(): gate_padded[source][:, None]]
    pallas_call x0 -> x11, Pallas kernels: none -> 221 us  [the longest x4 141 us: expert_step(): pl.pallas_call(functools.partial(expert_kernel, adds), grid_spec=pltpu.Pr...]
    scatter-add x1 -> x0, other arithmetic: 108 us -> none  [on_device(): normed_gradient = jnp.zeros((rows + 1, width), jnp.float32).at[token_of]....]
    reduce_sum x10 -> x3, other arithmetic: 53.9 us -> 1.35 us  [the longest x1 0.97 us: on_device(): jnp.sum((docs_window[:, None] < docs[None, :]).astype(jnp.int32), axis=0)]
    psum x4 -> x1, waiting for transfers between devices: 142 us -> 92.3 us  [summed_over_tokens(): half = lax.psum(half, 'dp', axis_index_groups=chip_rings())]
    dynamic_update_slice x8 -> x0, local copies, waits for them, and re-layouts: 45.5 us -> none  [the longest x4 41.4 us: on_device(): lax.scan(backward_block, (zero_pairs, zero_pairs), (query_blocks, place_b...]
  transfers between devices with their start and end apart: 7 -> 18, of which waited for: 5 -> 4; matrix products, arithmetic and copies ran while one was open for 16% -> 23% of each run, Pallas kernels for 0% -> 29%
where the time goes in v1:
time: 613 us; the launch traced here: 609 us
  Pallas kernels  221 us (36%)
  waiting for transfers between devices  135 us (22%)
  matrix products  76.4 us (12%)
  other arithmetic  60.9 us (10%)
  local copies, waits for them, and re-layouts  55.6 us (9%)
  starting transfers between devices  45.1 us (7%)
  between operations  14.6 us (2%)
    pallas_call x4, Pallas kernels, expert_step(): pl.pallas_call(functools.partial(expert_kernel, adds), grid_spec=pltpu.Pr...  141 us
    psum x1, waiting for transfers between devices, summed_over_tokens(): half = lax.psum(half, 'dp', axis_index_groups=chip_rings())  92.3 us
    dot_general x5, matrix products, dot(): lax.dot_general(left, right, (((left_dim,), (right_dim,)), ((), ())), pre...  75.9 us
    ppermute x7, waiting for transfers between devices, from_other_half(): return lax.ppermute(shard, 'tensor', [(0, 1), (1, 0)])  39.6 us
    unnamed x134, local copies, waits for them, and re-layouts  35.5 us
    convert_element_type x2, other arithmetic, on_device(): chip_sum = (keep.astype(f32) + received.astype(f32)).astype(bf16)  31.6 us
    pallas_call x2, Pallas kernels, attend_back(): pl.pallas_call(functools.partial(attend_back_kernel, group, earlier, befo...  29.5 us
    ppermute x1, starting transfers between devices, summed_over_tokens(): received = lax.ppermute(jnp.where(is_first, high, low), 'dp', swap)  17.4 us
  transfers between devices with their start and end apart: 18, of which 4 were waited for; matrix products, arithmetic and copies ran while one was open for 23% of the time, Pallas kernels for 29%

profile of v1, /device:TPU:0, one launch (start us, length us, event | category | flops | bytes accessed | tf_op | source)
XLA Modules:
  0.0 609.1 jit_solution(6990014221685215191)
XLA Ops:
  7.2 3.0 collective-permute-start.3
  11.5 1.1 copy-done.28
  12.7 1.0 copy-done.30
  13.7 7.7 %project.1 = (bf16[1024,1024]{1,0:T(8,128)(2,1)}, bf16[512,1024]{1,0:T(8,128)(2,1)S(1)}, bf16[8,1024,64]{2,1,0:T(8,128)(2,1)}, bf16[256,1024]{1,0:T(8,128)(2,1)S...) custom-call(bf16[1024,1024]{1,0:T(8,128)(2,1)} %x_ref.5, ...), custom_call_target="tpu_custom_call" | custom-call | flops 2147483648 | bytes 12582912 | tf_op jit(solution)/shard_map/project/pallas_call | solution.py:287
  23.3 1.0 copy-done.45
  24.3 1.5 collective-permute-start.1
  25.8 1.8 collective-permute-start
  30.3 1.5 copy-done.40
  31.8 1.2 copy-done.43
  33.0 15.5 %attend.1 = (bf16[512,1024]{1,0:T(8,128)(2,1)S(1)}, f32[4,2,1024]{2,1,0:T(2,128)S(1)}) custom-call(s32[4]{0:T(128)S(1)} %and_select_fusion.first_ref, s32[1,1024]{1,0:T(1,128)S(1)} %bitcast.54, bf16[512,1024]{1,0:T(8,128)(2,1)S(1)} %copy-done.40, bf16[4,1024,64]{2,1,0:T(8,128)(2,1)S(1)} %copy-done.43, bf16[256,1024]{1,0:T(8,128)(2,1)S(1)} %get-tuple-element.77.vt_ref, ...), custom_call_target="tpu_custom_call" | custom-call | flops 8589934592 | bytes 8388608 | tf_op jit(solution)/shard_map/attend/pallas_call | solution.py:113
  49.5 4.0 copy.45
  53.6 10.4 %collective-permute-done.2.refs_1_ = bf16[512,1024]{1,0:T(8,128)(2,1)S(1)} collective-permute-done((bf16[512,1024]{1,0:T(8,128)(2,1)S(1)}, bf16[512,1024]{1,0:T(8,128)(2,1)S(1)}, u32[]{:S(2)}, u32[]{:S(2)}) %collective-permute-start.2) | collective-permute-done | bytes 1048608 | tf_op jit(solution)/shard_map/ppermute | solution.py:585
  63.9 7.8 %enter_mixture.1 = (f32[1024,1024]{1,0:T(8,128)}, bf16[1024,1024]{1,0:T(8,128)(2,1)}, bf16[1024,1024]{1,0:T(8,128)(2,1)}, f32[32,1024]{1,0:T(8,128)S(1)}) custom-call(bf16[1024,1024]{1,0:T(8,128)(2,1)} %x_ref.5, bf16[1,1024]{1,0:T(2,128)(2,1)S(1)} %broadcast_in_dim.21.gain_ref, bf16[32,1024]{1,0:T(8,128)(2,1)S(1)} %bitcast.50, s32[8,1024]{1,0:T(8,128)S(1)} %bitcast.53, ...), custom_call_target="tpu_custom_call" | custom-call | flops 2147483648 | bytes 16777216 | tf_op jit(solution)/shard_map/enter_mixture/pallas_call | solution.py:344
  71.9 1.6 copy-done
  73.5 1.6 copy-done.2
  75.1 35.2 %experts.4 = (bf16[8,3,256,1024]{3,2,1,0:T(8,128)(2,1)}, bf16[32,2,256,1024]{3,2,1,0:T(8,128)(2,1)}, bf16[32,256,1024]{2,1,0:T(8,128)(2,1)}, f32[32,1,1024]{2,1,0:T(1,128)S(1)}) custom-call(s32[8]{0:T(128)S(1)} %get-tuple-element.177.ids_ref, f32[32,1,1024]{2,1,0:T(1,128)S(1)} %broadcast_in_dim.22.gates_ref, bf16[1024,1024]{1,0:T(8,128)(2,1)S(1)} %copy-done.2, ...), custom_call_target="tpu_custom_call" | custom-call | flops 25769803776 | bytes 33554432 | tf_op jit(solution)/shard_map/experts/pallas_call | solution.py:542
  110.2 14.4 %collective-permute-start.4 = (bf16[8,3,256,1024]{3,2,1,0:T(8,128)(2,1)}, bf16[8,3,256,1024]{3,2,1,0:T(8,128)(2,1)}, u32[]{:S(2)}, u32[]{:S(2)}) collective-permute-start(bf16[8,3,256,1024]{3,2,1,0:T(8,128)(2,1)} %get-tuple-element.88), channel_id=1, source_target_pairs={{0,2},{2,0},{4,6},{6,4},{8,10},{10,8},{12,14},{14,12},{16,18},{18,... | collective-permute-start | bytes 37748744 | tf_op jit(solution)/shard_map/ppermute | solution.py:721
  124.7 35.2 %experts.5 = (bf16[8,3,256,1024]{3,2,1,0:T(8,128)(2,1)}, bf16[32,2,256,1024]{3,2,1,0:T(8,128)(2,1)}, bf16[32,256,1024]{2,1,0:T(8,128)(2,1)}, f32[32,1,1024]{2,1,0:T(1,128)S(1)}) custom-call(s32[8]{0:T(128)S(1)} %get-tuple-element.195.ids_ref, ...), custom_call_target="tpu_custom_call", output_to_operand_aliasing={{1}: (8, {}), {2}: (9, {}), {3}: (10, {})} | custom-call | flops 25769803776 | bytes 33554432 | tf_op jit(solution)/shard_map/experts/pallas_call | solution.py:542
  159.9 15.7 %add_convert_fusion.1 = bf16[8,3,256,1024]{3,2,1,0:T(8,128)(2,1)} fusion(bf16[8,3,256,1024]{3,2,1,0:T(8,128)(2,1)} %collective-permute-done.4, bf16[8,3,256,1024]{3,2,1,0:T(8,128)(2,1)} %get-tuple-element.87), kind=kLoop, calls=%fused_computation.1 | loop fusion | flops 25165824 | bytes 37748736 | tf_op jit(solution)/shard_map/convert_element_type | solution.py:724
  175.6 1.5 copy-done.1
  177.1 1.6 copy-done.3
  178.7 35.4 %experts.6 = (bf16[8,3,256,1024]{3,2,1,0:T(8,128)(2,1)}, bf16[32,2,256,1024]{3,2,1,0:T(8,128)(2,1)}, bf16[32,256,1024]{2,1,0:T(8,128)(2,1)}, f32[32,1,1024]{2,1,0:T(1,128)S(1)}) custom-call(s32[8]{0:T(128)S(1)} %get-tuple-element.176.ids_ref, ...), custom_call_target="tpu_custom_call", output_to_operand_aliasing={{1}: (8, {}), {2}: (9, {}), {3}: (10, {})} | custom-call | flops 25769803776 | bytes 33554432 | tf_op jit(solution)/shard_map/experts/pallas_call | solution.py:542
  214.6 35.0 %experts.7 = (bf16[8,3,256,1024]{3,2,1,0:T(8,128)(2,1)}, bf16[32,2,256,1024]{3,2,1,0:T(8,128)(2,1)}, bf16[32,256,1024]{2,1,0:T(8,128)(2,1)}, f32[32,1,1024]{2,1,0:T(1,128)S(1)}) custom-call(s32[8]{0:T(128)S(1)} %get-tuple-element.194.ids_ref, ...), custom_call_target="tpu_custom_call", output_to_operand_aliasing={{1}: (8, {}), {2}: (9, {}), {3}: (10, {})} | custom-call | flops 25769803776 | bytes 33554432 | tf_op jit(solution)/shard_map/experts/pallas_call | solution.py:542
  249.7 25.0 %fusion = f32[512,1024]{1,0:T(8,128)S(1)} fusion(bf16[16384,1024]{1,0:T(8,128)(2,1)} %bitcast.57, bf16[16384,1024]{1,0:T(8,128)(2,1)} %bitcast.59), kind=kOutput, calls=%fused_computation.2 | convolution fusion | flops 17179869184 | bytes 52428800 | tf_op jit(solution)/shard_map/dot_general | solution.py:26
  276.0 25.0 %fusion.2 = f32[512,1024]{1,0:T(8,128)S(1)} fusion(bf16[16384,1024]{1,0:T(8,128)(2,1)} %bitcast.58, bf16[16384,1024]{1,0:T(8,128)(2,1)} %bitcast.60), kind=kOutput, calls=%fused_computation.4 | convolution fusion | flops 17179869184 | bytes 52428800 | tf_op jit(solution)/shard_map/dot_general | solution.py:26
  301.8 1.3 subtract_convert_fusion
  303.1 15.9 %add_convert_fusion = bf16[8,3,256,1024]{3,2,1,0:T(8,128)(2,1)} fusion(bf16[8,3,256,1024]{3,2,1,0:T(8,128)(2,1)} %collective-permute-done.5, bf16[8,3,256,1024]{3,2,1,0:T(8,128)(2,1)} %get-tuple-element.120), kind=kLoop, calls=%fused_computation | loop fusion | flops 25165824 | bytes 37748736 | tf_op jit(solution)/shard_map/convert_element_type | solution.py:756
  320.1 1.3 copy.47
  321.4 1.7 collective-permute-start.7
  323.1 24.3 %bitcast_convert_fusion = bf16[1024,1024]{1,0:T(8,128)(2,1)} fusion(bf16[32,256,1024]{2,1,0:T(8,128)(2,1)} %get-tuple-element.108, bf16[32,256,1024]{2,1,0:T(8,128)(2,1)} %down_ref.7), kind=kOutput, calls=%fused_computation.7 | convolution fusion | flops 17180917760 | bytes 35651584 | tf_op jit(solution)/shard_map/dot_general | solution.py:26
  347.5 1.5 pad_maximum_fusion.own_ref
  349.1 1.5 pad_maximum_fusion.1.other_ref
  351.3 9.7 %enter_back.1 = (f32[1024,1024]{1,0:T(8,128)}, bf16[512,1024]{1,0:T(8,128)(2,1)S(1)}, bf16[8,1024,64]{2,1,0:T(8,128)(2,1)S(1)}, f32[8,1024]{1,0:T(8,128)S(1)}, f32[512,1024]{1,0:T(8,128)}) custom-call(bf16[1024,1024]{1,0:T(8,128)(2,1)} %c_ref.9, bf16[1024,1024]{1,0:T(8,128)(2,1)} %pad_maximum_fusion.own_ref, bf16[1024,1024]{1,0:T(8,128)(2,1)} %pad_maximum_fusion.1.other_ref, ...), custom_call_target="tpu_custom_call" | custom-call | flops 2147483648 | bytes 20971520 | tf_op jit(solution)/shard_map/enter_back/pallas_call | solution.py:397
  361.0 1.3 copy-done.23
  362.3 1.0 copy-done.25
  363.4 1.6 broadcast_in_dim.45.sum_ref
  365.7 1.0 copy-done.12
  366.7 1.2 copy-done.26
  368.0 1.2 copy-done.41
  369.2 6.7 %attend_back.2 = (f32[512,1024]{1,0:T(8,128)}, bf16[256,1024]{1,0:T(8,128)(2,1)}, bf16[256,1024]{1,0:T(8,128)(2,1)}) custom-call(s32[4]{0:T(128)S(1)} %copy-done.38, s32[1,1024]{1,0:T(1,128)S(1)} %bitcast.55, f32[4,2,1024]{2,1,0:T(2,128)S(1)} %copy-done.51, f32[4,2,1024]{2,1,0:T(2,128)S(1)} %reshape.131.spread_ref, bf16[512,1024]{1,0:T(8,128)(2,1)S(1)} %copy-done.41, ...), custom_call_target="tpu_custom_call" | custom-call | flops 10737418240 | bytes 10485760 | tf_op jit(solution)/shard_map/attend_back/pallas_call | solution.py:206
  375.9 1.3 collective-permute-start.9
  377.2 1.3 collective-permute-start.10
  378.6 22.7 %attend_back.3 = (f32[512,1024]{1,0:T(8,128)}, f32[256,1024]{1,0:T(8,128)S(1)}, f32[256,1024]{1,0:T(8,128)S(1)}) custom-call(s32[4]{0:T(128)S(1)} %copy-done.38, s32[1,1024]{1,0:T(1,128)S(1)} %bitcast.56, f32[4,2,1024]{2,1,0:T(2,128)S(1)} %copy-done.51, f32[4,2,1024]{2,1,0:T(2,128)S(1)} %reshape.131.spread_ref, bf16[512,1024]{1,0:T(8,128)(2,1)S(1)} %copy-done.41, ...), custom_call_target="tpu_custom_call" | custom-call | flops 10737418240 | bytes 10485760 | tf_op jit(solution)/shard_map/attend_back/pallas_call | solution.py:206
  402.3 5.2 add_convert_fusion.3
  407.6 1.0 copy-done.29
  408.6 1.0 copy-done.31
  409.7 1.2 copy-done.47
  410.9 1.3 copy-done.49
  412.1 10.4 %leave_back.1 = (bf16[1024,1024]{1,0:T(8,128)(2,1)}, f32[1,1024]{1,0:T(1,128)S(1)}, bf16[1024,1024]{1,0:T(8,128)(2,1)}) custom-call(bf16[1024,1024]{1,0:T(8,128)(2,1)} %x_ref.5, bf16[1,1024]{1,0:T(2,128)(2,1)S(1)} %copy-done.22, f32[32,1024]{1,0:T(8,128)S(1)} %copy-done.20, f32[32,1024]{1,0:T(8,128)S(1)} %copy-done.18, bf16[1024,512]{1,0:T(8,128)(2,1)S(1)} %copy-done.24, ...), custom_call_target="tpu_custom_call" | custom-call | flops 4294967296 | bytes 20971520 | tf_op jit(solution)/shard_map/leave_back/pallas_call | solution.py:463
  422.6 1.5 collective-permute-start.12
  425.3 1.1 convert_element_type.105
  426.4 29.2 %collective-permute-done.11 = bf16[34,1024]{1,0:T(8,128)(2,1)S(1)} collective-permute-done((bf16[34,1024]{1,0:T(8,128)(2,1)S(1)}, bf16[34,1024]{1,0:T(8,128)(2,1)S(1)}, u32[]{:S(2)}, u32[]{:S(2)}) %collective-permute-start.11) | collective-permute-done | bytes 69664 | tf_op jit(solution)/shard_map/ppermute | solution.py:585
  455.6 11.5 %concatenate.26 = bf16[1600,1024]{1,0:T(8,128)(2,1)S(1)} concatenate(bf16[1024,1024]{1,0:T(8,128)(2,1)} %get-tuple-element.130, bf16[512,1024]{1,0:T(8,128)(2,1)} %convert_element_type.105, bf16[34,1024]{1,0:T(8,128)(2,1)S(1)} %add_convert_fusion.5, bf16[30,1024]{1,0:T(8,128)(2,1)S(1)} %broadcast_in_dim.46), dimensions={0} | concatenate | bytes 6553600 | tf_op jit(solution)/shard_map/concatenate | solution.py:796
  467.2 5.9 add_convert_fusion.2
  473.2 17.4 %collective-permute-start.13 = (bf16[800,1024]{1,0:T(8,128)(2,1)S(1)}, bf16[800,1024]{1,0:T(8,128)(2,1)S(1)}, u32[]{:S(2)}, u32[]{:S(2)}) collective-permute-start(bf16[800,1024]{1,0:T(8,128)(2,1)S(1)} %broadcast_select_fusion.2), channel_id=1, source_target_pairs={{0,2},{2,0},{4,6},{6,4},{8,10},{10,8},{12,14},{14,12},{16,18},{18,... | collective-permute-start | bytes 4915208 | tf_op jit(solution)/shard_map/ppermute | solution.py:639
  490.7 3.1 collective-permute-done.13
  493.8 2.3 add_convert_fusion.4
  496.1 92.3 %all-reduce.2.cloned.1.call-done = bf16[800,1024]{1,0:T(8,128)(2,1)} async-done(((bf16[800,1024]{1,0:T(8,128)(2,1)}), bf16[800,1024]{1,0:T(8,128)(2,1)}) %all-reduce.2.cloned.1.call-update) | async-done | bytes 1638416 | tf_op jit(solution)/shard_map/psum | solution.py:641
  588.4 1.8 maximum_convert_fusion.1
  590.2 2.6 slice.65
  592.8 1.5 convert_bitcast_fusion
  596.5 1.6 maximum_convert_fusion.2
  598.9 1.6 fusion.24
  600.5 1.8 copy.48
  (180 shorter events, 17.6 us)
Async XLA Ops:
  7.2 400.3 %reduce-scatter.5.cloned.1.call-start = ((), (), s32[]{:S(2)}) async-start(), calls=%async_computation.3 | async-start | bytes 14155776 | tf_op jit(solution)/shard_map/reduce_scatter | solution.py:630
  7.2 46.3 %collective-permute-start.3 = (bf16[512,1024]{1,0:T(8,128)(2,1)}, bf16[512,1024]{1,0:T(8,128)(2,1)}, u32[]{:S(2)}, u32[]{:S(2)}) collective-permute-start(bf16[512,1024]{1,0:T(8,128)(2,1)} %wo_ref.1), channel_id=1, source_target_pairs={{0,1},{1,0},{2,3},{3,2},{4,5},{5,4},{6,7},{7,6},{8,9},{9,8},{10,11... | collective-permute-start | bytes 3145736 | tf_op jit(solution)/shard_map/ppermute | solution.py:585
  11.0 10.4 %copy-start.21 = (bf16[1,1024]{1,0:T(2,128)(2,1)}, bf16[1,1024]{1,0:T(2,128)(2,1)S(1)}, u32[]{:S(2)}) copy-start(bf16[1,1024]{1,0:T(2,128)(2,1)S(1)} %broadcast_in_dim.20.gain_ref) | copy-start | bytes 6148
  11.5 9.9 %copy-start.17 = (f32[32,1024]{1,0:T(8,128)}, f32[32,1024]{1,0:T(8,128)S(1)}, u32[]{:S(2)}) copy-start(f32[32,1024]{1,0:T(8,128)S(1)} %get-tuple-element.190.sin_ref) | copy-start | bytes 393220
  11.5 9.9 %copy-start.19 = (f32[32,1024]{1,0:T(8,128)}, f32[32,1024]{1,0:T(8,128)S(1)}, u32[]{:S(2)}) copy-start(f32[32,1024]{1,0:T(8,128)S(1)} %get-tuple-element.191.cos_ref) | copy-start | bytes 393220
  24.3 5.7 copy-start.32
  24.3 5.7 collective-permute-start.1
  25.8 3.7 collective-permute-start
  29.3 19.1 %copy-start.35 = (s32[1024]{0:T(1024)}, s32[1024]{0:T(1024)S(1)}, u32[]{:S(2)}) copy-start(s32[1024]{0:T(1024)S(1)} %convert_reduce_fusion) | copy-start | bytes 12292
  29.5 19.0 %copy-start.37 = (s32[4]{0:T(128)}, s32[4]{0:T(128)S(1)}, u32[]{:S(2)}) copy-start(s32[4]{0:T(128)S(1)} %and_select_fusion.first_ref) | copy-start | bytes 52
  30.0 18.5 %copy-start.4 = (bf16[4,64,1024]{1,2,0:T(8,128)(2,1)}, bf16[4,64,1024]{1,2,0:T(8,128)(2,1)S(1)}, u32[]{:S(2)}) copy-start(bf16[4,64,1024]{1,2,0:T(8,128)(2,1)S(1)} %copy.44) | copy-start | bytes 1572868
  30.0 18.5 %copy-start.13 = (bf16[256,1024]{1,0:T(8,128)(2,1)}, bf16[256,1024]{1,0:T(8,128)(2,1)S(1)}, u32[]{:S(2)}) copy-start(bf16[256,1024]{1,0:T(8,128)(2,1)S(1)} %collective-permute-done.1.old_vt_ref) | copy-start | bytes 1572868
  33.0 16.5 %copy-start.63 = (bf16[1024]{0:T(1024)(128)(2,1)S(1)}, bf16[1024]{0:T(1024)(128)(2,1)}, u32[]{:S(2)}) copy-start(bf16[1024]{0:T(1024)(128)(2,1)} %param.23) | copy-start | bytes 6148
  49.1 14.8 %copy-start.9 = (bf16[512,1024]{1,0:T(8,128)(2,1)}, bf16[512,1024]{1,0:T(8,128)(2,1)S(1)}, u32[]{:S(2)}) copy-start(bf16[512,1024]{1,0:T(8,128)(2,1)S(1)} %get-tuple-element.80.refs_0_.ctx_ref) | copy-start | bytes 3145732
  49.1 14.8 %collective-permute-start.2 = (bf16[512,1024]{1,0:T(8,128)(2,1)S(1)}, bf16[512,1024]{1,0:T(8,128)(2,1)S(1)}, u32[]{:S(2)}, u32[]{:S(2)}) collective-permute-start(bf16[512,1024]{1,0:T(8,128)(2,1)S(1)} %get-tuple-element.80.refs_0_.ctx_ref), channel_id=1, source_target_pairs={{0,1},{1,0},{2,3},{3,2},{4,5},{5,4},{6,7},{7,6},{8,9},{9,8},{10,11... | collective-permute-start | bytes 3145736 | tf_op jit(solution)/shard_map/ppermute | solution.py:585
  49.4 4.1 copy-start.64
  49.5 4.1 copy-start.65
  49.5 14.5 %copy-start.7 = (bf16[512,1024]{1,0:T(8,128)(2,1)S(1)}, bf16[512,1024]{1,0:T(8,128)(2,1)}, u32[]{:S(2)}) copy-start(bf16[512,1024]{1,0:T(8,128)(2,1)} %wo_ref.1) | copy-start | bytes 3145732
  49.5 14.5 %copy-start.15 = (bf16[1024,32]{0,1:T(8,128)(2,1)S(1)}, bf16[1024,32]{0,1:T(8,128)(2,1)}, u32[]{:S(2)}) copy-start(bf16[1024,32]{0,1:T(8,128)(2,1)} %param.24) | copy-start | bytes 196612
  49.5 14.4 %copy-start.34 = (s32[1024,8]{0,1:T(8,128)S(1)}, s32[1024,8]{0,1:T(8,128)}, u32[]{:S(2)}) copy-start(s32[1024,8]{0,1:T(8,128)} %param.17) | copy-start | bytes 98308
  71.9 1.6 copy-start
  73.5 1.6 copy-start.2
  110.2 49.7 %collective-permute-start.4 = (bf16[8,3,256,1024]{3,2,1,0:T(8,128)(2,1)}, bf16[8,3,256,1024]{3,2,1,0:T(8,128)(2,1)}, u32[]{:S(2)}, u32[]{:S(2)}) collective-permute-start(bf16[8,3,256,1024]{3,2,1,0:T(8,128)(2,1)} %get-tuple-element.88), channel_id=1, source_target_pairs={{0,2},{2,0},{4,6},{6,4},{8,10},{10,8},{12,14},{14,12},{16,18},{18,... | collective-permute-start | bytes 37748744 | tf_op jit(solution)/shard_map/ppermute | solution.py:721
  175.5 1.6 copy-start.1
  175.6 297.5 %reduce-scatter.3.cloned.1.call-start = ((), (), s32[]{:S(2)}) async-start(), calls=%async_computation.2 | async-start | bytes 14155776 | tf_op jit(solution)/shard_map/reduce_scatter | solution.py:630
  177.1 1.6 copy-start.3
  178.7 35.5 %copy-start.52 = (f32[1024,1024]{1,0:T(8,128)S(1)}, f32[1024,1024]{1,0:T(8,128)}, u32[]{:S(2)}) copy-start(f32[1024,1024]{1,0:T(8,128)} %get-tuple-element.99) | copy-start | bytes 12582916
  214.2 89.0 %collective-permute-start.5 = (bf16[8,3,256,1024]{3,2,1,0:T(8,128)(2,1)}, bf16[8,3,256,1024]{3,2,1,0:T(8,128)(2,1)}, u32[]{:S(2)}, u32[]{:S(2)}) collective-permute-start(bf16[8,3,256,1024]{3,2,1,0:T(8,128)(2,1)} %get-tuple-element.105), channel_id=1, source_target_pairs={{0,2},{2,0},{4,6},{6,4},{8,10},{10,8},{12,14},{14,12},{16,18},{18,... | collective-permute-start | bytes 37748744 | tf_op jit(solution)/shard_map/ppermute | solution.py:721
  249.6 25.0 %copy-start.16 = (bf16[1024,32]{0,1:T(8,128)(2,1)S(1)}, bf16[1024,32]{0,1:T(8,128)(2,1)}, u32[]{:S(2)}) copy-start(bf16[1024,32]{0,1:T(8,128)(2,1)} %param.24) | copy-start | bytes 196612
  275.9 25.1 %copy-start.56 = (bf16[512,1024]{1,0:T(8,128)(2,1)}, bf16[512,1024]{1,0:T(8,128)(2,1)S(1)}, u32[]{:S(2)}) copy-start(bf16[512,1024]{1,0:T(8,128)(2,1)S(1)} %subtract_convert_fusion.1) | copy-start | bytes 3145732
  275.9 27.2 %collective-permute-start.6 = (bf16[512,1024]{1,0:T(8,128)(2,1)S(1)}, bf16[512,1024]{1,0:T(8,128)(2,1)S(1)}, u32[]{:S(2)}, u32[]{:S(2)}) collective-permute-start(bf16[512,1024]{1,0:T(8,128)(2,1)S(1)} %subtract_convert_fusion.1), channel_id=1, source_target_pairs={{0,1},{1,0},{2,3},{3,2},{4,5},{5,4},{6,7},{7,6},{8,9},{9,8},{10,11... | collective-permute-start | bytes 3145736 | tf_op jit(solution)/shard_map/ppermute | solution.py:585
  303.1 15.9 %copy-start.61 = (bf16[512,1024]{1,0:T(8,128)(2,1)}, bf16[512,1024]{1,0:T(8,128)(2,1)S(1)}, u32[]{:S(2)}) copy-start(bf16[512,1024]{1,0:T(8,128)(2,1)S(1)} %collective-permute-done.6) | copy-start | bytes 3145732
  319.1 269.3 %all-reduce.2.cloned.1.call-start = ((), (), s32[]{:S(2)}) async-start(), calls=%async_computation.4 | async-start | bytes 3276800 | tf_op jit(solution)/shard_map/psum | solution.py:641
  321.4 26.0 %copy-start.57 = (bf16[512,1024]{1,0:T(8,128)(2,1)S(1)}, bf16[512,1024]{1,0:T(8,128)(2,1)}, u32[]{:S(2)}) copy-start(bf16[512,1024]{1,0:T(8,128)(2,1)} %copy-done.56) | copy-start | bytes 3145732
  321.4 26.0 %copy-start.58 = (bf16[512,1024]{1,0:T(8,128)(2,1)S(1)}, bf16[512,1024]{1,0:T(8,128)(2,1)}, u32[]{:S(2)}) copy-start(bf16[512,1024]{1,0:T(8,128)(2,1)} %subtract_convert_fusion) | copy-start | bytes 3145732
  321.4 27.5 %collective-permute-start.7 = (bf16[512,1024]{1,0:T(8,128)(2,1)}, bf16[512,1024]{1,0:T(8,128)(2,1)S(1)}, u32[]{:S(2)}, u32[]{:S(2)}) collective-permute-start(bf16[512,1024]{1,0:T(8,128)(2,1)} %subtract_convert_fusion), channel_id=1, source_target_pairs={{0,1},{1,0},{2,3},{3,2},{4,5},{5,4},{6,7},{7,6},{8,9},{9,8},{10,11... | collective-permute-start | bytes 3145736 | tf_op jit(solution)/shard_map/ppermute | solution.py:585
  347.5 1.6 copy-start.62
  348.9 1.6 copy-start.8
  349.0 2.3 copy-start.10
  350.6 51.7 %collective-permute-start.8 = (bf16[1024,1024]{1,0:T(8,128)(2,1)}, bf16[1024,1024]{1,0:T(8,128)(2,1)}, u32[]{:S(2)}, u32[]{:S(2)}) collective-permute-start(bf16[1024,1024]{1,0:T(8,128)(2,1)} %bitcast_convert_fusion), channel_id=1, source_target_pairs={{0,1},{1,0},{2,3},{3,2},{4,5},{5,4},{6,7},{7,6},{8,9},{9,8},{10,11... | collective-permute-start | bytes 6291464 | tf_op jit(solution)/shard_map/ppermute | solution.py:585
  363.3 1.6 copy-start.5
  363.3 1.6 copy-start.36
  363.3 1.6 copy-start.38
  363.3 1.6 copy-start.51
  363.4 2.3 copy-start.6
  369.2 9.3 %copy-start.27 = (bf16[512,1024]{1,0:T(8,128)(2,1)S(1)}, bf16[512,1024]{1,0:T(8,128)(2,1)}, u32[]{:S(2)}) copy-start(bf16[512,1024]{1,0:T(8,128)(2,1)} %copy-done.25) | copy-start | bytes 3145732
  369.2 9.3 %copy-start.33 = (bf16[256,1024]{1,0:T(8,128)(2,1)S(1)}, bf16[256,1024]{1,0:T(8,128)(2,1)}, u32[]{:S(2)}) copy-start(bf16[256,1024]{1,0:T(8,128)(2,1)} %copy-done.32) | copy-start | bytes 1572868
  369.2 9.3 %copy-start.44 = (bf16[4,1024,64]{2,1,0:T(8,128)(2,1)S(1)}, bf16[4,1024,64]{2,1,0:T(8,128)(2,1)}, u32[]{:S(2)}) copy-start(bf16[4,1024,64]{2,1,0:T(8,128)(2,1)} %copy-done.42) | copy-start | bytes 1572868
  375.9 31.6 %collective-permute-start.9 = (bf16[256,1024]{1,0:T(8,128)(2,1)}, bf16[256,1024]{1,0:T(8,128)(2,1)}, u32[]{:S(2)}, u32[]{:S(2)}) collective-permute-start(bf16[256,1024]{1,0:T(8,128)(2,1)} %get-tuple-element.128), channel_id=1, source_target_pairs={{2,0},{6,4},{10,8},{14,12},{18,16},{22,20},{26,24},{30,28},{3,1},{... | collective-permute-start | bytes 1572872 | tf_op jit(solution)/shard_map/ppermute | solution.py:780
  377.2 30.3 %collective-permute-start.10 = (bf16[256,1024]{1,0:T(8,128)(2,1)}, bf16[256,1024]{1,0:T(8,128)(2,1)}, u32[]{:S(2)}, u32[]{:S(2)}) collective-permute-start(bf16[256,1024]{1,0:T(8,128)(2,1)} %get-tuple-element.129), channel_id=1, source_target_pairs={{2,0},{6,4},{10,8},{14,12},{18,16},{22,20},{26,24},{30,28},{3,1},{... | collective-permute-start | bytes 1572872 | tf_op jit(solution)/shard_map/ppermute | solution.py:781
  378.5 23.8 %copy-start.53 = (f32[1024,1024]{1,0:T(8,128)S(1)}, f32[1024,1024]{1,0:T(8,128)}, u32[]{:S(2)}) copy-start(f32[1024,1024]{1,0:T(8,128)} %get-tuple-element.99) | copy-start | bytes 12582916
  402.3 5.2 copy-start.48
  402.3 5.3 copy-start.18
  402.3 5.3 copy-start.20
  402.3 5.3 copy-start.22
  402.3 5.3 copy-start.24
  422.6 2.7 copy-start.59
  422.6 44.6 %collective-permute-start.12 = (bf16[1024,1024]{1,0:T(8,128)(2,1)}, bf16[1024,1024]{1,0:T(8,128)(2,1)}, u32[]{:S(2)}, u32[]{:S(2)}) collective-permute-start(bf16[1024,1024]{1,0:T(8,128)(2,1)} %get-tuple-element.134), channel_id=1, source_target_pairs={{0,1},{1,0},{2,3},{3,2},{4,5},{5,4},{6,7},{7,6},{8,9},{9,8},{10,11... | collective-permute-start | bytes 6291464 | tf_op jit(solution)/shard_map/ppermute | solution.py:585
  424.6 30.9 %collective-permute-start.11 = (bf16[34,1024]{1,0:T(8,128)(2,1)S(1)}, bf16[34,1024]{1,0:T(8,128)(2,1)S(1)}, u32[]{:S(2)}, u32[]{:S(2)}) collective-permute-start(bf16[34,1024]{1,0:T(8,128)(2,1)S(1)} %pad_maximum_fusion.2), channel_id=1, source_target_pairs={{0,1},{1,0},{2,3},{3,2},{4,5},{5,4},{6,7},{7,6},{8,9},{9,8},{10,11... | collective-permute-start | bytes 208904 | tf_op jit(solution)/shard_map/ppermute | solution.py:585
  473.2 20.6 %collective-permute-start.13 = (bf16[800,1024]{1,0:T(8,128)(2,1)S(1)}, bf16[800,1024]{1,0:T(8,128)(2,1)S(1)}, u32[]{:S(2)}, u32[]{:S(2)}) collective-permute-start(bf16[800,1024]{1,0:T(8,128)(2,1)S(1)} %broadcast_select_fusion.2), channel_id=1, source_target_pairs={{0,2},{2,0},{4,6},{6,4},{8,10},{10,8},{12,14},{14,12},{16,18},{18,... | collective-permute-start | bytes 4915208 | tf_op jit(solution)/shard_map/ppermute | solution.py:639
  496.1 92.3 %copy-start.54 = (bf16[1,3,256,1024]{3,2,1,0:T(8,128)(2,1)S(1)}, bf16[1,3,256,1024]{3,2,1,0:T(8,128)(2,1)}, u32[]{:S(2)}) copy-start(bf16[1,3,256,1024]{3,2,1,0:T(8,128)(2,1)} %reduce-scatter.5.cloned.1.call-done) | copy-start | bytes 4718596
  588.3 5.9 collective-permute-start.14
  590.2 2.6 copy-start.55
  592.8 2.2 copy-start.60
  (20 other events, 21.6 us)
Sparse Core Ops, SparseCore 0:
  175.7 128.2 reduce-scatter.4
  319.2 129.2 reduce-scatter.2
  496.2 92.0 all-reduce.1

commit v2 on v1

--- a/solution.py
+++ b/solution.py
@@ -17,7 +17,8 @@
 residual_scale = 0.22
 rope_base = 10000.0
 masked_value = -1e30
-vmem_bytes = 48 * 1024 * 1024
+vmem_bytes = 24 * 1024 * 1024
+expert_vmem_bytes = 40 * 1024 * 1024
 f32 = jnp.float32
 bf16 = jnp.bfloat16
 
@@ -105,11 +106,12 @@
             log_ref[0, h : h + 1, cut] = logs[:, side]
 
 
-def attend(first, lo, q_t, k, v_t, old_k, old_v_t, group):
-    pair_heads, rows, _ = k.shape
+def attend(first, lo, q_t, k, v_t, old_k, old_v_t, group, base, pair_heads):
+    rows = k.shape[1]
     before = old_k.shape[1]
     tall = group * HEAD_DIM
-    by_head = lambda h, s: (h, 0, 0)
+    by_head = lambda h, s: (base + h, 0, 0)
+    flat = lambda h, s: (base + h, 0)
     return pl.pallas_call(
         functools.partial(attend_kernel, group),
         grid_spec=pltpu.PrefetchScalarGridSpec(
@@ -117,15 +119,15 @@
             grid=(pair_heads,),
             in_specs=[
                 pl.BlockSpec((1, rows), lambda h, s: (0, 0)),
-                pl.BlockSpec((tall, rows), lambda h, s: (h, 0)),
+                pl.BlockSpec((tall, rows), flat),
                 pl.BlockSpec((1, rows, HEAD_DIM), by_head),
-                pl.BlockSpec((HEAD_DIM, rows), lambda h, s: (h, 0)),
+                pl.BlockSpec((HEAD_DIM, rows), flat),
                 pl.BlockSpec((1, before, HEAD_DIM), by_head),
-                pl.BlockSpec((HEAD_DIM, before), lambda h, s: (h, 0)),
+                pl.BlockSpec((HEAD_DIM, before), flat),
             ],
             out_specs=[
                 pl.BlockSpec((tall, rows), lambda h, s: (h, 0)),
-                pl.BlockSpec((1, group, rows), by_head),
+                pl.BlockSpec((1, group, rows), lambda h, s: (h, 0, 0)),
             ],
         ),
         out_shape=[
@@ -143,13 +145,16 @@
 
 
 def attend_back_kernel(
-    group, earlier, before,
+    group,
     first_ref, lo_ref, log_ref, spread_ref, qt_ref, dt_ref, q_ref, d_ref, k_ref, kt_ref, v_ref,
-    sum_ref, dq_ref, dk_ref, dv_ref, pair_ref,
+    old_k_ref, old_kt_ref, old_v_ref,
+    dq_ref, dk_ref, dv_ref, old_dk_ref, old_dv_ref, pair_ref, old_pair_ref,
 ):
     lanes = group * BLOCK
+    before = old_k_ref.shape[1]
     passed = before // BLOCK
     pair_ref[...] = jnp.zeros_like(pair_ref)
+    old_pair_ref[...] = jnp.zeros_like(old_pair_ref)
     for block in range(qt_ref.shape[1] // BLOCK):
         cut = pl.ds(block * BLOCK, BLOCK)
         lo, hi = window_of(lo_ref, block, before, group)
@@ -168,43 +173,48 @@
         logs = jnp.concatenate([log_ref[0, h : h + 1, cut] for h in range(group)], axis=1)
         spread = jnp.concatenate([spread_ref[0, h : h + 1, cut] for h in range(group)], axis=1)
 
-        def step(number, acc):
+        def step(keys_ref, keys_t_ref, values_ref, sums_ref, offset, number, acc):
             start = pl.multiple_of(number * BLOCK, BLOCK)
             here = pl.ds(start, BLOCK)
-            scores = mm(k_ref[0, here, :], query)
-            mask = block_mask(lo, hi, start + (0 if earlier else before), lanes)
+            scores = mm(keys_ref[0, here, :], query)
+            mask = block_mask(lo, hi, start + offset, lanes)
             probs = jnp.exp(jnp.where(mask, scores - logs, masked_value))
-            change = mm(v_ref[0, here, :], upstream)
+            change = mm(values_ref[0, here, :], upstream)
             scores_change = (probs * (change - spread)).astype(bf16)
-            pair_ref[here, :] += mm(
+            sums_ref[here, :] += mm(
                 jnp.concatenate([scores_change, probs.astype(bf16)], axis=1), both_rows
             )
-            return acc + mm(kt_ref[:, here], scores_change)
+            return acc + mm(keys_t_ref[:, here], scores_change)
 
         first = first_ref[block]
-        bounds = (first, passed) if earlier else (jnp.maximum(first - passed, 0), block + 1)
-        acc = lax.fori_loop(*bounds, step, jnp.zeros((HEAD_DIM, lanes), f32))
+        acc = jnp.zeros((HEAD_DIM, lanes), f32)
+        earlier = functools.partial(step, old_k_ref, old_kt_ref, old_v_ref, old_pair_ref, 0)
+        acc = lax.fori_loop(first, passed, earlier, acc)
+        own = functools.partial(step, k_ref, kt_ref, v_ref, pair_ref, before)
+        acc = lax.fori_loop(jnp.maximum(first - passed, 0), block + 1, own, acc)
         for h in range(group):
-            side = slice(h * HEAD_DIM, (h + 1) * HEAD_DIM)
-            dq_ref[side, cut] = sum_ref[side, cut] + (
+            dq_ref[h * HEAD_DIM : (h + 1) * HEAD_DIM, cut] = (
                 acc[:, h * BLOCK : (h + 1) * BLOCK] * score_scale
             )
     pair_t = pair_ref[...].T
-    dk_ref[...] = pair_t[:HEAD_DIM].astype(dk_ref.dtype)
-    dv_ref[...] = pair_t[HEAD_DIM:].astype(dv_ref.dtype)
+    dk_ref[...] = pair_t[:HEAD_DIM]
+    dv_ref[...] = pair_t[HEAD_DIM:]
+    pair_t = old_pair_ref[...].T
+    old_dk_ref[...] = pair_t[:HEAD_DIM].astype(bf16)
+    old_dv_ref[...] = pair_t[HEAD_DIM:].astype(bf16)
 
 
 def attend_back(
-    first, lo, logs, spread, q_t, d_t, q_rows, d_rows, k, k_t, v, dq_sum, before, earlier
+    first, lo, logs, spread, q_t, d_t, q_rows, d_rows, k, k_t, v, old_k, old_k_t, old_v
 ):
-    pair_heads, keys, _ = k.shape
+    pair_heads, before, _ = old_k.shape
     group, rows = q_rows.shape[1:3]
     tall = group * HEAD_DIM
     by_head = lambda h, s: (h, 0, 0)
     flat = lambda h, s: (h, 0)
-    pair_type = bf16 if earlier else f32
+    split = pair_heads * HEAD_DIM
     return pl.pallas_call(
-        functools.partial(attend_back_kernel, group, earlier, before),
+        functools.partial(attend_back_kernel, group),
         grid_spec=pltpu.PrefetchScalarGridSpec(
             num_scalar_prefetch=1,
             grid=(pair_heads,),
@@ -216,31 +226,40 @@
                 pl.BlockSpec((tall, rows), flat),
                 pl.BlockSpec((1, group, rows, HEAD_DIM), lambda h, s: (h, 0, 0, 0)),
                 pl.BlockSpec((1, group, rows, HEAD_DIM), lambda h, s: (h, 0, 0, 0)),
-                pl.BlockSpec((1, keys, HEAD_DIM), by_head),
-                pl.BlockSpec((HEAD_DIM, keys), flat),
-                pl.BlockSpec((1, keys, HEAD_DIM), by_head),
-                pl.BlockSpec((tall, rows), flat),
+                pl.BlockSpec((1, rows, HEAD_DIM), by_head),
+                pl.BlockSpec((HEAD_DIM, rows), flat),
+                pl.BlockSpec((1, rows, HEAD_DIM), by_head),
+                pl.BlockSpec((1, before, HEAD_DIM), by_head),
+                pl.BlockSpec((HEAD_DIM, before), flat),
+                pl.BlockSpec((1, before, HEAD_DIM), by_head),
             ],
             out_specs=[
                 pl.BlockSpec((tall, rows), flat),
-                pl.BlockSpec((HEAD_DIM, keys), flat),
-                pl.BlockSpec((HEAD_DIM, keys), flat),
+                pl.BlockSpec((HEAD_DIM, rows), flat),
+                pl.BlockSpec((HEAD_DIM, rows), flat),
+                pl.BlockSpec((HEAD_DIM, before), flat),
+                pl.BlockSpec((HEAD_DIM, before), flat),
             ],
-            scratch_shapes=[pltpu.VMEM((keys, 2 * HEAD_DIM), f32)],
+            scratch_shapes=[
+                pltpu.VMEM((rows, 2 * HEAD_DIM), f32),
+                pltpu.VMEM((before, 2 * HEAD_DIM), f32),
+            ],
         ),
         out_shape=[
             jax.ShapeDtypeStruct((pair_heads * tall, rows), f32),
-            jax.ShapeDtypeStruct((pair_heads * HEAD_DIM, keys), pair_type),
-            jax.ShapeDtypeStruct((pair_heads * HEAD_DIM, keys), pair_type),
+            jax.ShapeDtypeStruct((split, rows), f32),
+            jax.ShapeDtypeStruct((split, rows), f32),
+            jax.ShapeDtypeStruct((split, before), bf16),
+            jax.ShapeDtypeStruct((split, before), bf16),
         ],
         compiler_params=pltpu.CompilerParams(vmem_limit_bytes=vmem_bytes),
         cost_estimate=pl.CostEstimate(
-            flops=pair_heads * group * rows * keys * 1280,
-            bytes_accessed=10 * 1024 * 1024,
-            transcendentals=pair_heads * group * rows * keys,
+            flops=pair_heads * group * rows * (rows + before) * 1280,
+            bytes_accessed=16 * 1024 * 1024,
+            transcendentals=pair_heads * group * rows * (rows + before),
         ),
         name="attend_back",
-    )(first, lo, logs, spread, q_t, d_t, q_rows, d_rows, k, k_t, v, dq_sum)
+    )(first, lo, logs, spread, q_t, d_t, q_rows, d_rows, k, k_t, v, old_k, old_k_t, old_v)
 
 
 def turn(tall, cosine, sine):
@@ -316,9 +335,14 @@
 
 def enter_mixture_kernel(count, x_ref, gain_ref, router_ref, routes_ref, *refs):
     pieces, (hidden_ref, normed_ref, normed_t_ref, gates_ref) = refs[: 2 * count], refs[2 * count :]
-    projected = 0.0
-    for context_ref, w_ref in zip(pieces[:count], pieces[count:]):
-        projected = projected + mm(context_ref[...].astype(f32).T.astype(bf16), w_ref[...])
+    products = [
+        mm(context_ref[...].astype(f32).T.astype(bf16), w_ref[...])
+        for context_ref, w_ref in zip(pieces[:count], pieces[count:])
+    ]
+    sides = max(1, count // 2)
+    projected = functools.reduce(jnp.add, products[:sides])
+    if count > sides:
+        projected = projected + functools.reduce(jnp.add, products[sides:])
     hidden = x_ref[...].astype(f32) + residual_scale * projected
     hidden_ref[...] = hidden
     normed = hidden * scale_of(hidden) * gain_ref[...].astype(f32)
@@ -364,7 +388,9 @@
     )(tokens, gain, router_t, routes_t, *contexts, *weights)
 
 
-def enter_back_kernel(c_ref, own_ref, other_ref, wo_ref, ctx_ref, hidden_ref, dt_ref, d_ref, spread_ref, wo_grad_ref):
+def enter_back_kernel(
+    c_ref, own_ref, other_ref, wo_ref, ctx_ref, hidden_ref, dt_ref, d_ref, spread_ref, wo_grad_ref
+):
     hidden_gradient = c_ref[...].astype(f32) + (
         own_ref[...].astype(f32) + other_ref[...].astype(f32)
     )
@@ -419,9 +445,9 @@
 
 
 def leave_back_kernel(
-    x_ref, gain_ref, cos_ref, sin_ref, wq_ref, wk_ref, wv_ref, normed_ref,
-    dq_ref, dk_ref, dv_ref, more_dk_ref, more_dv_ref,
-    part_ref, gain_grad_ref, w_grad_ref, w_sum_ref,
+    core_ref, x_ref, gain_ref, cos_ref, sin_ref, wq_ref, wk_ref, wv_ref, normed_ref,
+    dq_ref, dk_ref, dv_ref, more_dk_ref, more_dv_ref, wo_grad_ref, router_grad_ref, gain_two_grad_ref,
+    part_ref, send_ref, keep_ref, sum_ref, gain_grad_ref,
 ):
     step = pl.program_id(0)
     cosine, sine = cos_ref[...], -sin_ref[...]
@@ -432,10 +458,11 @@
 
     @pl.when(step == 0)
     def start():
-        w_sum_ref[...] = jnp.zeros_like(w_sum_ref)
+        sum_ref[...] = jnp.zeros_like(sum_ref)
         gain_grad_ref[...] = jnp.zeros_like(gain_grad_ref)
 
-    w_sum_ref[...] += mm(jnp.concatenate([dq_t, dk_t, dv_t], axis=0), normed)
+    stacked = jnp.concatenate([dq_t, dk_t, dv_t], axis=0)
+    sum_ref[: stacked.shape[0]] += mm(stacked, normed)
     rows_of = lambda tall: tall.astype(f32).T.astype(bf16)
     upstream = (
         dot(rows_of(dq_t), wq_ref[...], 1, 1)
@@ -449,44 +476,58 @@
 
     @pl.when(step == pl.num_programs(0) - 1)
     def finish():
-        w_grad_ref[...] = w_sum_ref[...].astype(bf16)
+        place = stacked.shape[0]
+        sum_ref[place : place + wo_grad_ref.shape[0]] = wo_grad_ref[...]
+        place += wo_grad_ref.shape[0]
+        sum_ref[place : place + EXPERTS] = router_grad_ref[...]
+        place += EXPERTS
+        sum_ref[place : place + 1] = gain_two_grad_ref[...]
+        sum_ref[place + 1 : place + 2] = gain_grad_ref[...]
+        high = keep_ref.shape[0]
+        send_from = pl.multiple_of((1 - core_ref[0]) * high, 16)
+        keep_from = pl.multiple_of(core_ref[0] * high, 16)
+        send_ref[...] = sum_ref[pl.ds(send_from, high)].astype(bf16)
+        keep_ref[...] = sum_ref[pl.ds(keep_from, high)].astype(bf16)
 
 
 def leave_back(
-    tokens, gain, cosine, sine, w_query, w_key, w_value, normed, dq_t, dk_t, dv_t, more_dk, more_dv
+    core, high, tokens, gain, cosine, sine, w_query, w_key, w_value, normed, dq_t, dk_t, dv_t,
+    more_dk, more_dv, w_out_gradient, router_gradient, second_gain_gradient,
 ):
     rows, width = tokens.shape
     tall, split = w_query.shape[1], w_key.shape[0]
-    whole = lambda shape: pl.BlockSpec(shape, lambda t: (0,) * len(shape))
-    down = lambda wide: pl.BlockSpec((BLOCK, wide), lambda t: (t, 0))
-    across = lambda high: pl.BlockSpec((high, BLOCK), lambda t: (0, t))
+    whole = lambda shape: pl.BlockSpec(shape, lambda t, s: (0,) * len(shape))
+    down = lambda wide: pl.BlockSpec((BLOCK, wide), lambda t, s: (t, 0))
+    across = lambda high: pl.BlockSpec((high, BLOCK), lambda t, s: (0, t))
     return pl.pallas_call(
         leave_back_kernel,
-        grid=(rows // BLOCK,),
-        in_specs=[
-            down(width), whole((1, width)), across(HEAD_DIM // 2), across(HEAD_DIM // 2),
-            whole((width, tall)), whole((split, width)), whole((split, width)), down(width),
-            across(tall), across(split), across(split), across(split), across(split),
-        ],
-        out_specs=[
-            down(width), whole((1, width)), whole((tall + 2 * split, width)),
-        ],
+        grid_spec=pltpu.PrefetchScalarGridSpec(
+            num_scalar_prefetch=1,
+            grid=(rows // BLOCK,),
+            in_specs=[
+                down(width), whole((1, width)), across(HEAD_DIM // 2), across(HEAD_DIM // 2),
+                whole((width, tall)), whole((split, width)), whole((split, width)), down(width),
+                across(tall), across(split), across(split), across(split), across(split),
+                whole((tall, width)), whole((EXPERTS, width)), whole((1, width)),
+            ],
+            out_specs=[down(width), whole((high, width)), whole((high, width))],
+            scratch_shapes=[pltpu.VMEM((2 * high, width), f32), pltpu.VMEM((1, width), f32)],
+        ),
         out_shape=[
             jax.ShapeDtypeStruct((rows, width), bf16),
-            jax.ShapeDtypeStruct((1, width), f32),
-            jax.ShapeDtypeStruct((tall + 2 * split, width), bf16),
-        ],
-        scratch_shapes=[pltpu.VMEM((tall + 2 * split, width), f32)],
-        compiler_params=pltpu.CompilerParams(vmem_limit_bytes=vmem_bytes),
+            jax.ShapeDtypeStruct((high, width), bf16),
+            jax.ShapeDtypeStruct((high, width), bf16),
+        ],
+        compiler_params=pltpu.CompilerParams(vmem_limit_bytes=expert_vmem_bytes),
         cost_estimate=pl.CostEstimate(
             flops=4 * rows * width * (tall + 2 * split),
-            bytes_accessed=20 * 1024 * 1024,
+            bytes_accessed=24 * 1024 * 1024,
             transcendentals=0,
         ),
         name="leave_back",
     )(
-        tokens, gain, cosine, sine, w_query, w_key, w_value, normed, dq_t, dk_t, dv_t, more_dk,
-        more_dv,
+        core, tokens, gain, cosine, sine, w_query, w_key, w_value, normed, dq_t, dk_t, dv_t,
+        more_dk, more_dv, w_out_gradient, router_gradient, second_gain_gradient,
     )
 
 
@@ -508,7 +549,7 @@
         silu = gate * share
         active = silu * up
         weight = gates_ref[0, :, cut] * residual_scale
-        gate_grad_ref[0, :, cut] = residual_scale * jnp.sum(
+        gate_grad_ref[0, 0, :, cut] = residual_scale * jnp.sum(
             active * active_grad, axis=0, keepdims=True
         )
         active_grad = active_grad * weight
@@ -529,10 +570,10 @@
     put(2, mm(act_ref[0], c_ref[...]))
 
 
-def expert_step(ids, gates, xt, x, ct, c, w_up, w_down, more, old):
+def expert_step(ids, half, gates, xt, x, ct, c, w_up, w_down, more, old):
     count = ids.shape[0]
     rows, width = x.shape
-    units = w_down.shape[1]
+    units = w_down.shape[1] // 2
     whole = lambda shape: pl.BlockSpec(shape, lambda e, s: (0,) * len(shape))
     fresh = old is None
     adds = more is not None
@@ -550,8 +591,8 @@
                 whole((rows, width)),
                 whole((width, rows)),
                 whole((rows, width)),
-                pl.BlockSpec((1, 2, units, width), lambda e, s: (s[e], 0, 0, 0)),
-                pl.BlockSpec((1, units, width), lambda e, s: (s[e], 0, 0)),
+                pl.BlockSpec((1, 2, units, width), lambda e, s: (s[e], 0, half, 0)),
+                pl.BlockSpec((1, units, width), lambda e, s: (s[e], half, 0)),
                 *([each] if adds else []),
                 pl.BlockSpec(memory_space=pl.ANY),
                 pl.BlockSpec(memory_space=pl.ANY),
@@ -559,19 +600,19 @@
             ],
             out_specs=[
                 each,
-                pl.BlockSpec((1, 2, units, rows), lambda e, s: (s[e], 0, 0, 0)),
-                pl.BlockSpec((1, units, rows), lambda e, s: (s[e], 0, 0)),
-                pl.BlockSpec((1, 1, rows), lambda e, s: (s[e], 0, 0)),
+                pl.BlockSpec((1, 2, units, rows), lambda e, s: (s[e], 0, half, 0)),
+                pl.BlockSpec((1, units, rows), lambda e, s: (s[e], half, 0)),
+                pl.BlockSpec((1, 1, 1, rows), lambda e, s: (half, s[e], 0, 0)),
             ],
         ),
         out_shape=[
             jax.ShapeDtypeStruct((count, 3, units, width), bf16),
-            jax.ShapeDtypeStruct((EXPERTS, 2, units, rows), bf16),
-            jax.ShapeDtypeStruct((EXPERTS, units, rows), bf16),
-            jax.ShapeDtypeStruct((EXPERTS, 1, rows), f32),
+            jax.ShapeDtypeStruct((EXPERTS, 2, 2 * units, rows), bf16),
+            jax.ShapeDtypeStruct((EXPERTS, 2 * units, rows), bf16),
+            jax.ShapeDtypeStruct((2, EXPERTS, 1, rows), f32),
         ],
         input_output_aliases={} if fresh else {8 + adds: 1, 9 + adds: 2, 10 + adds: 3},
-        compiler_params=pltpu.CompilerParams(vmem_limit_bytes=vmem_bytes),
+        compiler_params=pltpu.CompilerParams(vmem_limit_bytes=expert_vmem_bytes),
         cost_estimate=pl.CostEstimate(
             flops=count * 12 * rows * width * units,
             bytes_accessed=count * units * width * 12 + 8 * rows * width,
@@ -632,17 +673,19 @@
     )
 
 
-def summed_over_tokens(part):
+def summed_over_tokens(send, keep, beside_one, beside_two):
     swap = [(i, i ^ 1) for i in range(lax.axis_size("dp"))]
+    received = lax.ppermute(send, "dp", swap)
+    half = (keep.astype(f32) + received.astype(f32)).astype(bf16)
+    rings = chip_rings()
+    half = lax.psum_scatter(half, "dp", scatter_dimension=0, axis_index_groups=rings, tiled=True)
+    half, beside_one = lax.optimization_barrier((half, beside_one))
+    half = lax.all_gather(half, "dp", axis=0, axis_index_groups=rings, tiled=True)
+    half, beside_two = lax.optimization_barrier((half, beside_two))
+    other = lax.ppermute(half, "dp", swap)
     is_first = lax.axis_index("dp") % 2 == 0
-    low, high = jnp.split(part, 2, axis=0)
-    received = lax.ppermute(jnp.where(is_first, high, low), "dp", swap)
-    half = (jnp.where(is_first, low, high).astype(f32) + received.astype(f32)).astype(bf16)
-    half = lax.psum(half, "dp", axis_index_groups=chip_rings())
-    other = lax.ppermute(half, "dp", swap)
-    return jnp.concatenate(
-        [jnp.where(is_first, half, other), jnp.where(is_first, other, half)], axis=0
-    )
+    low, high = jnp.where(is_first, half, other), jnp.where(is_first, other, half)
+    return jnp.concatenate([low, high], axis=0), beside_one, beside_two
 
 
 def angles(position):
@@ -698,34 +741,48 @@
     across = lambda tall: jnp.swapaxes(tall.reshape(pair_heads, HEAD_DIM, before), 1, 2)
     old_k_rows, old_v_rows = across(old_k_t), across(old_v_t)
 
-    context_t, logs = attend(first_block, lo, q_t, k_rows, v_t, old_k_rows, old_v_t, group)
+    calls = 2 if pair_heads % 2 == 0 else 1
+    here = pair_heads // calls
+    pieces = [
+        attend(
+            first_block, lo, q_t, k_rows, v_t, old_k_rows, old_v_t, group, call * here, here
+        )
+        for call in range(calls)
+    ]
+    context_parts = [gathered(piece[0]) for piece in pieces]
+    contexts = [parts[side] for side in range(len(context_parts[0])) for parts in context_parts]
+    context_t = jnp.concatenate([piece[0] for piece in pieces], axis=0)
+    logs = jnp.concatenate([piece[1] for piece in pieces], axis=0)
+    w_out_pieces = [
+        piece for part in w_out_parts for piece in jnp.split(part, calls, axis=0)
+    ]
     hidden, normed_mixture, normed_t, gates = enter_mixture(
-        tokens, mixture_gain[None, :], w_router.T, routes.T, gathered(context_t), w_out_parts
+        tokens, mixture_gain[None, :], w_router.T, routes.T, contexts, w_out_pieces
     )
     gain_two = mixture_gain.astype(f32)
     scale_two = scale_of(hidden)
 
     upstream_t = out_cotangent.T
     swap_cores = [(i, i ^ 1) for i in range(peers)]
-    shares, old = [], None
-
-    def run_experts(ids):
+    shares, arrived, old = [], [], None
+    pieces = [(number, half) for number in range(chunks) for half in range(2)]
+
+    def run_experts(piece, side, more):
+        ids = chunk_experts(device, peers, piece[0])[side]
         return expert_step(
-            ids, gates[:, None, :], normed_t, normed_mixture, upstream_t, out_cotangent,
-            expert_gate_up, expert_down, None, old,
+            ids, piece[1], gates[:, None, :], normed_t, normed_mixture, upstream_t, out_cotangent,
+            expert_gate_up, expert_down, more, old,
         )
 
-    for number in range(chunks):
-        other_ids, own_ids = chunk_experts(device, peers, number)
-        send, *old = run_experts(other_ids)
-        received = lax.ppermute(send, "dp", swap_cores)
-        keep, *old = run_experts(own_ids)
-        if number < chunks - 1:
-            chip_sum = (keep.astype(f32) + received.astype(f32)).astype(bf16)
-            chip_sum, *old = lax.optimization_barrier((chip_sum, *old))
+    for number in range(len(pieces) + 1):
+        if number < len(pieces):
+            send, *old = run_experts(pieces[number], 0, None)
+            arrived.append(lax.ppermute(send, "dp", swap_cores))
+        if number > 0:
+            chip_sum, *old = run_experts(pieces[number - 1], 1, arrived[number - 1])
             shares.append(to_owner(chip_sum))
     up_grad, act, gates_gradient = old
-    gates_gradient = gates_gradient[:, 0]
+    gates_gradient = gates_gradient[0, :, 0] + gates_gradient[1, :, 0]
     units = expert_down.shape[1]
     wide = EXPERTS * units
 
@@ -745,16 +802,12 @@
         part, gain_part = norm_back(hidden[cut], scale_two[cut], gain_two, normed_gradient)
         part = part.astype(bf16)
         if start > 0:
-            part, act, keep, received, other_parts[0] = lax.optimization_barrier(
-                (part, act, keep, received, other_parts[0])
-            )
+            part, act, other_parts[0] = lax.optimization_barrier((part, act, other_parts[0]))
         own, other = both_parts(part)
         own_parts.append(own)
         other_parts.append(other)
         gain_parts.append(gain_part)
     second_gain_part = gain_parts[0] + gain_parts[1]
-    chip_sum = (keep.astype(f32) + received.astype(f32)).astype(bf16)
-    shares.append(to_owner(chip_sum))
 
     mixture_part = dot(act.reshape(wide, rows), expert_down.reshape(wide, width), 0, 0)
     mixture_low = mixture_part.astype(bf16)
@@ -763,45 +816,50 @@
     own_part, other_part, mixture_low = lax.optimization_barrier(
         (own_part, other_part, mixture_low)
     )
-    mixed = (hidden + summed_parts(mixture_low)).astype(bf16)
+    mixture_own, mixture_other = both_parts(mixture_low)
 
     hidden_gradient, d_t, d_rows, spread, w_out_gradient = enter_back(
         out_cotangent, own_part, other_part, w_out, context_t
     )
     by_group = lambda rows_of_heads: rows_of_heads.reshape(pair_heads, group, rows, HEAD_DIM)
-    back = functools.partial(
-        attend_back, first_block, lo, logs, spread.reshape(pair_heads, group, rows), q_t, d_t,
-        by_group(q_rows), by_group(d_rows),
-    )
-    dq_t, old_dk, old_dv = back(
-        old_k_rows, old_k_t, old_v_rows, jnp.zeros((q_t.shape[0], rows), f32), before, True
+    dq_t, dk_t, dv_t, old_dk, old_dv = attend_back(
+        first_block, lo, logs, spread.reshape(pair_heads, group, rows), q_t, d_t, by_group(q_rows),
+        by_group(d_rows), k_rows, k_t, v_rows, old_k_rows, old_k_t, old_v_rows,
     )
     to_previous = [(i + 1, i) for i in range(0, peers, 2)]
     more_dk = lax.ppermute(old_dk, "dp", to_previous)
     more_dv = lax.ppermute(old_dv, "dp", to_previous)
-    dq_t, dk_t, dv_t = back(k_rows, k_t, v_rows, dq_t, before, False)
-    dq_t, mixed = lax.optimization_barrier((dq_t, mixed))
-    if chunks > 1:
-        dq_t, shares[0] = lax.optimization_barrier((dq_t, shares[0]))
-    input_part, first_gain_part, w_gradients = leave_back(
-        tokens, gain_one, cosine, sine, w_query, w_key, w_value, normed_attention, dq_t, dk_t, dv_t,
-        more_dk, more_dv,
-    )
-    tokens_gradient = (hidden_gradient + summed_parts(input_part)).astype(bf16)
-    small = jnp.concatenate([router_gradient, second_gain_part[None, :], first_gain_part], axis=0)
-    small = summed_parts(small).astype(bf16)
+    dq_t, mixture_other, *shares[:-2] = lax.optimization_barrier(
+        (dq_t, mixture_other, *shares[:-2])
+    )
     tall, split = w_query.shape[1], w_key.shape[0]
     ends = [tall, tall + split, tall + 2 * split, 2 * tall + 2 * split, 2 * tall + 2 * split + EXPERTS]
-    filler = jnp.zeros((-(ends[-1] + 2) % 64, width), bf16)
-    gradients = jnp.concatenate([w_gradients, w_out_gradient.astype(bf16), small, filler], axis=0)
-    shares[-1], gradients, tokens_gradient = lax.optimization_barrier(
-        (shares[-1], gradients, tokens_gradient)
-    )
-    gradients = summed_over_tokens(gradients).astype(f32)
-    w_q, w_k, w_v, w_o, router, gains = jnp.split(gradients, ends, axis=0)
-    experts_gradient = jnp.concatenate(shares, axis=0).astype(f32)
+    high = -(-(ends[-1] + 2) // (16 * peers)) * 8 * peers
+    input_part, send, keep = leave_back(
+        (device % 2)[None].astype(jnp.int32), high, tokens, gain_one, cosine, sine, w_query, w_key,
+        w_value, normed_attention, dq_t, dk_t, dv_t, more_dk, more_dv, w_out_gradient,
+        router_gradient, second_gain_part[None, :],
+    )
+    swapped = [both_parts(part) for part in jnp.split(input_part, 2, axis=0)]
+    *shares[-2:], keep = lax.optimization_barrier((*shares[-2:], keep))
+    swapped = [list(pair) for pair in swapped]
+    gradients, swapped[0][1], swapped[1][1] = summed_over_tokens(
+        send, keep, swapped[0][1], swapped[1][1]
+    )
+    input_sum = jnp.concatenate(
+        [own.astype(f32) + other.astype(f32) for own, other in swapped], axis=0
+    )
+    mixed = (hidden + (mixture_own.astype(f32) + mixture_other.astype(f32))).astype(bf16)
+    tokens_gradient = hidden_gradient + input_sum
+    w_q, w_k, w_v, w_o = jnp.split(gradients[: ends[3]].astype(f32), ends[:3], axis=0)
+    small = summed_parts(gradients[ends[3] :])
+    router, gains = small[:EXPERTS], small[EXPERTS:]
+    halves = [
+        jnp.concatenate(shares[start : start + 2], axis=2) for start in range(0, len(shares), 2)
+    ]
+    experts_gradient = jnp.concatenate(halves, axis=0).astype(f32)
     return (
-        mixed, tokens_gradient, gains[1], w_q.T, w_k, w_v, w_o, gains[0], router.T,
+        mixed, tokens_gradient.astype(bf16), gains[1], w_q.T, w_k, w_v, w_o, gains[0], router.T,
         experts_gradient[:, :2], experts_gradient[:, 2],
     )
 

time: 613 us -> 577 us (0.941)
  waiting for transfers between devices: 135 us -> 99.4 us
  local copies, waits for them, and re-layouts: 55.6 us -> 84.5 us
  other arithmetic: 60.9 us -> 33.1 us
  starting transfers between devices: 45.1 us -> 31.9 us
  Pallas kernels: 221 us -> 229 us
    psum x1 -> x0, waiting for transfers between devices: 92.3 us -> none  [summed_over_tokens(): half = lax.psum(half, 'dp', axis_index_groups=chip_rings())]
    unnamed x134 -> x184, local copies, waits for them, and re-layouts: 35.5 us -> 72.2 us
    convert_element_type x9 -> x5, other arithmetic: 48.7 us -> 14.1 us  [the longest x1 6.04 us: on_device(): (hidden + (mixture_own.astype(f32) + mixture_other.astype(f32))).astype(b...]
    ppermute x7 -> x9, waiting for transfers between devices: 39.6 us -> 60 us  [from_other_half(): return lax.ppermute(shard, 'tensor', [(0, 1), (1, 0)])]
    pallas_call x4 -> x8, Pallas kernels: 141 us -> 160 us  [expert_step(): pl.pallas_call(functools.partial(expert_kernel, adds), grid_spec=pltpu.Pr...]
    ppermute x3 -> x5, starting transfers between devices: 31.9 us -> 12.8 us  [the longest x4 12.1 us: on_device(): arrived.append(lax.ppermute(send, 'dp', swap_cores))]
    ppermute x1, waiting for transfers between devices: 0.01 us -> 17.6 us  [on_device(): more_dk = lax.ppermute(old_dk, 'dp', to_previous)]
    concatenate x1 -> x0, local copies, waits for them, and re-layouts: 11.5 us -> none  [on_device(): jnp.concatenate([w_gradients, w_out_gradient.astype(bf16), small, filler]...]
  transfers between devices with their start and end apart: 18 -> 25, of which waited for: 4 -> 10; matrix products, arithmetic and copies ran while one was open for 23% -> 22% of each run, Pallas kernels for 29% -> 32%
where the time goes in v2:
time: 577 us; the launch traced here: 573 us
  Pallas kernels  229 us (40%)
  waiting for transfers between devices  99.4 us (17%)
  local copies, waits for them, and re-layouts  84.5 us (15%)
  matrix products  80 us (14%)
  other arithmetic  33.1 us (6%)
  starting transfers between devices  31.9 us (6%)
  between operations  15.3 us (3%)
    pallas_call x8, Pallas kernels, expert_step(): pl.pallas_call(functools.partial(expert_kernel, adds), grid_spec=pltpu.Pr...  160 us
    dot_general x5, matrix products, dot(): lax.dot_general(left, right, (((left_dim,), (right_dim,)), ((), ())), pre...  79.5 us
    unnamed x184, local copies, waits for them, and re-layouts  72.2 us
    ppermute x9, waiting for transfers between devices, from_other_half(): return lax.ppermute(shard, 'tensor', [(0, 1), (1, 0)])  60 us
    pallas_call x1, Pallas kernels, attend_back(): pl.pallas_call(functools.partial(attend_back_kernel, group), grid_spec=pl...  20.2 us
    pallas_call x2, Pallas kernels, attend(): pl.pallas_call(functools.partial(attend_kernel, group), grid_spec=pltpu.P...  18 us
    ppermute x1, waiting for transfers between devices, on_device(): more_dk = lax.ppermute(old_dk, 'dp', to_previous)  17.6 us
    ppermute x9, starting transfers between devices, from_other_half(): return lax.ppermute(shard, 'tensor', [(0, 1), (1, 0)])  12.3 us
  transfers between devices with their start and end apart: 25, of which 10 were waited for; matrix products, arithmetic and copies ran while one was open for 22% of the time, Pallas kernels for 32%

profile of v2, /device:TPU:0, one launch (start us, length us, event | category | flops | bytes accessed | tf_op | source)
XLA Modules:
  0.0 572.7 jit_solution(5346466487623343825)
XLA Ops:
  7.2 3.0 collective-permute-start.4
  11.5 1.7 copy-done.35
  16.5 6.2 %project.1 = (bf16[1024,1024]{1,0:T(8,128)(2,1)S(1)}, bf16[512,1024]{1,0:T(8,128)(2,1)S(1)}, bf16[8,1024,64]{2,1,0:T(8,128)(2,1)S(1)}, bf16[256,1024]{1,0:T(8,12...) custom-call(bf16[1024,1024]{1,0:T(8,128)(2,1)S(1)} %copy-done.35, ...), custom_call_target="tpu_custom_call" | custom-call | flops 2147483648 | bytes 12582912 | tf_op jit(solution)/shard_map/project/pallas_call | solution.py:306
  29.8 2.3 collective-permute-start.1
  34.0 2.6 copy.63
  39.0 1.6 copy-done.67
  41.8 9.0 %attend.3 = (bf16[256,1024]{1,0:T(8,128)(2,1)S(1)}, f32[2,2,1024]{2,1,0:T(2,128)S(1)}) custom-call(s32[4]{0:T(128)S(1)} %and_select_fusion.first_ref, s32[1,1024]{1,0:T(1,128)S(1)} %bitcast.65, bf16[512,1024]{1,0:T(8,128)(2,1)S(1)} %copy-done.67, bf16[4,1024,64]{2,1,0:T(8,128)(2,1)S(1)} %copy-done.71, bf16[256,1024]{1,0:T(8,128)(2,1)} %get-tuple-element.92.vt_ref, ...), custom_call_target="tpu_custom_call" | custom-call | flops 4294967296 | bytes 8388608 | tf_op jit(solution)/shard_map/attend/pallas_call | solution.py:115
  51.2 9.0 %attend.2 = (bf16[256,1024]{1,0:T(8,128)(2,1)S(1)}, f32[2,2,1024]{2,1,0:T(2,128)S(1)}) custom-call(s32[4]{0:T(128)S(1)} %and_select_fusion.first_ref, s32[1,1024]{1,0:T(1,128)S(1)} %bitcast.66, bf16[512,1024]{1,0:T(8,128)(2,1)S(1)} %copy-done.68, bf16[4,1024,64]{2,1,0:T(8,128)(2,1)S(1)} %copy-done.71, bf16[256,1024]{1,0:T(8,128)(2,1)} %get-tuple-element.92.vt_ref, ...), custom_call_target="tpu_custom_call" | custom-call | flops 4294967296 | bytes 8388608 | tf_op jit(solution)/shard_map/attend/pallas_call | solution.py:115
  60.2 1.8 collective-permute-start.2
  63.4 7.9 %collective-permute-done.2.refs_2_ = bf16[256,1024]{1,0:T(8,128)(2,1)S(1)} collective-permute-done((bf16[256,1024]{1,0:T(8,128)(2,1)S(1)}, bf16[256,1024]{1,0:T(8,128)(2,1)S(1)}, u32[]{:S(2)}, u32[]{:S(2)}) %collective-permute-start.2) | collective-permute-done | bytes 524320 | tf_op jit(solution)/shard_map/ppermute | solution.py:626
  71.3 5.6 enter_mixture.1
  76.9 2.0 copy-done.11
  79.1 20.2 %experts.8 = (bf16[8,3,128,1024]{3,2,1,0:T(8,128)(2,1)}, bf16[32,2,256,1024]{3,2,1,0:T(8,128)(2,1)}, bf16[32,256,1024]{2,1,0:T(8,128)(2,1)}, f32[2,32,1,1024]{3,2,1,0:T(1,128)S(1)}) custom-call(s32[8]{0:T(128)S(1)} %get-tuple-element.207.ids_ref, f32[32,1,1024]{2,1,0:T(1,128)S(1)} %broadcast_in_dim.20.gates_ref, ...), custom_call_target="tpu_custom_call" | custom-call | flops 12884901888 | bytes 20971520 | tf_op jit(solution)/shard_map/experts/pallas_call | solution.py:583
  99.3 11.4 %collective-permute-start.6 = (bf16[8,3,128,1024]{3,2,1,0:T(8,128)(2,1)}, bf16[8,3,128,1024]{3,2,1,0:T(8,128)(2,1)S(1)}, u32[]{:S(2)}, u32[]{:S(2)}) collective-permute-start(bf16[8,3,128,1024]{3,2,1,0:T(8,128)(2,1)} %get-tuple-element.104), channel_id=1, source_target_pairs={{0,2},{2,0},{4,6},{6,4},{8,10},{10,8},{12,14},{14,12},{16,18},{18,... | collective-permute-start | bytes 18874376 | tf_op jit(solution)/shard_map/ppermute | solution.py:780
  110.7 19.7 %experts.9 = (bf16[8,3,128,1024]{3,2,1,0:T(8,128)(2,1)}, bf16[32,2,256,1024]{3,2,1,0:T(8,128)(2,1)}, bf16[32,256,1024]{2,1,0:T(8,128)(2,1)}, f32[2,32,1,1024]{3,2,1,0:T(1,128)S(1)}) custom-call(s32[8]{0:T(128)S(1)} %get-tuple-element.207.ids_ref, ...), custom_call_target="tpu_custom_call", output_to_operand_aliasing={{1}: (8, {}), {2}: (9, {}), {3}: (10, {})} | custom-call | flops 12884901888 | bytes 20971520 | tf_op jit(solution)/shard_map/experts/pallas_call | solution.py:583
  130.5 2.6 copy-done.78
  133.0 20.3 %experts.10 = (bf16[8,3,128,1024]{3,2,1,0:T(8,128)(2,1)}, bf16[32,2,256,1024]{3,2,1,0:T(8,128)(2,1)}, bf16[32,256,1024]{2,1,0:T(8,128)(2,1)}, f32[2,32,1,1024]{3,2,1,0:T(1,128)S(1)}) custom-call(s32[8]{0:T(128)S(1)} %get-tuple-element.232.ids_ref, ...), custom_call_target="tpu_custom_call", output_to_operand_aliasing={{1}: (9, {}), {2}: (10, {}), {3}: (11, {})} | custom-call | flops 12884901888 | bytes 20971520 | tf_op jit(solution)/shard_map/experts/pallas_call | solution.py:583
  153.5 1.6 copy-done.2
  155.1 1.6 copy-done.6
  156.7 1.6 copy-done.9
  158.3 19.6 %experts.11 = (bf16[8,3,128,1024]{3,2,1,0:T(8,128)(2,1)}, bf16[32,2,256,1024]{3,2,1,0:T(8,128)(2,1)}, bf16[32,256,1024]{2,1,0:T(8,128)(2,1)}, f32[2,32,1,1024]{3,2,1,0:T(1,128)S(1)}) custom-call(s32[8]{0:T(128)S(1)} %get-tuple-element.206.ids_ref, ...), custom_call_target="tpu_custom_call", output_to_operand_aliasing={{1}: (8, {}), {2}: (9, {}), {3}: (10, {})} | custom-call | flops 12884901888 | bytes 20971520 | tf_op jit(solution)/shard_map/experts/pallas_call | solution.py:583
  177.9 2.6 copy-done.79
  180.6 20.1 %experts.12 = (bf16[8,3,128,1024]{3,2,1,0:T(8,128)(2,1)}, bf16[32,2,256,1024]{3,2,1,0:T(8,128)(2,1)}, bf16[32,256,1024]{2,1,0:T(8,128)(2,1)}, f32[2,32,1,1024]{3,2,1,0:T(1,128)S(1)}) custom-call(s32[8]{0:T(128)S(1)} %get-tuple-element.232.ids_ref, ...), custom_call_target="tpu_custom_call", output_to_operand_aliasing={{1}: (9, {}), {2}: (10, {}), {3}: (11, {})} | custom-call | flops 12884901888 | bytes 20971520 | tf_op jit(solution)/shard_map/experts/pallas_call | solution.py:583
  201.4 1.6 copy-done.3
  203.0 1.6 copy-done.7
  204.6 1.6 copy-done.10
  206.2 20.0 %experts.13 = (bf16[8,3,128,1024]{3,2,1,0:T(8,128)(2,1)}, bf16[32,2,256,1024]{3,2,1,0:T(8,128)(2,1)}, bf16[32,256,1024]{2,1,0:T(8,128)(2,1)}, f32[2,32,1,1024]{3,2,1,0:T(1,128)S(1)}) custom-call(s32[8]{0:T(128)S(1)} %get-tuple-element.206.ids_ref, ...), custom_call_target="tpu_custom_call", output_to_operand_aliasing={{1}: (8, {}), {2}: (9, {}), {3}: (10, {})} | custom-call | flops 12884901888 | bytes 20971520 | tf_op jit(solution)/shard_map/experts/pallas_call | solution.py:583
  226.2 2.7 copy-done.77
  228.8 20.1 %experts.14 = (bf16[8,3,128,1024]{3,2,1,0:T(8,128)(2,1)}, bf16[32,2,256,1024]{3,2,1,0:T(8,128)(2,1)}, bf16[32,256,1024]{2,1,0:T(8,128)(2,1)}, f32[2,32,1,1024]{3,2,1,0:T(1,128)S(1)}) custom-call(s32[8]{0:T(128)S(1)} %get-tuple-element.231.ids_ref, ...), custom_call_target="tpu_custom_call", output_to_operand_aliasing={{1}: (9, {}), {2}: (10, {}), {3}: (11, {})} | custom-call | flops 12884901888 | bytes 20971520 | tf_op jit(solution)/shard_map/experts/pallas_call | solution.py:583
  248.9 2.7 copy-done.76
  251.6 20.0 %experts.15 = (bf16[8,3,128,1024]{3,2,1,0:T(8,128)(2,1)}, bf16[32,2,256,1024]{3,2,1,0:T(8,128)(2,1)}, bf16[32,256,1024]{2,1,0:T(8,128)(2,1)}, f32[2,32,1,1024]{3,2,1,0:T(1,128)S(1)}) custom-call(s32[8]{0:T(128)S(1)} %get-tuple-element.231.ids_ref, ...), custom_call_target="tpu_custom_call", output_to_operand_aliasing={{1}: (9, {}), {2}: (10, {}), {3}: (11, {})} | custom-call | flops 12884901888 | bytes 20971520 | tf_op jit(solution)/shard_map/experts/pallas_call | solution.py:583
  272.3 2.4 copy.65
  276.0 2.6 multiply_reduce_fusion
  279.0 1.8 fusion.13
  280.7 28.5 %multiply_reduce_fusion.2 = (f32[1024]{0:T(1024)S(1)}, f32[512]{0:T(512)S(1)}, f32[512,1024]{1,0:T(8,128)}) fusion(f32[1024,1024]{1,0:T(8,128)} %copy-done.11, f32[512]{0:T(512)S(1)} %get-tuple-element.230, f32[1024]{0:T(1024)S(1)} %convert_element_type.72, f32[512,1024]{1,0:T(8,128)} %fusion.13, bf16[16384,1024]{1,0:T(8,128)(2,1)} %bitcast.68, ...), kind=kOutput, calls=%fused_computation.21 | convolution fusion | flops 17183539200 | bytes 56635392 | tf_op jit(solution)/shard_map/dot_general | solution.py:27
  309.3 2.7 subtract_convert_fusion.1
  312.0 1.7 collective-permute-start.9
  313.7 24.9 %fusion.2 = f32[512,1024]{1,0:T(8,128)S(1)} fusion(bf16[16384,1024]{1,0:T(8,128)(2,1)} %bitcast.69, bf16[16384,1024]{1,0:T(8,128)(2,1)} %bitcast.71), kind=kOutput, calls=%fused_computation.2 | convolution fusion | flops 17179869184 | bytes 52428800 | tf_op jit(solution)/shard_map/dot_general | solution.py:27
  340.6 23.5 %bitcast_convert_fusion = bf16[1024,1024]{1,0:T(8,128)(2,1)} fusion(bf16[32,256,1024]{2,1,0:T(8,128)(2,1)} %get-tuple-element.132, bf16[32,256,1024]{2,1,0:T(8,128)(2,1)} %down_ref.15), kind=kOutput, calls=%fused_computation.7 | convolution fusion | flops 17180917760 | bytes 35651584 | tf_op jit(solution)/shard_map/dot_general | solution.py:27
  367.2 7.1 %enter_back.1 = (f32[1024,1024]{1,0:T(8,128)S(1)}, bf16[512,1024]{1,0:T(8,128)(2,1)S(1)}, bf16[8,1024,64]{2,1,0:T(8,128)(2,1)S(1)}, f32[8,1024]{1,0:T(8,128)S(1)}, f32[512,1024]{1,0:T(8,128)S(1)}) custom-call(bf16[1024,1024]{1,0:T(8,128)(2,1)S(1)} %copy-done, bf16[1024,1024]{1,0:T(8,128)(2,1)S(1)} %pad_maximum_fusion.1.own_ref, ...), custom_call_target="tpu_custom_call" | custom-call | flops 2147483648 | bytes 20971520 | tf_op jit(solution)/shard_map/enter_back/pallas_call | solution.py:423
  374.4 2.0 copy-done.13
  383.7 1.6 copy-done.40
  387.6 1.6 copy-done.55
  392.9 20.2 %attend_back.1 = (f32[512,1024]{1,0:T(8,128)S(1)}, f32[256,1024]{1,0:T(8,128)S(1)}, f32[256,1024]{1,0:T(8,128)S(1)}, bf16[256,1024]{1,0:T(8,128)(2,1)S(1)}, bf16[256,1024]{1,0:T(8,128)(2,1)S(1)}) custom-call(s32[4]{0:T(128)S(1)} %copy-done.59, s32[1,1024]{1,0:T(1,128)S(1)} %bitcast.67, f32[4,2,1024]{2,1,0:T(2,128)S(1)} %pad_maximum_fusion.4.log_ref, ...), custom_call_target="tpu_custom_call" | custom-call | flops 21474836480 | bytes 16777216 | tf_op jit(solution)/shard_map/attend_back/pallas_call | solution.py:216
  415.1 1.6 collective-permute-start.12
  418.5 17.6 %collective-permute-done.12.more_dk_ref = bf16[256,1024]{1,0:T(8,128)(2,1)S(1)} collective-permute-done((bf16[256,1024]{1,0:T(8,128)(2,1)S(1)}, bf16[256,1024]{1,0:T(8,128)(2,1)S(1)}, u32[]{:S(2)}, u32[]{:S(2)}) %collective-permute-start.12) | collective-permute-done | bytes 524320 | tf_op jit(solution)/shard_map/ppermute | solution.py:830
  437.7 1.6 copy-done.37
  444.9 11.2 %leave_back.1 = (bf16[1024,1024]{1,0:T(8,128)(2,1)S(1)}, bf16[896,1024]{1,0:T(8,128)(2,1)}, bf16[896,1024]{1,0:T(8,128)(2,1)S(1)}) custom-call(s32[1]{0:T(128)} %bitcast.19.core_ref, bf16[1024,1024]{1,0:T(8,128)(2,1)S(1)} %copy-done.37, bf16[1,1024]{1,0:T(2,128)(2,1)S(1)} %copy-done.34, f32[32,1024]{1,0:T(8,128)S(1)} %copy-done.32, ...), custom_call_target="tpu_custom_call" | custom-call | flops 4294967296 | bytes 25165824 | tf_op jit(solution)/shard_map/leave_back/pallas_call | solution.py:502
  457.9 3.7 collective-permute-done.14
  461.7 4.1 add_convert_fusion.1
  467.8 24.7 %collective-permute-done.15 = bf16[512,1024]{1,0:T(8,128)(2,1)} collective-permute-done((bf16[512,1024]{1,0:T(8,128)(2,1)S(1)}, bf16[512,1024]{1,0:T(8,128)(2,1)}, u32[]{:S(2)}, u32[]{:S(2)}) %collective-permute-start.15) | collective-permute-done | bytes 1048608 | tf_op jit(solution)/shard_map/ppermute | solution.py:626
  492.6 6.4 %reduce-scatter.14.cloned.1.call-done = bf16[112,1024]{1,0:T(8,128)(2,1)} async-done(((bf16[896,1024]{1,0:T(8,128)(2,1)}), bf16[112,1024]{1,0:T(8,128)(2,1)}) %reduce-scatter.14.cloned.1.call-update) | async-done | bytes 229392 | tf_op jit(solution)/shard_map/reduce_scatter | solution.py:681
  499.0 1.6 collective-permute-start.16
  500.6 20.7 %collective-permute-done.16 = bf16[512,1024]{1,0:T(8,128)(2,1)} collective-permute-done((bf16[512,1024]{1,0:T(8,128)(2,1)}, bf16[512,1024]{1,0:T(8,128)(2,1)}, u32[]{:S(2)}, u32[]{:S(2)}) %collective-permute-start.16) | collective-permute-done | bytes 1048608 | tf_op jit(solution)/shard_map/ppermute | solution.py:626
  521.2 10.8 %all-gather.2.cloned.1.call-done = bf16[896,1024]{1,0:T(8,128)(2,1)} async-done(((bf16[112,1024]{1,0:T(8,128)(2,1)}), bf16[896,1024]{1,0:T(8,128)(2,1)}) %all-gather.2.cloned.1.call-update) | async-done | bytes 1835024 | tf_op jit(solution)/shard_map/all_gather | solution.py:683
  532.0 6.0 %add_convert_fusion = bf16[1024,1024]{1,0:T(8,128)(2,1)} fusion(f32[1024,1024]{1,0:T(8,128)} %copy-done.11, bf16[1024,1024]{1,0:T(8,128)(2,1)} %collective-permute-done.11, bf16[1024,1024]{1,0:T(8,128)(2,1)} %bitcast_convert_fusion), kind=kLoop, calls=%fused_computation.8 | loop fusion | flops 5242880 | bytes 10485760 | tf_op jit(solution)/shard_map/convert_element_type | solution.py:852
  539.2 2.3 slice.90
  541.5 1.6 convert_bitcast_fusion
  543.1 2.6 convert_add_fusion.1
  545.9 2.1 fusion.4
  548.2 1.8 maximum_convert_fusion.2
  553.7 2.9 copy.66
  556.6 1.6 maximum_convert_fusion.1
  558.2 6.0 %collective-permute-done.18 = bf16[256,1024]{1,0:T(8,128)(2,1)S(1)} collective-permute-done((bf16[256,1024]{1,0:T(8,128)(2,1)S(1)}, bf16[256,1024]{1,0:T(8,128)(2,1)S(1)}, u32[]{:S(2)}, u32[]{:S(2)}) %collective-permute-start.18) | collective-permute-done | bytes 524320 | tf_op jit(solution)/shard_map/ppermute | solution.py:626
  (249 shorter events, 61.8 us)
Async XLA Ops:
  7.2 411.3 %reduce-scatter.6.cloned.1.call-start = ((), (), s32[]{:S(2)}) async-start(), calls=%async_computation.5 | async-start | bytes 7077888 | tf_op jit(solution)/shard_map/reduce_scatter | solution.py:671
  7.2 54.9 %collective-permute-start.4 = (bf16[512,1024]{1,0:T(8,128)(2,1)}, bf16[512,1024]{1,0:T(8,128)(2,1)}, u32[]{:S(2)}, u32[]{:S(2)}) collective-permute-start(bf16[512,1024]{1,0:T(8,128)(2,1)} %wo_ref.1), channel_id=1, source_target_pairs={{0,1},{1,0},{2,3},{3,2},{4,5},{5,4},{6,7},{7,6},{8,9},{9,8},{10,11... | collective-permute-start | bytes 3145736 | tf_op jit(solution)/shard_map/ppermute | solution.py:626
  11.0 11.8 %copy-start.33 = (bf16[1,1024]{1,0:T(2,128)(2,1)}, bf16[1,1024]{1,0:T(2,128)(2,1)S(1)}, u32[]{:S(2)}) copy-start(bf16[1,1024]{1,0:T(2,128)(2,1)S(1)} %broadcast_in_dim.19.gain_ref) | copy-start | bytes 6148
  11.5 11.2 %copy-start.29 = (f32[32,1024]{1,0:T(8,128)}, f32[32,1024]{1,0:T(8,128)S(1)}, u32[]{:S(2)}) copy-start(f32[32,1024]{1,0:T(8,128)S(1)} %get-tuple-element.227.sin_ref) | copy-start | bytes 393220
  11.5 11.2 %copy-start.31 = (f32[32,1024]{1,0:T(8,128)}, f32[32,1024]{1,0:T(8,128)S(1)}, u32[]{:S(2)}) copy-start(f32[32,1024]{1,0:T(8,128)S(1)} %get-tuple-element.228.cos_ref) | copy-start | bytes 393220
  16.5 17.3 %copy-start.87 = (bf16[1024]{0:T(1024)(128)(2,1)S(1)}, bf16[1024]{0:T(1024)(128)(2,1)}, u32[]{:S(2)}) copy-start(bf16[1024]{0:T(1024)(128)(2,1)} %param.29) | copy-start | bytes 6148
  16.5 17.4 %copy-start = (bf16[1024,1024]{1,0:T(8,128)(2,1)S(1)}, bf16[1024,1024]{1,0:T(8,128)(2,1)}, u32[]{:S(2)}) copy-start(bf16[1024,1024]{1,0:T(8,128)(2,1)} %c_ref.17) | copy-start | bytes 6291460
  28.3 8.2 %copy-start.49 = (bf16[256,1024]{1,0:T(8,128)(2,1)}, bf16[256,1024]{1,0:T(8,128)(2,1)S(1)}, u32[]{:S(2)}) copy-start(bf16[256,1024]{1,0:T(8,128)(2,1)S(1)} %get-tuple-element.93.kt_ref) | copy-start | bytes 1572868
  28.3 8.3 %collective-permute-start = (bf16[256,1024]{1,0:T(8,128)(2,1)S(1)}, bf16[256,1024]{1,0:T(8,128)(2,1)S(1)}, u32[]{:S(2)}, u32[]{:S(2)}) collective-permute-start(bf16[256,1024]{1,0:T(8,128)(2,1)S(1)} %get-tuple-element.93.kt_ref), channel_id=1, source_target_pairs={{0,2},{4,6},{8,10},{12,14},{16,18},{20,22},{24,26},{28,30},{1,3},{... | collective-permute-start | bytes 1572872 | tf_op jit(solution)/shard_map/ppermute | solution.py:739
  29.8 9.1 %collective-permute-start.1 = (bf16[256,1024]{1,0:T(8,128)(2,1)}, bf16[256,1024]{1,0:T(8,128)(2,1)}, u32[]{:S(2)}, u32[]{:S(2)}) collective-permute-start(bf16[256,1024]{1,0:T(8,128)(2,1)} %get-tuple-element.92.vt_ref), channel_id=1, source_target_pairs={{0,2},{4,6},{8,10},{12,14},{16,18},{20,22},{24,26},{28,30},{1,3},{... | collective-permute-start | bytes 1572872 | tf_op jit(solution)/shard_map/ppermute | solution.py:740
  33.8 17.3 %copy-start.56 = (s32[1024]{0:T(1024)}, s32[1024]{0:T(1024)S(1)}, u32[]{:S(2)}) copy-start(s32[1024]{0:T(1024)S(1)} %convert_reduce_fusion) | copy-start | bytes 12292
  36.6 14.6 %copy-start.58 = (s32[4]{0:T(128)}, s32[4]{0:T(128)S(1)}, u32[]{:S(2)}) copy-start(s32[4]{0:T(128)S(1)} %and_select_fusion.first_ref) | copy-start | bytes 52
  38.9 12.2 %copy-start.20 = (bf16[4,64,1024]{1,2,0:T(8,128)(2,1)}, bf16[4,64,1024]{1,2,0:T(8,128)(2,1)S(1)}, u32[]{:S(2)}) copy-start(bf16[4,64,1024]{1,2,0:T(8,128)(2,1)S(1)} %copy.62) | copy-start | bytes 1572868
  41.8 9.4 %copy-start.68 = (bf16[512,1024]{1,0:T(8,128)(2,1)S(1)}, bf16[512,1024]{1,0:T(8,128)(2,1)}, u32[]{:S(2)}) copy-start(bf16[512,1024]{1,0:T(8,128)(2,1)} %copy-done.66) | copy-start | bytes 3145732
  50.8 20.5 %copy-start.25 = (bf16[256,1024]{1,0:T(8,128)(2,1)}, bf16[256,1024]{1,0:T(8,128)(2,1)S(1)}, u32[]{:S(2)}) copy-start(bf16[256,1024]{1,0:T(8,128)(2,1)S(1)} %get-tuple-element.95.refs_1_) | copy-start | bytes 1572868
  50.8 11.2 %copy-start.15 = (bf16[512,1024]{1,0:T(8,128)(2,1)S(1)}, bf16[512,1024]{1,0:T(8,128)(2,1)}, u32[]{:S(2)}) copy-start(bf16[512,1024]{1,0:T(8,128)(2,1)} %wo_ref.1) | copy-start | bytes 3145732
  50.8 12.6 %collective-permute-start.3 = (bf16[256,1024]{1,0:T(8,128)(2,1)S(1)}, bf16[256,1024]{1,0:T(8,128)(2,1)S(1)}, u32[]{:S(2)}, u32[]{:S(2)}) collective-permute-start(bf16[256,1024]{1,0:T(8,128)(2,1)S(1)} %get-tuple-element.95.refs_1_), channel_id=1, source_target_pairs={{0,1},{1,0},{2,3},{3,2},{4,5},{5,4},{6,7},{7,6},{8,9},{9,8},{10,11... | collective-permute-start | bytes 1572872 | tf_op jit(solution)/shard_map/ppermute | solution.py:626
  60.2 11.1 %copy-start.26 = (bf16[256,1024]{1,0:T(8,128)(2,1)}, bf16[256,1024]{1,0:T(8,128)(2,1)S(1)}, u32[]{:S(2)}) copy-start(bf16[256,1024]{1,0:T(8,128)(2,1)S(1)} %get-tuple-element.94.refs_0_) | copy-start | bytes 1572868
  60.2 11.1 %copy-start.27 = (bf16[1024,32]{0,1:T(8,128)(2,1)S(1)}, bf16[1024,32]{0,1:T(8,128)(2,1)}, u32[]{:S(2)}) copy-start(bf16[1024,32]{0,1:T(8,128)(2,1)} %param.30) | copy-start | bytes 196612
  60.2 11.1 %copy-start.36 = (bf16[1024,1024]{1,0:T(8,128)(2,1)S(1)}, bf16[1024,1024]{1,0:T(8,128)(2,1)}, u32[]{:S(2)}) copy-start(bf16[1024,1024]{1,0:T(8,128)(2,1)} %x_ref.5) | copy-start | bytes 6291460
  60.2 11.1 %copy-start.53 = (s32[1024,8]{0,1:T(8,128)S(1)}, s32[1024,8]{0,1:T(8,128)}, u32[]{:S(2)}) copy-start(s32[1024,8]{0,1:T(8,128)} %param.23) | copy-start | bytes 98308
  60.2 11.1 %collective-permute-start.2 = (bf16[256,1024]{1,0:T(8,128)(2,1)S(1)}, bf16[256,1024]{1,0:T(8,128)(2,1)S(1)}, u32[]{:S(2)}, u32[]{:S(2)}) collective-permute-start(bf16[256,1024]{1,0:T(8,128)(2,1)S(1)} %get-tuple-element.94.refs_0_), channel_id=1, source_target_pairs={{0,1},{1,0},{2,3},{3,2},{4,5},{5,4},{6,7},{7,6},{8,9},{9,8},{10,11... | collective-permute-start | bytes 1572872 | tf_op jit(solution)/shard_map/ppermute | solution.py:626
  71.3 7.7 %copy-start.5 = (bf16[1024,1024]{0,1:T(8,128)(2,1)S(1)}, bf16[1024,1024]{0,1:T(8,128)(2,1)}, u32[]{:S(2)}) copy-start(bf16[1024,1024]{0,1:T(8,128)(2,1)} %copy.63) | copy-start | bytes 6291460
  78.9 20.4 %copy-start.18 = (f32[32,1024]{1,0:T(8,128)}, f32[32,1024]{1,0:T(8,128)S(1)}, u32[]{:S(2)}) copy-start(f32[32,1024]{1,0:T(8,128)S(1)} %get-tuple-element.97) | copy-start | bytes 393220
  78.9 51.5 %copy-start.1 = (bf16[1024,1024]{1,0:T(8,128)(2,1)}, bf16[1024,1024]{1,0:T(8,128)(2,1)S(1)}, u32[]{:S(2)}) copy-start(bf16[1024,1024]{1,0:T(8,128)(2,1)S(1)} %get-tuple-element.99.x_ref) | copy-start | bytes 6291460
  78.9 51.5 %copy-start.8 = (bf16[1024,1024]{1,0:T(8,128)(2,1)}, bf16[1024,1024]{1,0:T(8,128)(2,1)S(1)}, u32[]{:S(2)}) copy-start(bf16[1024,1024]{1,0:T(8,128)(2,1)S(1)} %get-tuple-element.98.xt_ref) | copy-start | bytes 6291460
  99.3 31.1 %collective-permute-start.6 = (bf16[8,3,128,1024]{3,2,1,0:T(8,128)(2,1)}, bf16[8,3,128,1024]{3,2,1,0:T(8,128)(2,1)S(1)}, u32[]{:S(2)}, u32[]{:S(2)}) collective-permute-start(bf16[8,3,128,1024]{3,2,1,0:T(8,128)(2,1)} %get-tuple-element.104), channel_id=1, source_target_pairs={{0,2},{2,0},{4,6},{6,4},{8,10},{10,8},{12,14},{14,12},{16,18},{18,... | collective-permute-start | bytes 18874376 | tf_op jit(solution)/shard_map/ppermute | solution.py:780
  153.4 265.2 %reduce-scatter.8.cloned.1.call-start = ((), (), s32[]{:S(2)}) async-start(), calls=%async_computation.6 | async-start | bytes 7077888 | tf_op jit(solution)/shard_map/reduce_scatter | solution.py:671
  153.4 24.5 %collective-permute-start.5 = (bf16[8,3,128,1024]{3,2,1,0:T(8,128)(2,1)}, bf16[8,3,128,1024]{3,2,1,0:T(8,128)(2,1)S(1)}, u32[]{:S(2)}, u32[]{:S(2)}) collective-permute-start(bf16[8,3,128,1024]{3,2,1,0:T(8,128)(2,1)} %get-tuple-element.103), channel_id=1, source_target_pairs={{0,2},{2,0},{4,6},{6,4},{8,10},{10,8},{12,14},{14,12},{16,18},{18,... | collective-permute-start | bytes 18874376 | tf_op jit(solution)/shard_map/ppermute | solution.py:780
  200.7 257.2 %reduce-scatter.12.cloned.1.call-start = ((), (), s32[]{:S(2)}) async-start(), calls=%async_computation.8 | async-start | bytes 7077888 | tf_op jit(solution)/shard_map/reduce_scatter | solution.py:671
  200.7 25.4 %collective-permute-start.8 = (bf16[8,3,128,1024]{3,2,1,0:T(8,128)(2,1)}, bf16[8,3,128,1024]{3,2,1,0:T(8,128)(2,1)S(1)}, u32[]{:S(2)}, u32[]{:S(2)}) collective-permute-start(bf16[8,3,128,1024]{3,2,1,0:T(8,128)(2,1)} %get-tuple-element.118), channel_id=1, source_target_pairs={{0,2},{2,0},{4,6},{6,4},{8,10},{10,8},{12,14},{14,12},{16,18},{18,... | collective-permute-start | bytes 18874376 | tf_op jit(solution)/shard_map/ppermute | solution.py:780
  226.1 22.8 %collective-permute-start.7 = (bf16[8,3,128,1024]{3,2,1,0:T(8,128)(2,1)}, bf16[8,3,128,1024]{3,2,1,0:T(8,128)(2,1)S(1)}, u32[]{:S(2)}, u32[]{:S(2)}) collective-permute-start(bf16[8,3,128,1024]{3,2,1,0:T(8,128)(2,1)} %get-tuple-element.117), channel_id=1, source_target_pairs={{0,2},{2,0},{4,6},{6,4},{8,10},{10,8},{12,14},{14,12},{16,18},{18,... | collective-permute-start | bytes 18874376 | tf_op jit(solution)/shard_map/ppermute | solution.py:780
  271.7 186.3 %reduce-scatter.10.cloned.1.call-start = ((), (), s32[]{:S(2)}) async-start(), calls=%async_computation.7 | async-start | bytes 7077888 | tf_op jit(solution)/shard_map/reduce_scatter | solution.py:671
  276.0 2.8 copy-start.19
  276.0 2.9 copy-start.28
  279.0 59.7 %copy-start.85 = (bf16[32,1024]{1,0:T(8,128)(2,1)}, bf16[32,1024]{1,0:T(8,128)(2,1)S(1)}, u32[]{:S(2)}) copy-start(bf16[32,1024]{1,0:T(8,128)(2,1)S(1)} %fusion.11) | copy-start | bytes 196612
  309.3 189.7 %reduce-scatter.14.cloned.1.call-start = ((), (), s32[]{:S(2)}) async-start(), calls=%async_computation.9 | async-start | bytes 2064384 | tf_op jit(solution)/shard_map/reduce_scatter | solution.py:681
  312.0 26.6 %copy-start.12 = (f32[1024,1024]{1,0:T(8,128)S(1)}, f32[1024,1024]{1,0:T(8,128)}, u32[]{:S(2)}) copy-start(f32[1024,1024]{1,0:T(8,128)} %copy-done.11) | copy-start | bytes 12582916
  312.0 27.8 %collective-permute-start.9 = (bf16[512,1024]{1,0:T(8,128)(2,1)S(1)}, bf16[512,1024]{1,0:T(8,128)(2,1)}, u32[]{:S(2)}, u32[]{:S(2)}) collective-permute-start(bf16[512,1024]{1,0:T(8,128)(2,1)S(1)} %subtract_convert_fusion.1), channel_id=1, source_target_pairs={{0,1},{1,0},{2,3},{3,2},{4,5},{5,4},{6,7},{7,6},{8,9},{9,8},{10,11... | collective-permute-start | bytes 3145736 | tf_op jit(solution)/shard_map/ppermute | solution.py:626
  339.8 25.2 %collective-permute-start.10 = (bf16[512,1024]{1,0:T(8,128)(2,1)S(1)}, bf16[512,1024]{1,0:T(8,128)(2,1)S(1)}, u32[]{:S(2)}, u32[]{:S(2)}) collective-permute-start(bf16[512,1024]{1,0:T(8,128)(2,1)S(1)} %subtract_convert_fusion), channel_id=1, source_target_pairs={{0,1},{1,0},{2,3},{3,2},{4,5},{5,4},{6,7},{7,6},{8,9},{9,8},{10,11... | collective-permute-start | bytes 3145736 | tf_op jit(solution)/shard_map/ppermute | solution.py:626
  364.3 2.9 copy-start.16
  366.5 13.7 %copy-start.57 = (s32[1024]{0:T(1024)S(1)}, s32[1024]{0:T(1024)}, u32[]{:S(2)}) copy-start(s32[1024]{0:T(1024)} %copy-done.56) | copy-start | bytes 12292
  366.5 13.7 %copy-start.59 = (s32[4]{0:T(128)S(1)}, s32[4]{0:T(128)}, u32[]{:S(2)}) copy-start(s32[4]{0:T(128)} %copy-done.58) | copy-start | bytes 52
  366.5 52.0 %collective-permute-start.11 = (bf16[1024,1024]{1,0:T(8,128)(2,1)}, bf16[1024,1024]{1,0:T(8,128)(2,1)}, u32[]{:S(2)}, u32[]{:S(2)}) collective-permute-start(bf16[1024,1024]{1,0:T(8,128)(2,1)} %bitcast_convert_fusion), channel_id=1, source_target_pairs={{0,1},{1,0},{2,3},{3,2},{4,5},{5,4},{6,7},{7,6},{8,9},{9,8},{10,11... | collective-permute-start | bytes 6291464 | tf_op jit(solution)/shard_map/ppermute | solution.py:626
  392.9 25.1 %copy-start.4 = (bf16[1024,1024]{1,0:T(8,128)(2,1)S(1)}, bf16[1024,1024]{1,0:T(8,128)(2,1)}, u32[]{:S(2)}) copy-start(bf16[1024,1024]{1,0:T(8,128)(2,1)} %copy-done.1) | copy-start | bytes 6291460
  392.9 25.1 %copy-start.86 = (bf16[32,1024]{1,0:T(8,128)(2,1)S(1)}, bf16[32,1024]{1,0:T(8,128)(2,1)}, u32[]{:S(2)}) copy-start(bf16[32,1024]{1,0:T(8,128)(2,1)} %copy-done.85) | copy-start | bytes 196612
  415.1 3.4 copy-start.61
  415.1 22.6 %copy-start.30 = (f32[32,1024]{1,0:T(8,128)S(1)}, f32[32,1024]{1,0:T(8,128)}, u32[]{:S(2)}) copy-start(f32[32,1024]{1,0:T(8,128)} %copy-done.29) | copy-start | bytes 393220
  415.1 22.6 %copy-start.32 = (f32[32,1024]{1,0:T(8,128)S(1)}, f32[32,1024]{1,0:T(8,128)}, u32[]{:S(2)}) copy-start(f32[32,1024]{1,0:T(8,128)} %copy-done.31) | copy-start | bytes 393220
  415.1 22.6 %copy-start.34 = (bf16[1,1024]{1,0:T(2,128)(2,1)S(1)}, bf16[1,1024]{1,0:T(2,128)(2,1)}, u32[]{:S(2)}) copy-start(bf16[1,1024]{1,0:T(2,128)(2,1)} %copy-done.33) | copy-start | bytes 6148
  415.1 22.6 %copy-start.42 = (bf16[1024,512]{1,0:T(8,128)(2,1)S(1)}, bf16[1024,512]{1,0:T(8,128)(2,1)}, u32[]{:S(2)}) copy-start(bf16[1024,512]{1,0:T(8,128)(2,1)} %wq_ref.3) | copy-start | bytes 3145732
  415.1 21.1 %collective-permute-start.12 = (bf16[256,1024]{1,0:T(8,128)(2,1)S(1)}, bf16[256,1024]{1,0:T(8,128)(2,1)S(1)}, u32[]{:S(2)}, u32[]{:S(2)}) collective-permute-start(bf16[256,1024]{1,0:T(8,128)(2,1)S(1)} %get-tuple-element.152), channel_id=1, source_target_pairs={{2,0},{6,4},{10,8},{14,12},{18,16},{22,20},{26,24},{30,28},{3,1},{... | collective-permute-start | bytes 1572872 | tf_op jit(solution)/shard_map/ppermute | solution.py:830
  416.7 21.0 %collective-permute-start.13 = (bf16[256,1024]{1,0:T(8,128)(2,1)S(1)}, bf16[256,1024]{1,0:T(8,128)(2,1)}, u32[]{:S(2)}, u32[]{:S(2)}) collective-permute-start(bf16[256,1024]{1,0:T(8,128)(2,1)S(1)} %get-tuple-element.153), channel_id=1, source_target_pairs={{2,0},{6,4},{10,8},{14,12},{18,16},{22,20},{26,24},{30,28},{3,1},{... | collective-permute-start | bytes 1572872 | tf_op jit(solution)/shard_map/ppermute | solution.py:831
  457.3 4.4 collective-permute-start.14
  465.8 66.2 %all-gather.2.cloned.1.call-start = ((), (), s32[]{:S(2)}) async-start(), calls=%async_computation.10 | async-start | bytes 2064384 | tf_op jit(solution)/shard_map/all_gather | solution.py:683
  467.0 25.5 %collective-permute-start.15 = (bf16[512,1024]{1,0:T(8,128)(2,1)S(1)}, bf16[512,1024]{1,0:T(8,128)(2,1)}, u32[]{:S(2)}, u32[]{:S(2)}) collective-permute-start(bf16[512,1024]{1,0:T(8,128)(2,1)S(1)} %get-tuple-element.217), channel_id=1, source_target_pairs={{0,1},{1,0},{2,3},{3,2},{4,5},{5,4},{6,7},{7,6},{8,9},{9,8},{10,11... | collective-permute-start | bytes 3145736 | tf_op jit(solution)/shard_map/ppermute | solution.py:626
  499.0 39.1 %copy-start.80 = (bf16[1,3,128,1024]{3,2,1,0:T(8,128)(2,1)S(1)}, bf16[1,3,128,1024]{3,2,1,0:T(8,128)(2,1)}, u32[]{:S(2)}) copy-start(bf16[1,3,128,1024]{3,2,1,0:T(8,128)(2,1)} %reduce-scatter.6.cloned.1.call-done) | copy-start | bytes 2359300
  499.0 22.2 %collective-permute-start.16 = (bf16[512,1024]{1,0:T(8,128)(2,1)}, bf16[512,1024]{1,0:T(8,128)(2,1)}, u32[]{:S(2)}, u32[]{:S(2)}) collective-permute-start(bf16[512,1024]{1,0:T(8,128)(2,1)} %get-tuple-element.216), channel_id=1, source_target_pairs={{0,1},{1,0},{2,3},{3,2},{4,5},{5,4},{6,7},{7,6},{8,9},{9,8},{10,11... | collective-permute-start | bytes 3145736 | tf_op jit(solution)/shard_map/ppermute | solution.py:626
  532.0 6.1 %copy-start.81 = (bf16[1,3,128,1024]{3,2,1,0:T(8,128)(2,1)S(1)}, bf16[1,3,128,1024]{3,2,1,0:T(8,128)(2,1)}, u32[]{:S(2)}) copy-start(bf16[1,3,128,1024]{3,2,1,0:T(8,128)(2,1)} %reduce-scatter.8.cloned.1.call-done) | copy-start | bytes 2359300
  532.0 6.1 %copy-start.82 = (bf16[1,3,128,1024]{3,2,1,0:T(8,128)(2,1)S(1)}, bf16[1,3,128,1024]{3,2,1,0:T(8,128)(2,1)}, u32[]{:S(2)}) copy-start(bf16[1,3,128,1024]{3,2,1,0:T(8,128)(2,1)} %reduce-scatter.12.cloned.1.call-done) | copy-start | bytes 2359300
  532.0 6.1 %copy-start.83 = (bf16[1,3,128,1024]{3,2,1,0:T(8,128)(2,1)S(1)}, bf16[1,3,128,1024]{3,2,1,0:T(8,128)(2,1)}, u32[]{:S(2)}) copy-start(bf16[1,3,128,1024]{3,2,1,0:T(8,128)(2,1)} %reduce-scatter.10.cloned.1.call-done) | copy-start | bytes 2359300
  532.0 15.9 %collective-permute-start.17 = (bf16[896,1024]{1,0:T(8,128)(2,1)}, bf16[896,1024]{1,0:T(8,128)(2,1)S(1)}, u32[]{:S(2)}, u32[]{:S(2)}) collective-permute-start(bf16[896,1024]{1,0:T(8,128)(2,1)} %all-gather.2.cloned.1.call-done), channel_id=1, source_target_pairs={{0,2},{2,0},{4,6},{6,4},{8,10},{10,8},{12,14},{14,12},{16,18},{18,... | collective-permute-start | bytes 5505032 | tf_op jit(solution)/shard_map/ppermute | solution.py:685
  548.2 3.3 copy-start.75
  550.0 14.2 %collective-permute-start.18 = (bf16[256,1024]{1,0:T(8,128)(2,1)S(1)}, bf16[256,1024]{1,0:T(8,128)(2,1)S(1)}, u32[]{:S(2)}, u32[]{:S(2)}) collective-permute-start(bf16[256,1024]{1,0:T(8,128)(2,1)S(1)} %get-tuple-element.218), channel_id=1, source_target_pairs={{0,1},{1,0},{2,3},{3,2},{4,5},{5,4},{6,7},{7,6},{8,9},{9,8},{10,11... | collective-permute-start | bytes 1572872 | tf_op jit(solution)/shard_map/ppermute | solution.py:626
  (52 other events, 76.6 us)
Sparse Core Ops, SparseCore 0:
  153.5 69.7 reduce-scatter.5
  225.6 68.3 reduce-scatter.7
  296.3 68.3 reduce-scatter.11
  366.8 68.3 reduce-scatter.9
  465.9 32.9 reduce-scatter.13
  500.4 31.5 all-gather.1

commit v3 on v2

--- a/solution.py
+++ b/solution.py
@@ -17,8 +17,7 @@
 residual_scale = 0.22
 rope_base = 10000.0
 masked_value = -1e30
-vmem_bytes = 24 * 1024 * 1024
-expert_vmem_bytes = 40 * 1024 * 1024
+vmem_bytes = 60 * 1024 * 1024
 f32 = jnp.float32
 bf16 = jnp.bfloat16
 
@@ -55,83 +54,96 @@
     )
 
 
-def heads_one_above(ref, block, group):
+def heads_one_above(ref, j, block, group):
     cut = pl.ds(block * BLOCK, BLOCK)
-    return jnp.concatenate([ref[0, h, cut, :] for h in range(group)], axis=0)
+    return jnp.concatenate([ref[j, h, cut, :] for h in range(group)], axis=0)
 
 
 def attend_kernel(
     group, first_ref, lo_ref, qt_ref, k_ref, vt_ref, old_k_ref, old_vt_ref, out_ref, log_ref
 ):
     lanes = group * BLOCK
-    before = old_k_ref.shape[1]
+    together, before, _ = old_k_ref.shape
+    tall = group * HEAD_DIM
     passed = before // BLOCK
     for block in range(qt_ref.shape[1] // BLOCK):
         lo, hi = window_of(lo_ref, block, before, group)
-        query = heads_side_by_side(qt_ref, block, group)
+        queries = [
+            heads_side_by_side(qt_ref.at[pl.ds(j * tall, tall)], block, group)
+            for j in range(together)
+        ]
 
         def step(keys_ref, values_ref, offset, number, carry):
-            peak, total, acc = carry
             start = pl.multiple_of(number * BLOCK, BLOCK)
-            scores = mm(keys_ref[0, pl.ds(start, BLOCK), :], query)
-            scores = jnp.where(block_mask(lo, hi, offset + start, lanes), scores, masked_value)
-            top = jnp.maximum(peak, jnp.max(scores, axis=0, keepdims=True))
-            weights = jnp.exp(scores - top)
-            fade = jnp.exp(peak - top)
-            total = total * fade + jnp.sum(weights, axis=0, keepdims=True)
-            acc = acc * fade + mm(values_ref[:, pl.ds(start, BLOCK)], weights.astype(bf16))
-            return (top, total, acc)
+            here = pl.ds(start, BLOCK)
+            mask = block_mask(lo, hi, offset + start, lanes)
+            result = []
+            for j, (peak, total, acc) in enumerate(carry):
+                scores = mm(keys_ref[j, here, :], queries[j])
+                scores = jnp.where(mask, scores, masked_value)
+                top = jnp.maximum(peak, jnp.max(scores, axis=0, keepdims=True))
+                weights = jnp.exp(scores - top)
+                fade = jnp.exp(peak - top)
+                total = total * fade + jnp.sum(weights, axis=0, keepdims=True)
+                values = values_ref[j * HEAD_DIM : (j + 1) * HEAD_DIM, here]
+                result.append((top, total, acc * fade + mm(values, weights.astype(bf16))))
+            return tuple(result)
 
         first = first_ref[block]
-        carry = (
+        nothing = (
             jnp.full((1, lanes), masked_value, f32),
             jnp.zeros((1, lanes), f32),
             jnp.zeros((HEAD_DIM, lanes), f32),
         )
         carry = lax.fori_loop(
-            first, passed, functools.partial(step, old_k_ref, old_vt_ref, 0), carry
+            first, passed, functools.partial(step, old_k_ref, old_vt_ref, 0), (nothing,) * together
         )
-        peak, total, acc = lax.fori_loop(
+        carry = lax.fori_loop(
             jnp.maximum(first - passed, 0),
             block + 1,
             functools.partial(step, k_ref, vt_ref, before),
             carry,
         )
-        result = (acc / total).astype(bf16)
-        logs = peak + jnp.log(total)
         cut = pl.ds(block * BLOCK, BLOCK)
-        for h in range(group):
-            side = slice(h * BLOCK, (h + 1) * BLOCK)
-            out_ref[h * HEAD_DIM : (h + 1) * HEAD_DIM, cut] = result[:, side]
-            log_ref[0, h : h + 1, cut] = logs[:, side]
+        for j, (peak, total, acc) in enumerate(carry):
+            result = (acc / total).astype(bf16)
+            logs = peak + jnp.log(total)
+            for h in range(group):
+                side = slice(h * BLOCK, (h + 1) * BLOCK)
+                high = j * tall + h * HEAD_DIM
+                out_ref[high : high + HEAD_DIM, cut] = result[:, side]
+                log_ref[j, h : h + 1, cut] = logs[:, side]
 
 
 def attend(first, lo, q_t, k, v_t, old_k, old_v_t, group, base, pair_heads):
     rows = k.shape[1]
     before = old_k.shape[1]
-    tall = group * HEAD_DIM
-    by_head = lambda h, s: (base + h, 0, 0)
-    flat = lambda h, s: (base + h, 0)
+    together = 1
+    start = base // together
+    tall = together * group * HEAD_DIM
+    split = together * HEAD_DIM
+    by_head = lambda h, s: (start + h, 0, 0)
+    flat = lambda h, s: (start + h, 0)
     return pl.pallas_call(
         functools.partial(attend_kernel, group),
         grid_spec=pltpu.PrefetchScalarGridSpec(
             num_scalar_prefetch=1,
-            grid=(pair_heads,),
+            grid=(pair_heads // together,),
             in_specs=[
                 pl.BlockSpec((1, rows), lambda h, s: (0, 0)),
                 pl.BlockSpec((tall, rows), flat),
-                pl.BlockSpec((1, rows, HEAD_DIM), by_head),
-                pl.BlockSpec((HEAD_DIM, rows), flat),
-                pl.BlockSpec((1, before, HEAD_DIM), by_head),
-                pl.BlockSpec((HEAD_DIM, before), flat),
+                pl.BlockSpec((together, rows, HEAD_DIM), by_head),
+                pl.BlockSpec((split, rows), flat),
+                pl.BlockSpec((together, before, HEAD_DIM), by_head),
+                pl.BlockSpec((split, before), flat),
             ],
             out_specs=[
                 pl.BlockSpec((tall, rows), lambda h, s: (h, 0)),
-                pl.BlockSpec((1, group, rows), lambda h, s: (h, 0, 0)),
+                pl.BlockSpec((together, group, rows), lambda h, s: (h, 0, 0)),
             ],
         ),
         out_shape=[
-            jax.ShapeDtypeStruct((pair_heads * tall, rows), bf16),
+            jax.ShapeDtypeStruct((pair_heads * group * HEAD_DIM, rows), bf16),
             jax.ShapeDtypeStruct((pair_heads, group, rows), f32),
         ],
         compiler_params=pltpu.CompilerParams(vmem_limit_bytes=vmem_bytes),
@@ -151,57 +163,74 @@
     dq_ref, dk_ref, dv_ref, old_dk_ref, old_dv_ref, pair_ref, old_pair_ref,
 ):
     lanes = group * BLOCK
-    before = old_k_ref.shape[1]
+    together, before, _ = old_k_ref.shape
+    tall = group * HEAD_DIM
     passed = before // BLOCK
     pair_ref[...] = jnp.zeros_like(pair_ref)
     old_pair_ref[...] = jnp.zeros_like(old_pair_ref)
     for block in range(qt_ref.shape[1] // BLOCK):
         cut = pl.ds(block * BLOCK, BLOCK)
         lo, hi = window_of(lo_ref, block, before, group)
-        query = heads_side_by_side(qt_ref, block, group)
-        upstream = heads_side_by_side(dt_ref, block, group)
-        query_rows = heads_one_above(q_ref, block, group)
-        upstream_rows = heads_one_above(d_ref, block, group)
-        nothing = jnp.zeros_like(query_rows)
-        both_rows = jnp.concatenate(
-            [
-                jnp.concatenate([query_rows, nothing], axis=1),
-                jnp.concatenate([nothing, upstream_rows], axis=1),
-            ],
-            axis=0,
-        )
-        logs = jnp.concatenate([log_ref[0, h : h + 1, cut] for h in range(group)], axis=1)
-        spread = jnp.concatenate([spread_ref[0, h : h + 1, cut] for h in range(group)], axis=1)
-
-        def step(keys_ref, keys_t_ref, values_ref, sums_ref, offset, number, acc):
+        heads = []
+        for j in range(together):
+            here = pl.ds(j * tall, tall)
+            query_rows = heads_one_above(q_ref, j, block, group)
+            upstream_rows = heads_one_above(d_ref, j, block, group)
+            nothing = jnp.zeros_like(query_rows)
+            both_rows = jnp.concatenate(
+                [
+                    jnp.concatenate([query_rows, nothing], axis=1),
+                    jnp.concatenate([nothing, upstream_rows], axis=1),
+                ],
+                axis=0,
+            )
+            heads.append(
+                (
+                    heads_side_by_side(qt_ref.at[here], block, group),
+                    heads_side_by_side(dt_ref.at[here], block, group),
+                    both_rows,
+                    jnp.concatenate([log_ref[j, h : h + 1, cut] for h in range(group)], axis=1),
+                    jnp.concatenate([spread_ref[j, h : h + 1, cut] for h in range(group)], axis=1),
+                )
+            )
+
+        def step(keys_ref, keys_t_ref, values_ref, sums_ref, offset, number, sums):
             start = pl.multiple_of(number * BLOCK, BLOCK)
             here = pl.ds(start, BLOCK)
-            scores = mm(keys_ref[0, here, :], query)
             mask = block_mask(lo, hi, start + offset, lanes)
-            probs = jnp.exp(jnp.where(mask, scores - logs, masked_value))
-            change = mm(values_ref[0, here, :], upstream)
-            scores_change = (probs * (change - spread)).astype(bf16)
-            sums_ref[here, :] += mm(
-                jnp.concatenate([scores_change, probs.astype(bf16)], axis=1), both_rows
-            )
-            return acc + mm(keys_t_ref[:, here], scores_change)
+            result = []
+            for j, (query, upstream, both_rows, logs, spread) in enumerate(heads):
+                scores = mm(keys_ref[j, here, :], query)
+                probs = jnp.exp(jnp.where(mask, scores - logs, masked_value))
+                change = mm(values_ref[j, here, :], upstream)
+                scores_change = (probs * (change - spread)).astype(bf16)
+                sums_ref[j, here, :] += mm(
+                    jnp.concatenate([scores_change, probs.astype(bf16)], axis=1), both_rows
+                )
+                keys_t = keys_t_ref[j * HEAD_DIM : (j + 1) * HEAD_DIM, here]
+                result.append(sums[j] + mm(keys_t, scores_change))
+            return tuple(result)
 
         first = first_ref[block]
-        acc = jnp.zeros((HEAD_DIM, lanes), f32)
+        sums = (jnp.zeros((HEAD_DIM, lanes), f32),) * together
         earlier = functools.partial(step, old_k_ref, old_kt_ref, old_v_ref, old_pair_ref, 0)
-        acc = lax.fori_loop(first, passed, earlier, acc)
+        sums = lax.fori_loop(first, passed, earlier, sums)
         own = functools.partial(step, k_ref, kt_ref, v_ref, pair_ref, before)
-        acc = lax.fori_loop(jnp.maximum(first - passed, 0), block + 1, own, acc)
-        for h in range(group):
-            dq_ref[h * HEAD_DIM : (h + 1) * HEAD_DIM, cut] = (
-                acc[:, h * BLOCK : (h + 1) * BLOCK] * score_scale
-            )
-    pair_t = pair_ref[...].T
-    dk_ref[...] = pair_t[:HEAD_DIM]
-    dv_ref[...] = pair_t[HEAD_DIM:]
-    pair_t = old_pair_ref[...].T
-    old_dk_ref[...] = pair_t[:HEAD_DIM].astype(bf16)
-    old_dv_ref[...] = pair_t[HEAD_DIM:].astype(bf16)
+        sums = lax.fori_loop(jnp.maximum(first - passed, 0), block + 1, own, sums)
+        for j in range(together):
+            for h in range(group):
+                high = j * tall + h * HEAD_DIM
+                dq_ref[high : high + HEAD_DIM, cut] = (
+                    sums[j][:, h * BLOCK : (h + 1) * BLOCK] * score_scale
+                )
+    for j in range(together):
+        side = slice(j * HEAD_DIM, (j + 1) * HEAD_DIM)
+        pair_t = pair_ref[j].T
+        dk_ref[side] = pair_t[:HEAD_DIM]
+        dv_ref[side] = pair_t[HEAD_DIM:]
+        pair_t = old_pair_ref[j].T
+        old_dk_ref[side] = pair_t[:HEAD_DIM].astype(bf16)
+        old_dv_ref[side] = pair_t[HEAD_DIM:].astype(bf16)
 
 
 def attend_back(
@@ -209,48 +238,49 @@
 ):
     pair_heads, before, _ = old_k.shape
     group, rows = q_rows.shape[1:3]
-    tall = group * HEAD_DIM
+    together = 2 if pair_heads % 2 == 0 else 1
+    tall = together * group * HEAD_DIM
+    split = together * HEAD_DIM
     by_head = lambda h, s: (h, 0, 0)
     flat = lambda h, s: (h, 0)
-    split = pair_heads * HEAD_DIM
     return pl.pallas_call(
         functools.partial(attend_back_kernel, group),
         grid_spec=pltpu.PrefetchScalarGridSpec(
             num_scalar_prefetch=1,
-            grid=(pair_heads,),
+            grid=(pair_heads // together,),
             in_specs=[
                 pl.BlockSpec((1, rows), lambda h, s: (0, 0)),
-                pl.BlockSpec((1, group, rows), by_head),
-                pl.BlockSpec((1, group, rows), by_head),
+                pl.BlockSpec((together, group, rows), by_head),
+                pl.BlockSpec((together, group, rows), by_head),
                 pl.BlockSpec((tall, rows), flat),
                 pl.BlockSpec((tall, rows), flat),
-                pl.BlockSpec((1, group, rows, HEAD_DIM), lambda h, s: (h, 0, 0, 0)),
-                pl.BlockSpec((1, group, rows, HEAD_DIM), lambda h, s: (h, 0, 0, 0)),
-                pl.BlockSpec((1, rows, HEAD_DIM), by_head),
-                pl.BlockSpec((HEAD_DIM, rows), flat),
-                pl.BlockSpec((1, rows, HEAD_DIM), by_head),
-                pl.BlockSpec((1, before, HEAD_DIM), by_head),
-                pl.BlockSpec((HEAD_DIM, before), flat),
-                pl.BlockSpec((1, before, HEAD_DIM), by_head),
+                pl.BlockSpec((together, group, rows, HEAD_DIM), lambda h, s: (h, 0, 0, 0)),
+                pl.BlockSpec((together, group, rows, HEAD_DIM), lambda h, s: (h, 0, 0, 0)),
+                pl.BlockSpec((together, rows, HEAD_DIM), by_head),
+                pl.BlockSpec((split, rows), flat),
+                pl.BlockSpec((together, rows, HEAD_DIM), by_head),
+                pl.BlockSpec((together, before, HEAD_DIM), by_head),
+                pl.BlockSpec((split, before), flat),
+                pl.BlockSpec((together, before, HEAD_DIM), by_head),
             ],
             out_specs=[
                 pl.BlockSpec((tall, rows), flat),
-                pl.BlockSpec((HEAD_DIM, rows), flat),
-                pl.BlockSpec((HEAD_DIM, rows), flat),
-                pl.BlockSpec((HEAD_DIM, before), flat),
-                pl.BlockSpec((HEAD_DIM, before), flat),
+                pl.BlockSpec((split, rows), flat),
+                pl.BlockSpec((split, rows), flat),
+                pl.BlockSpec((split, before), flat),
+                pl.BlockSpec((split, before), flat),
             ],
             scratch_shapes=[
-                pltpu.VMEM((rows, 2 * HEAD_DIM), f32),
-                pltpu.VMEM((before, 2 * HEAD_DIM), f32),
+                pltpu.VMEM((together, rows, 2 * HEAD_DIM), f32),
+                pltpu.VMEM((together, before, 2 * HEAD_DIM), f32),
             ],
         ),
         out_shape=[
-            jax.ShapeDtypeStruct((pair_heads * tall, rows), f32),
-            jax.ShapeDtypeStruct((split, rows), f32),
-            jax.ShapeDtypeStruct((split, rows), f32),
-            jax.ShapeDtypeStruct((split, before), bf16),
-            jax.ShapeDtypeStruct((split, before), bf16),
+            jax.ShapeDtypeStruct((pair_heads * group * HEAD_DIM, rows), f32),
+            jax.ShapeDtypeStruct((pair_heads * HEAD_DIM, rows), f32),
+            jax.ShapeDtypeStruct((pair_heads * HEAD_DIM, rows), f32),
+            jax.ShapeDtypeStruct((pair_heads * HEAD_DIM, before), bf16),
+            jax.ShapeDtypeStruct((pair_heads * HEAD_DIM, before), bf16),
         ],
         compiler_params=pltpu.CompilerParams(vmem_limit_bytes=vmem_bytes),
         cost_estimate=pl.CostEstimate(
@@ -518,7 +548,7 @@
             jax.ShapeDtypeStruct((high, width), bf16),
             jax.ShapeDtypeStruct((high, width), bf16),
         ],
-        compiler_params=pltpu.CompilerParams(vmem_limit_bytes=expert_vmem_bytes),
+        compiler_params=pltpu.CompilerParams(vmem_limit_bytes=vmem_bytes),
         cost_estimate=pl.CostEstimate(
             flops=4 * rows * width * (tall + 2 * split),
             bytes_accessed=24 * 1024 * 1024,
@@ -532,11 +562,27 @@
 
 
 def expert_kernel(
-    adds, ids_ref, gates_ref, xt_ref, x_ref, ct_ref, c_ref, up_ref, down_ref, *refs
+    adds, ids_ref, gates_ref, xt_hbm, ct_hbm, x_hbm, c_hbm, up_ref, down_ref, *refs
 ):
     if adds:
         more_ref, *refs = refs
-    _, _, _, grad_ref, up_grad_ref, act_ref, gate_grad_ref = refs
+    _, _, _, grad_ref, up_grad_ref, act_ref, gate_grad_ref, *refs = refs
+    xt_ref, ct_ref, x_ref, c_ref, arrived = refs
+    copies = [
+        pltpu.make_async_copy(source, target, arrived.at[place])
+        for place, (source, target) in enumerate(
+            [(xt_hbm, xt_ref), (ct_hbm, ct_ref), (x_hbm, x_ref), (c_hbm, c_ref)]
+        )
+    ]
+    first_step = pl.program_id(0) == 0
+
+    @pl.when(first_step)
+    def begin():
+        for copy in copies:
+            copy.start()
+        copies[0].wait()
+        copies[1].wait()
+
     rows = x_ref.shape[0]
     chunk = min(BLOCK, rows)
     for part in range(rows // chunk):
@@ -552,6 +598,8 @@
         gate_grad_ref[0, 0, :, cut] = residual_scale * jnp.sum(
             active * active_grad, axis=0, keepdims=True
         )
+        for place in range(1, gate_grad_ref.shape[0]):
+            gate_grad_ref[place, 0, :, cut] = jnp.zeros((1, chunk), f32)
         active_grad = active_grad * weight
         act_ref[0, :, cut] = (active * weight).astype(bf16)
         up_grad_ref[0, 0, :, cut] = (
@@ -564,17 +612,22 @@
             total = total + more_ref[0, place].astype(f32)
         grad_ref[0, place] = total.astype(bf16)
 
+    @pl.when(first_step)
+    def complete():
+        copies[2].wait()
+        copies[3].wait()
+
     x = x_ref[...]
     put(0, mm(up_grad_ref[0, 0], x))
     put(1, mm(up_grad_ref[0, 1], x))
     put(2, mm(act_ref[0], c_ref[...]))
 
 
-def expert_step(ids, half, gates, xt, x, ct, c, w_up, w_down, more, old):
+def expert_step(ids, half, halves, gates, xt, x, ct, c, w_up, w_down, more, old):
     count = ids.shape[0]
     rows, width = x.shape
-    units = w_down.shape[1] // 2
-    whole = lambda shape: pl.BlockSpec(shape, lambda e, s: (0,) * len(shape))
+    units = w_down.shape[1] // 2 * halves
+    any_place = pl.BlockSpec(memory_space=pl.ANY)
     fresh = old is None
     adds = more is not None
     each = pl.BlockSpec((1, 3, units, width), lambda e, s: (e, 0, 0, 0))
@@ -587,39 +640,46 @@
             grid=(count,),
             in_specs=[
                 pl.BlockSpec((1, 1, rows), lambda e, s: (s[e], 0, 0)),
-                whole((width, rows)),
-                whole((rows, width)),
-                whole((width, rows)),
-                whole((rows, width)),
+                any_place,
+                any_place,
+                any_place,
+                any_place,
                 pl.BlockSpec((1, 2, units, width), lambda e, s: (s[e], 0, half, 0)),
                 pl.BlockSpec((1, units, width), lambda e, s: (s[e], half, 0)),
                 *([each] if adds else []),
-                pl.BlockSpec(memory_space=pl.ANY),
-                pl.BlockSpec(memory_space=pl.ANY),
-                pl.BlockSpec(memory_space=pl.ANY),
+                any_place,
+                any_place,
+                any_place,
             ],
             out_specs=[
                 each,
                 pl.BlockSpec((1, 2, units, rows), lambda e, s: (s[e], 0, half, 0)),
                 pl.BlockSpec((1, units, rows), lambda e, s: (s[e], half, 0)),
-                pl.BlockSpec((1, 1, 1, rows), lambda e, s: (half, s[e], 0, 0)),
+                pl.BlockSpec((halves, 1, 1, rows), lambda e, s: (half, s[e], 0, 0)),
+            ],
+            scratch_shapes=[
+                pltpu.VMEM((width, rows), bf16),
+                pltpu.VMEM((width, rows), bf16),
+                pltpu.VMEM((rows, width), bf16),
+                pltpu.VMEM((rows, width), bf16),
+                pltpu.SemaphoreType.DMA((4,)),
             ],
         ),
         out_shape=[
             jax.ShapeDtypeStruct((count, 3, units, width), bf16),
-            jax.ShapeDtypeStruct((EXPERTS, 2, 2 * units, rows), bf16),
-            jax.ShapeDtypeStruct((EXPERTS, 2 * units, rows), bf16),
+            jax.ShapeDtypeStruct((EXPERTS, 2, w_down.shape[1], rows), bf16),
+            jax.ShapeDtypeStruct((EXPERTS, w_down.shape[1], rows), bf16),
             jax.ShapeDtypeStruct((2, EXPERTS, 1, rows), f32),
         ],
         input_output_aliases={} if fresh else {8 + adds: 1, 9 + adds: 2, 10 + adds: 3},
-        compiler_params=pltpu.CompilerParams(vmem_limit_bytes=expert_vmem_bytes),
+        compiler_params=pltpu.CompilerParams(vmem_limit_bytes=vmem_bytes),
         cost_estimate=pl.CostEstimate(
             flops=count * 12 * rows * width * units,
             bytes_accessed=count * units * width * 12 + 8 * rows * width,
             transcendentals=count * units * rows,
         ),
         name="experts",
-    )(ids, gates, xt, x, ct, c, w_up, w_down, *([more] if adds else []), *old)
+    )(ids, gates, xt, ct, x, c, w_up, w_down, *([more] if adds else []), *old)
 
 
 def from_other_half(shard):
@@ -765,12 +825,12 @@
     upstream_t = out_cotangent.T
     swap_cores = [(i, i ^ 1) for i in range(peers)]
     shares, arrived, old = [], [], None
-    pieces = [(number, half) for number in range(chunks) for half in range(2)]
+    pieces = [(number, half, 1) for number in range(chunks) for half in range(2)]
 
     def run_experts(piece, side, more):
         ids = chunk_experts(device, peers, piece[0])[side]
         return expert_step(
-            ids, piece[1], gates[:, None, :], normed_t, normed_mixture, upstream_t, out_cotangent,
+            ids, piece[1], piece[2], gates[:, None, :], normed_t, normed_mixture, upstream_t, out_cotangent,
             expert_gate_up, expert_down, more, old,
         )
 
@@ -842,25 +902,27 @@
     )
     swapped = [both_parts(part) for part in jnp.split(input_part, 2, axis=0)]
     *shares[-2:], keep = lax.optimization_barrier((*shares[-2:], keep))
-    swapped = [list(pair) for pair in swapped]
-    gradients, swapped[0][1], swapped[1][1] = summed_over_tokens(
-        send, keep, swapped[0][1], swapped[1][1]
+    mixed = (hidden + (mixture_own.astype(f32) + mixture_other.astype(f32))).astype(bf16)
+    shares = [
+        jnp.concatenate(shares[start : start + 2], axis=2) for start in range(0, len(shares), 2)
+    ]
+    experts_gradient = jnp.concatenate(shares, axis=0).astype(f32)
+    up_gradient, down_gradient = experts_gradient[:, :2], experts_gradient[:, 2]
+    (own_one, other_one), (own_two, other_two) = swapped
+    gradients, (other_one, mixed, up_gradient, down_gradient), other_two = summed_over_tokens(
+        send, keep, (other_one, mixed, up_gradient, down_gradient), other_two
     )
     input_sum = jnp.concatenate(
-        [own.astype(f32) + other.astype(f32) for own, other in swapped], axis=0
-    )
-    mixed = (hidden + (mixture_own.astype(f32) + mixture_other.astype(f32))).astype(bf16)
+        [own_one.astype(f32) + other_one.astype(f32), own_two.astype(f32) + other_two.astype(f32)],
+        axis=0,
+    )
     tokens_gradient = hidden_gradient + input_sum
     w_q, w_k, w_v, w_o = jnp.split(gradients[: ends[3]].astype(f32), ends[:3], axis=0)
     small = summed_parts(gradients[ends[3] :])
     router, gains = small[:EXPERTS], small[EXPERTS:]
-    halves = [
-        jnp.concatenate(shares[start : start + 2], axis=2) for start in range(0, len(shares), 2)
-    ]
-    experts_gradient = jnp.concatenate(halves, axis=0).astype(f32)
     return (
         mixed, tokens_gradient.astype(bf16), gains[1], w_q.T, w_k, w_v, w_o, gains[0], router.T,
-        experts_gradient[:, :2], experts_gradient[:, 2],
+        up_gradient, down_gradient,
     )
 
 

time: 577 us -> 566 us (0.981); the launches traced: 573 us -> 555 us
  local copies, waits for them, and re-layouts: 84.5 us -> 26.2 us
  Pallas kernels: 229 us -> 275 us
  waiting for transfers between devices: 99.4 us -> 88.3 us
    unnamed x184 -> x58, local copies, waits for them, and re-layouts: 72.2 us -> 8.48 us
    pallas_call x8, Pallas kernels: 160 us -> 190 us  [expert_step(): pl.pallas_call(functools.partial(expert_kernel, adds), grid_spec=pltpu.Pr...]
    ppermute x1, waiting for transfers between devices: 17.6 us -> 8.59 us  [on_device(): more_dk = lax.ppermute(old_dk, 'dp', to_previous)]
    ppermute x9, waiting for transfers between devices: 60 us -> 53 us  [from_other_half(): return lax.ppermute(shard, 'tensor', [(0, 1), (1, 0)])]
  transfers between devices with their start and end apart: 25 -> 25, of which waited for: 10 -> 11; matrix products, arithmetic and copies ran while one was open for 22% -> 23% of each run, Pallas kernels for 32% -> 40%
where the time goes in v3:
time: 566 us; the launch traced here: 555 us
  Pallas kernels  275 us (49%)
  waiting for transfers between devices  88.3 us (16%)
  matrix products  80.2 us (14%)
  other arithmetic  36.3 us (6%)
  starting transfers between devices  33.3 us (6%)
  local copies, waits for them, and re-layouts  26.2 us (5%)
  between operations  15.1 us (3%)
    pallas_call x8, Pallas kernels, expert_step(): pl.pallas_call(functools.partial(expert_kernel, adds), grid_spec=pltpu.Pr...  190 us
    dot_general x5, matrix products, dot(): lax.dot_general(left, right, (((left_dim,), (right_dim,)), ((), ())), pre...  79.1 us
    ppermute x9, waiting for transfers between devices, from_other_half(): return lax.ppermute(shard, 'tensor', [(0, 1), (1, 0)])  53 us
    pallas_call x1, Pallas kernels, attend_back(): pl.pallas_call(functools.partial(attend_back_kernel, group), grid_spec=pl...  23.5 us
    pallas_call x2, Pallas kernels, attend(): pl.pallas_call(functools.partial(attend_kernel, group), grid_spec=pltpu.P...  20.2 us
    pallas_call x1, Pallas kernels, leave_back(): pl.pallas_call(leave_back_kernel, grid_spec=pltpu.PrefetchScalarGridSpec(...  13.7 us
    ppermute x9, starting transfers between devices, from_other_half(): return lax.ppermute(shard, 'tensor', [(0, 1), (1, 0)])  13.1 us
    ppermute x4, starting transfers between devices, on_device(): arrived.append(lax.ppermute(send, 'dp', swap_cores))  12.6 us
  transfers between devices with their start and end apart: 25, of which 11 were waited for; matrix products, arithmetic and copies ran while one was open for 23% of the time, Pallas kernels for 40%

profile of v3, /device:TPU:0, one launch (start us, length us, event | category | flops | bytes accessed | tf_op | source)
XLA Modules:
  0.0 554.8 jit_solution(4421498320936955121)
XLA Ops:
  7.2 3.0 collective-permute-start.4
  10.3 1.3 broadcast_in_dim.19.gain_ref
  11.6 1.2 multiply_sine_fusion
  12.8 8.4 %project.1 = (bf16[1024,1024]{1,0:T(8,128)(2,1)}, bf16[512,1024]{1,0:T(8,128)(2,1)}, bf16[8,1024,64]{2,1,0:T(8,128)(2,1)}, bf16[256,1024]{1,0:T(8,128)(2,1)}, bf...) custom-call(bf16[1024,1024]{1,0:T(8,128)(2,1)} %x_ref.5, ...), custom_call_target="tpu_custom_call" | custom-call | flops 2147483648 | bytes 12582912 | tf_op jit(solution)/shard_map/project/pallas_call | solution.py:336
  21.2 2.2 collective-permute-start
  23.5 2.1 collective-permute-start.1
  28.1 2.6 copy.63
  31.8 2.4 copy.62
  34.1 10.1 %attend.3 = (bf16[256,1024]{1,0:T(8,128)(2,1)}, f32[2,2,1024]{2,1,0:T(2,128)}) custom-call(s32[4]{0:T(128)} %and_select_fusion.first_ref, s32[1,1024]{1,0:T(1,128)} %bitcast.76, bf16[512,1024]{1,0:T(8,128)(2,1)} %get-tuple-element.93.qt_ref, bf16[4,1024,64]{2,1,0:T(8,128)(2,1)} %get-tuple-element.94.k_ref, bf16[256,1024]{1,0:T(8,128)(2,1)} %get-tuple-element.95.vt_ref, ...), custom_call_target="tpu_custom_call" | custom-call | flops 4294967296 | bytes 8388608 | tf_op jit(solution)/shard_map/attend/pallas_call | solution.py:127
  44.6 10.2 %attend.2 = (bf16[256,1024]{1,0:T(8,128)(2,1)}, f32[2,2,1024]{2,1,0:T(2,128)}) custom-call(s32[4]{0:T(128)} %and_select_fusion.first_ref, s32[1,1024]{1,0:T(1,128)} %bitcast.77, bf16[512,1024]{1,0:T(8,128)(2,1)} %get-tuple-element.93.qt_ref, bf16[4,1024,64]{2,1,0:T(8,128)(2,1)} %get-tuple-element.94.k_ref, bf16[256,1024]{1,0:T(8,128)(2,1)} %get-tuple-element.95.vt_ref, ...), custom_call_target="tpu_custom_call" | custom-call | flops 4294967296 | bytes 8388608 | tf_op jit(solution)/shard_map/attend/pallas_call | solution.py:127
  54.7 1.7 collective-permute-start.2
  58.5 6.3 %collective-permute-done.2.refs_2_ = bf16[256,1024]{1,0:T(8,128)(2,1)S(1)} collective-permute-done((bf16[256,1024]{1,0:T(8,128)(2,1)}, bf16[256,1024]{1,0:T(8,128)(2,1)S(1)}, u32[]{:S(2)}, u32[]{:S(2)}) %collective-permute-start.2) | collective-permute-done | bytes 524320 | tf_op jit(solution)/shard_map/ppermute | solution.py:686
  65.7 8.7 %enter_mixture.1 = (f32[1024,1024]{1,0:T(8,128)}, bf16[1024,1024]{1,0:T(8,128)(2,1)}, bf16[1024,1024]{1,0:T(8,128)(2,1)}, f32[32,1024]{1,0:T(8,128)}) custom-call(bf16[1024,1024]{1,0:T(8,128)(2,1)} %x_ref.5, bf16[1,1024]{1,0:T(2,128)(2,1)} %broadcast_in_dim.16.gain_ref, bf16[32,1024]{1,0:T(8,128)(2,1)} %bitcast.63, s32[8,1024]{1,0:T(8,128)} %bitcast.74, ...), custom_call_target="tpu_custom_call" | custom-call | flops 2147483648 | bytes 16777216 | tf_op jit(solution)/shard_map/enter_mixture/pallas_call | solution.py:398
  74.4 1.6 broadcast_in_dim.20.gates_ref
  76.6 23.5 %experts.8 = (bf16[8,3,128,1024]{3,2,1,0:T(8,128)(2,1)}, bf16[32,2,256,1024]{3,2,1,0:T(8,128)(2,1)}, bf16[32,256,1024]{2,1,0:T(8,128)(2,1)}, f32[2,32,1,1024]{3,2,1,0:T(1,128)}) custom-call(s32[8]{0:T(128)} %get-tuple-element.213.ids_ref, f32[32,1,1024]{2,1,0:T(1,128)} %broadcast_in_dim.20.gates_ref, bf16[1024,1024]{1,0:T(8,128)(2,1)} %get-tuple-element.100.xt_hbm, ...), custom_call_target="tpu_custom_call" | custom-call | flops 12884901888 | bytes 20971520 | tf_op jit(solution)/shard_map/experts/pallas_call | solution.py:636
  100.1 11.8 %collective-permute-start.5 = (bf16[8,3,128,1024]{3,2,1,0:T(8,128)(2,1)}, bf16[8,3,128,1024]{3,2,1,0:T(8,128)(2,1)}, u32[]{:S(2)}, u32[]{:S(2)}) collective-permute-start(bf16[8,3,128,1024]{3,2,1,0:T(8,128)(2,1)} %get-tuple-element.102), channel_id=1, source_target_pairs={{0,2},{2,0},{4,6},{6,4},{8,10},{10,8},{12,14},{14,12},{16,18},{18,... | collective-permute-start | bytes 18874376 | tf_op jit(solution)/shard_map/ppermute | solution.py:840
  111.9 23.4 %experts.9 = (bf16[8,3,128,1024]{3,2,1,0:T(8,128)(2,1)}, bf16[32,2,256,1024]{3,2,1,0:T(8,128)(2,1)}, bf16[32,256,1024]{2,1,0:T(8,128)(2,1)}, f32[2,32,1,1024]{3,2,1,0:T(1,128)}) custom-call(s32[8]{0:T(128)} %get-tuple-element.213.ids_ref, f32[32,1,1024]{2,1,0:T(1,128)} %broadcast_in_dim.20.gates_ref, ...), custom_call_target="tpu_custom_call", output_to_operand_aliasing={{1}: (8, {}), {2}: (9, {}), {3}: (10, {})} | custom-call | flops 12884901888 | bytes 20971520 | tf_op jit(solution)/shard_map/experts/pallas_call | solution.py:636
  135.4 24.0 %experts.10 = (bf16[8,3,128,1024]{3,2,1,0:T(8,128)(2,1)}, bf16[32,2,256,1024]{3,2,1,0:T(8,128)(2,1)}, bf16[32,256,1024]{2,1,0:T(8,128)(2,1)}, f32[2,32,1,1024]{3,2,1,0:T(1,128)}) custom-call(s32[8]{0:T(128)} %get-tuple-element.238.ids_ref, f32[32,1,1024]{2,1,0:T(1,128)} %broadcast_in_dim.20.gates_ref, ...), custom_call_target="tpu_custom_call", output_to_operand_aliasing={{1}: (9, {}), {2}: (10, {}), {3}: (11, {})} | custom-call | flops 12884901888 | bytes 20971520 | tf_op jit(solution)/shard_map/experts/pallas_call | solution.py:636
  159.7 23.5 %experts.11 = (bf16[8,3,128,1024]{3,2,1,0:T(8,128)(2,1)}, bf16[32,2,256,1024]{3,2,1,0:T(8,128)(2,1)}, bf16[32,256,1024]{2,1,0:T(8,128)(2,1)}, f32[2,32,1,1024]{3,2,1,0:T(1,128)}) custom-call(s32[8]{0:T(128)} %get-tuple-element.212.ids_ref, f32[32,1,1024]{2,1,0:T(1,128)} %broadcast_in_dim.20.gates_ref, ...), custom_call_target="tpu_custom_call", output_to_operand_aliasing={{1}: (8, {}), {2}: (9, {}), {3}: (10, {})} | custom-call | flops 12884901888 | bytes 20971520 | tf_op jit(solution)/shard_map/experts/pallas_call | solution.py:636
  183.2 23.9 %experts.12 = (bf16[8,3,128,1024]{3,2,1,0:T(8,128)(2,1)}, bf16[32,2,256,1024]{3,2,1,0:T(8,128)(2,1)}, bf16[32,256,1024]{2,1,0:T(8,128)(2,1)}, f32[2,32,1,1024]{3,2,1,0:T(1,128)}) custom-call(s32[8]{0:T(128)} %get-tuple-element.238.ids_ref, f32[32,1,1024]{2,1,0:T(1,128)} %broadcast_in_dim.20.gates_ref, ...), custom_call_target="tpu_custom_call", output_to_operand_aliasing={{1}: (9, {}), {2}: (10, {}), {3}: (11, {})} | custom-call | flops 12884901888 | bytes 20971520 | tf_op jit(solution)/shard_map/experts/pallas_call | solution.py:636
  207.7 23.5 %experts.13 = (bf16[8,3,128,1024]{3,2,1,0:T(8,128)(2,1)}, bf16[32,2,256,1024]{3,2,1,0:T(8,128)(2,1)}, bf16[32,256,1024]{2,1,0:T(8,128)(2,1)}, f32[2,32,1,1024]{3,2,1,0:T(1,128)}) custom-call(s32[8]{0:T(128)} %get-tuple-element.212.ids_ref, f32[32,1,1024]{2,1,0:T(1,128)} %broadcast_in_dim.20.gates_ref, ...), custom_call_target="tpu_custom_call", output_to_operand_aliasing={{1}: (8, {}), {2}: (9, {}), {3}: (10, {})} | custom-call | flops 12884901888 | bytes 20971520 | tf_op jit(solution)/shard_map/experts/pallas_call | solution.py:636
  231.2 23.9 %experts.14 = (bf16[8,3,128,1024]{3,2,1,0:T(8,128)(2,1)}, bf16[32,2,256,1024]{3,2,1,0:T(8,128)(2,1)}, bf16[32,256,1024]{2,1,0:T(8,128)(2,1)}, f32[2,32,1,1024]{3,2,1,0:T(1,128)}) custom-call(s32[8]{0:T(128)} %get-tuple-element.237.ids_ref, f32[32,1,1024]{2,1,0:T(1,128)} %broadcast_in_dim.20.gates_ref, ...), custom_call_target="tpu_custom_call", output_to_operand_aliasing={{1}: (9, {}), {2}: (10, {}), {3}: (11, {})} | custom-call | flops 12884901888 | bytes 20971520 | tf_op jit(solution)/shard_map/experts/pallas_call | solution.py:636
  255.8 2.4 copy.65
  259.8 2.6 multiply_reduce_fusion
  262.4 3.3 collective-permute-done.8.refs_0_
  265.8 24.4 %experts.15 = (bf16[8,3,128,1024]{3,2,1,0:T(8,128)(2,1)}, bf16[32,2,256,1024]{3,2,1,0:T(8,128)(2,1)}, bf16[32,256,1024]{2,1,0:T(8,128)(2,1)}, f32[2,32,1,1024]{3,2,1,0:T(1,128)}) custom-call(s32[8]{0:T(128)} %get-tuple-element.237.ids_ref, f32[32,1,1024]{2,1,0:T(1,128)} %broadcast_in_dim.20.gates_ref, ...), custom_call_target="tpu_custom_call", output_to_operand_aliasing={{1}: (9, {}), {2}: (10, {}), {3}: (11, {})} | custom-call | flops 12884901888 | bytes 20971520 | tf_op jit(solution)/shard_map/experts/pallas_call | solution.py:636
  291.4 1.8 fusion.13
  293.2 28.1 %multiply_reduce_fusion.2 = (f32[1024]{0:T(1024)S(1)}, f32[512]{0:T(512)S(1)}, f32[512,1024]{1,0:T(8,128)S(1)}) fusion(f32[1024,1024]{1,0:T(8,128)} %get-tuple-element.133, f32[512]{0:T(512)S(1)} %get-tuple-element.236, f32[1024]{0:T(1024)S(1)} %convert_element_type.72, f32[512,1024]{1,0:T(8,128)} %fusion.13, bf16[16384,1024]{1,0:T(8,128)(2,1)} %bitcast.47, ...), kind=kOutput, calls=%fused_computation.21 | convolution fusion | flops 17183539200 | bytes 56635392 | tf_op jit(solution)/shard_map/dot_general | solution.py:26
  321.4 2.0 subtract_convert_fusion.1
  323.5 1.7 collective-permute-start.9
  325.1 24.9 %fusion.2 = f32[512,1024]{1,0:T(8,128)S(1)} fusion(bf16[16384,1024]{1,0:T(8,128)(2,1)} %bitcast.48, bf16[16384,1024]{1,0:T(8,128)(2,1)} %bitcast.50), kind=kOutput, calls=%fused_computation.2 | convolution fusion | flops 17179869184 | bytes 52428800 | tf_op jit(solution)/shard_map/dot_general | solution.py:26
  352.1 23.5 %bitcast_convert_fusion = bf16[1024,1024]{1,0:T(8,128)(2,1)} fusion(bf16[32,256,1024]{2,1,0:T(8,128)(2,1)} %get-tuple-element.140, bf16[32,256,1024]{2,1,0:T(8,128)(2,1)} %down_ref.15), kind=kOutput, calls=%fused_computation.7 | convolution fusion | flops 17180917760 | bytes 35651584 | tf_op jit(solution)/shard_map/dot_general | solution.py:26
  375.6 1.5 pad_maximum_fusion.1.own_ref
  377.1 1.6 pad_maximum_fusion.2.other_ref
  378.7 1.2 collective-permute-start.11
  380.0 10.6 %enter_back.1 = (f32[1024,1024]{1,0:T(8,128)}, bf16[512,1024]{1,0:T(8,128)(2,1)}, bf16[8,1024,64]{2,1,0:T(8,128)(2,1)}, f32[8,1024]{1,0:T(8,128)}, f32[512,1024]{1,0:T(8,128)}) custom-call(bf16[1024,1024]{1,0:T(8,128)(2,1)} %c_ref.1, bf16[1024,1024]{1,0:T(8,128)(2,1)} %pad_maximum_fusion.1.own_ref, bf16[1024,1024]{1,0:T(8,128)(2,1)} %pad_maximum_fusion.2.other_ref, ...), custom_call_target="tpu_custom_call" | custom-call | flops 2147483648 | bytes 20971520 | tf_op jit(solution)/shard_map/enter_back/pallas_call | solution.py:453
  390.6 1.4 reshape.131.spread_ref
  392.0 23.5 %attend_back.1 = (f32[512,1024]{1,0:T(8,128)}, f32[256,1024]{1,0:T(8,128)}, f32[256,1024]{1,0:T(8,128)}, bf16[256,1024]{1,0:T(8,128)(2,1)}, bf16[256,1024]{1,0:T(8,128)(2,1)}) custom-call(s32[4]{0:T(128)} %and_select_fusion.first_ref, s32[1,1024]{1,0:T(1,128)} %bitcast.78, f32[4,2,1024]{2,1,0:T(2,128)} %pad_maximum_fusion.4.log_ref, ...), custom_call_target="tpu_custom_call" | custom-call | flops 21474836480 | bytes 16777216 | tf_op jit(solution)/shard_map/attend_back/pallas_call | solution.py:246
  415.5 1.3 collective-permute-start.12
  416.8 1.3 collective-permute-start.13
  418.7 1.1 fusion.35.router_grad_ref
  419.8 6.1 %collective-permute-done.11 = bf16[1024,1024]{1,0:T(8,128)(2,1)} collective-permute-done((bf16[1024,1024]{1,0:T(8,128)(2,1)}, bf16[1024,1024]{1,0:T(8,128)(2,1)}, u32[]{:S(2)}, u32[]{:S(2)}) %collective-permute-start.11) | collective-permute-done | bytes 2097184 | tf_op jit(solution)/shard_map/ppermute | solution.py:686
  425.9 8.6 %collective-permute-done.12.more_dk_ref = bf16[256,1024]{1,0:T(8,128)(2,1)S(1)} collective-permute-done((bf16[256,1024]{1,0:T(8,128)(2,1)}, bf16[256,1024]{1,0:T(8,128)(2,1)S(1)}, u32[]{:S(2)}, u32[]{:S(2)}) %collective-permute-start.12) | collective-permute-done | bytes 524320 | tf_op jit(solution)/shard_map/ppermute | solution.py:890
  434.5 1.3 collective-permute-done.13.more_dv_ref
  436.6 13.7 %leave_back.1 = (bf16[1024,1024]{1,0:T(8,128)(2,1)}, bf16[896,1024]{1,0:T(8,128)(2,1)}, bf16[896,1024]{1,0:T(8,128)(2,1)}) custom-call(s32[1]{0:T(128)} %bitcast.6.core_ref, bf16[1024,1024]{1,0:T(8,128)(2,1)} %x_ref.5, bf16[1,1024]{1,0:T(2,128)(2,1)} %broadcast_in_dim.19.gain_ref, f32[32,1024]{1,0:T(8,128)} %get-tuple-element.234.cos_ref, ...), custom_call_target="tpu_custom_call" | custom-call | flops 4294967296 | bytes 25165824 | tf_op jit(solution)/shard_map/leave_back/pallas_call | solution.py:532
  450.8 3.8 collective-permute-done.14
  454.5 4.2 add_convert_fusion.1
  459.1 1.2 collective-permute-start.15
  461.1 4.8 add_convert_fusion
  466.8 2.3 slice.86
  469.1 1.6 convert_bitcast_fusion
  470.7 14.0 %collective-permute-done.15 = bf16[512,1024]{1,0:T(8,128)(2,1)} collective-permute-done((bf16[512,1024]{1,0:T(8,128)(2,1)S(1)}, bf16[512,1024]{1,0:T(8,128)(2,1)}, u32[]{:S(2)}, u32[]{:S(2)}) %collective-permute-start.15) | collective-permute-done | bytes 1048608 | tf_op jit(solution)/shard_map/ppermute | solution.py:686
  484.7 7.1 %reduce-scatter.14.cloned.1.call-done = bf16[112,1024]{1,0:T(8,128)(2,1)} async-done(((bf16[896,1024]{1,0:T(8,128)(2,1)}), bf16[112,1024]{1,0:T(8,128)(2,1)}) %reduce-scatter.14.cloned.1.call-update) | async-done | bytes 229392 | tf_op jit(solution)/shard_map/reduce_scatter | solution.py:741
  491.8 1.5 collective-permute-start.16
  493.3 20.4 %collective-permute-done.16 = bf16[512,1024]{1,0:T(8,128)(2,1)} collective-permute-done((bf16[512,1024]{1,0:T(8,128)(2,1)S(1)}, bf16[512,1024]{1,0:T(8,128)(2,1)}, u32[]{:S(2)}, u32[]{:S(2)}) %collective-permute-start.16) | collective-permute-done | bytes 1048608 | tf_op jit(solution)/shard_map/ppermute | solution.py:686
  513.8 11.1 %all-gather.2.cloned.1.call-done = bf16[896,1024]{1,0:T(8,128)(2,1)} async-done(((bf16[112,1024]{1,0:T(8,128)(2,1)}), bf16[896,1024]{1,0:T(8,128)(2,1)}) %all-gather.2.cloned.1.call-update) | async-done | bytes 1835024 | tf_op jit(solution)/shard_map/all_gather | solution.py:743
  524.8 2.6 convert_add_fusion.1
  527.7 2.1 fusion.4
  530.0 1.7 maximum_convert_fusion.2
  531.7 1.5 collective-permute-start.18
  534.0 1.5 slice_bitcast_fusion
  535.5 2.9 copy.66
  538.3 1.6 maximum_convert_fusion.1
  539.9 6.1 %collective-permute-done.18 = bf16[256,1024]{1,0:T(8,128)(2,1)S(1)} collective-permute-done((bf16[256,1024]{1,0:T(8,128)(2,1)S(1)}, bf16[256,1024]{1,0:T(8,128)(2,1)S(1)}, u32[]{:S(2)}, u32[]{:S(2)}) %collective-permute-start.18) | collective-permute-done | bytes 524320 | tf_op jit(solution)/shard_map/ppermute | solution.py:686
  (123 shorter events, 20.3 us)
Async XLA Ops:
  7.2 418.7 %reduce-scatter.10.cloned.1.call-start = ((), (), s32[]{:S(2)}) async-start(), calls=%async_computation.7 | async-start | bytes 7077888 | tf_op jit(solution)/shard_map/reduce_scatter | solution.py:731
  7.2 50.3 %collective-permute-start.4 = (bf16[512,1024]{1,0:T(8,128)(2,1)}, bf16[512,1024]{1,0:T(8,128)(2,1)S(1)}, u32[]{:S(2)}, u32[]{:S(2)}) collective-permute-start(bf16[512,1024]{1,0:T(8,128)(2,1)} %wo_ref.1), channel_id=1, source_target_pairs={{0,1},{1,0},{2,3},{3,2},{4,5},{5,4},{6,7},{7,6},{8,9},{9,8},{10,11... | collective-permute-start | bytes 3145736 | tf_op jit(solution)/shard_map/ppermute | solution.py:686
  12.8 14.6 %copy-start.19 = (bf16[1024]{0:T(1024)(128)(2,1)S(1)}, bf16[1024]{0:T(1024)(128)(2,1)}, u32[]{:S(2)}) copy-start(bf16[1024]{0:T(1024)(128)(2,1)} %param.29) | copy-start | bytes 6148
  12.8 15.3 %copy-start = (bf16[1024,1024]{1,0:T(8,128)(2,1)S(1)}, bf16[1024,1024]{1,0:T(8,128)(2,1)}, u32[]{:S(2)}) copy-start(bf16[1024,1024]{1,0:T(8,128)(2,1)} %c_ref.1) | copy-start | bytes 6291460
  21.2 10.5 %collective-permute-start = (bf16[256,1024]{1,0:T(8,128)(2,1)}, bf16[256,1024]{1,0:T(8,128)(2,1)}, u32[]{:S(2)}, u32[]{:S(2)}) collective-permute-start(bf16[256,1024]{1,0:T(8,128)(2,1)} %get-tuple-element.96.kt_ref), channel_id=1, source_target_pairs={{0,2},{4,6},{8,10},{12,14},{16,18},{20,22},{24,26},{28,30},{1,3},{... | collective-permute-start | bytes 1572872 | tf_op jit(solution)/shard_map/ppermute | solution.py:799
  23.5 10.7 %collective-permute-start.1 = (bf16[256,1024]{1,0:T(8,128)(2,1)}, bf16[256,1024]{1,0:T(8,128)(2,1)}, u32[]{:S(2)}, u32[]{:S(2)}) collective-permute-start(bf16[256,1024]{1,0:T(8,128)(2,1)} %get-tuple-element.95.vt_ref), channel_id=1, source_target_pairs={{0,2},{4,6},{8,10},{12,14},{16,18},{20,22},{24,26},{28,30},{1,3},{... | collective-permute-start | bytes 1572872 | tf_op jit(solution)/shard_map/ppermute | solution.py:800
  27.3 3.3 copy-start.27
  28.1 3.1 copy-start.21
  28.1 3.1 copy-start.22
  44.2 12.3 %copy-start.7 = (bf16[512,1024]{1,0:T(8,128)(2,1)S(1)}, bf16[512,1024]{1,0:T(8,128)(2,1)}, u32[]{:S(2)}) copy-start(bf16[512,1024]{1,0:T(8,128)(2,1)} %wo_ref.1) | copy-start | bytes 3145732
  44.2 14.3 %collective-permute-start.3 = (bf16[256,1024]{1,0:T(8,128)(2,1)}, bf16[256,1024]{1,0:T(8,128)(2,1)S(1)}, u32[]{:S(2)}, u32[]{:S(2)}) collective-permute-start(bf16[256,1024]{1,0:T(8,128)(2,1)} %get-tuple-element.98.refs_1_), channel_id=1, source_target_pairs={{0,1},{1,0},{2,3},{3,2},{4,5},{5,4},{6,7},{7,6},{8,9},{9,8},{10,11... | collective-permute-start | bytes 1572872 | tf_op jit(solution)/shard_map/ppermute | solution.py:686
  54.7 10.2 %collective-permute-start.2 = (bf16[256,1024]{1,0:T(8,128)(2,1)}, bf16[256,1024]{1,0:T(8,128)(2,1)S(1)}, u32[]{:S(2)}, u32[]{:S(2)}) collective-permute-start(bf16[256,1024]{1,0:T(8,128)(2,1)} %get-tuple-element.97.refs_0_), channel_id=1, source_target_pairs={{0,1},{1,0},{2,3},{3,2},{4,5},{5,4},{6,7},{7,6},{8,9},{9,8},{10,11... | collective-permute-start | bytes 1572872 | tf_op jit(solution)/shard_map/ppermute | solution.py:686
  58.5 6.3 %copy-start.25 = (bf16[256,1024]{1,0:T(8,128)(2,1)}, bf16[256,1024]{1,0:T(8,128)(2,1)S(1)}, u32[]{:S(2)}) copy-start(bf16[256,1024]{1,0:T(8,128)(2,1)S(1)} %collective-permute-done.3.refs_3_) | copy-start | bytes 1572868
  64.9 0.8 copy-start.26
  100.1 35.2 %collective-permute-start.5 = (bf16[8,3,128,1024]{3,2,1,0:T(8,128)(2,1)}, bf16[8,3,128,1024]{3,2,1,0:T(8,128)(2,1)}, u32[]{:S(2)}, u32[]{:S(2)}) collective-permute-start(bf16[8,3,128,1024]{3,2,1,0:T(8,128)(2,1)} %get-tuple-element.102), channel_id=1, source_target_pairs={{0,2},{2,0},{4,6},{6,4},{8,10},{10,8},{12,14},{14,12},{16,18},{18,... | collective-permute-start | bytes 18874376 | tf_op jit(solution)/shard_map/ppermute | solution.py:840
  159.4 266.5 %reduce-scatter.12.cloned.1.call-start = ((), (), s32[]{:S(2)}) async-start(), calls=%async_computation.8 | async-start | bytes 7077888 | tf_op jit(solution)/shard_map/reduce_scatter | solution.py:731
  159.5 23.7 %collective-permute-start.7 = (bf16[8,3,128,1024]{3,2,1,0:T(8,128)(2,1)}, bf16[8,3,128,1024]{3,2,1,0:T(8,128)(2,1)}, u32[]{:S(2)}, u32[]{:S(2)}) collective-permute-start(bf16[8,3,128,1024]{3,2,1,0:T(8,128)(2,1)} %get-tuple-element.113), channel_id=1, source_target_pairs={{0,2},{2,0},{4,6},{6,4},{8,10},{10,8},{12,14},{14,12},{16,18},{18,... | collective-permute-start | bytes 18874376 | tf_op jit(solution)/shard_map/ppermute | solution.py:840
  207.2 243.6 %reduce-scatter.6.cloned.1.call-start = ((), (), s32[]{:S(2)}) async-start(), calls=%async_computation.5 | async-start | bytes 7077888 | tf_op jit(solution)/shard_map/reduce_scatter | solution.py:731
  207.2 24.0 %collective-permute-start.6 = (bf16[8,3,128,1024]{3,2,1,0:T(8,128)(2,1)}, bf16[8,3,128,1024]{3,2,1,0:T(8,128)(2,1)}, u32[]{:S(2)}, u32[]{:S(2)}) collective-permute-start(bf16[8,3,128,1024]{3,2,1,0:T(8,128)(2,1)} %get-tuple-element.112), channel_id=1, source_target_pairs={{0,2},{2,0},{4,6},{6,4},{8,10},{10,8},{12,14},{14,12},{16,18},{18,... | collective-permute-start | bytes 18874376 | tf_op jit(solution)/shard_map/ppermute | solution.py:840
  255.1 0.7 copy-start.20
  255.1 3.1 copy-start.17
  255.1 3.1 copy-start.18
  255.1 3.7 copy-start.14
  255.1 3.7 copy-start.15
  255.2 195.6 %reduce-scatter.8.cloned.1.call-start = ((), (), s32[]{:S(2)}) async-start(), calls=%async_computation.6 | async-start | bytes 7077888 | tf_op jit(solution)/shard_map/reduce_scatter | solution.py:731
  255.2 10.6 %collective-permute-start.8 = (bf16[8,3,128,1024]{3,2,1,0:T(8,128)(2,1)}, bf16[8,3,128,1024]{3,2,1,0:T(8,128)(2,1)}, u32[]{:S(2)}, u32[]{:S(2)}) collective-permute-start(bf16[8,3,128,1024]{3,2,1,0:T(8,128)(2,1)} %get-tuple-element.124), channel_id=1, source_target_pairs={{0,2},{2,0},{4,6},{6,4},{8,10},{10,8},{12,14},{14,12},{16,18},{18,... | collective-permute-start | bytes 18874376 | tf_op jit(solution)/shard_map/ppermute | solution.py:840
  265.8 25.6 %copy-start.13 = (f32[32,1024]{1,0:T(8,128)S(1)}, f32[32,1024]{1,0:T(8,128)}, u32[]{:S(2)}) copy-start(f32[32,1024]{1,0:T(8,128)} %get-tuple-element.99) | copy-start | bytes 393220
  265.8 25.7 %copy-start.16 = (bf16[1024,32]{0,1:T(8,128)(2,1)S(1)}, bf16[1024,32]{0,1:T(8,128)(2,1)}, u32[]{:S(2)}) copy-start(bf16[1024,32]{0,1:T(8,128)(2,1)} %param.30) | copy-start | bytes 196612
  321.4 170.4 %reduce-scatter.14.cloned.1.call-start = ((), (), s32[]{:S(2)}) async-start(), calls=%async_computation.9 | async-start | bytes 2064384 | tf_op jit(solution)/shard_map/reduce_scatter | solution.py:741
  323.5 26.6 %copy-start.2 = (f32[1024,1024]{1,0:T(8,128)S(1)}, f32[1024,1024]{1,0:T(8,128)}, u32[]{:S(2)}) copy-start(f32[1024,1024]{1,0:T(8,128)} %get-tuple-element.133) | copy-start | bytes 12582916
  323.5 27.8 %collective-permute-start.9 = (bf16[512,1024]{1,0:T(8,128)(2,1)S(1)}, bf16[512,1024]{1,0:T(8,128)(2,1)S(1)}, u32[]{:S(2)}, u32[]{:S(2)}) collective-permute-start(bf16[512,1024]{1,0:T(8,128)(2,1)S(1)} %subtract_convert_fusion.1), channel_id=1, source_target_pairs={{0,1},{1,0},{2,3},{3,2},{4,5},{5,4},{6,7},{7,6},{8,9},{9,8},{10,11... | collective-permute-start | bytes 3145736 | tf_op jit(solution)/shard_map/ppermute | solution.py:686
  351.3 25.9 %collective-permute-start.10 = (bf16[512,1024]{1,0:T(8,128)(2,1)S(1)}, bf16[512,1024]{1,0:T(8,128)(2,1)S(1)}, u32[]{:S(2)}, u32[]{:S(2)}) collective-permute-start(bf16[512,1024]{1,0:T(8,128)(2,1)S(1)} %subtract_convert_fusion), channel_id=1, source_target_pairs={{0,1},{1,0},{2,3},{3,2},{4,5},{5,4},{6,7},{7,6},{8,9},{9,8},{10,11... | collective-permute-start | bytes 3145736 | tf_op jit(solution)/shard_map/ppermute | solution.py:686
  378.7 47.2 %collective-permute-start.11 = (bf16[1024,1024]{1,0:T(8,128)(2,1)}, bf16[1024,1024]{1,0:T(8,128)(2,1)}, u32[]{:S(2)}, u32[]{:S(2)}) collective-permute-start(bf16[1024,1024]{1,0:T(8,128)(2,1)} %bitcast_convert_fusion), channel_id=1, source_target_pairs={{0,1},{1,0},{2,3},{3,2},{4,5},{5,4},{6,7},{7,6},{8,9},{9,8},{10,11... | collective-permute-start | bytes 6291464 | tf_op jit(solution)/shard_map/ppermute | solution.py:686
  392.0 26.7 %copy-start.1 = (bf16[1024,1024]{1,0:T(8,128)(2,1)S(1)}, bf16[1024,1024]{1,0:T(8,128)(2,1)}, u32[]{:S(2)}) copy-start(bf16[1024,1024]{1,0:T(8,128)(2,1)} %get-tuple-element.101.x_hbm) | copy-start | bytes 6291460
  415.5 19.0 %collective-permute-start.12 = (bf16[256,1024]{1,0:T(8,128)(2,1)}, bf16[256,1024]{1,0:T(8,128)(2,1)S(1)}, u32[]{:S(2)}, u32[]{:S(2)}) collective-permute-start(bf16[256,1024]{1,0:T(8,128)(2,1)} %get-tuple-element.155), channel_id=1, source_target_pairs={{2,0},{6,4},{10,8},{14,12},{18,16},{22,20},{26,24},{30,28},{3,1},{... | collective-permute-start | bytes 1572872 | tf_op jit(solution)/shard_map/ppermute | solution.py:890
  416.8 19.0 %collective-permute-start.13 = (bf16[256,1024]{1,0:T(8,128)(2,1)}, bf16[256,1024]{1,0:T(8,128)(2,1)S(1)}, u32[]{:S(2)}, u32[]{:S(2)}) collective-permute-start(bf16[256,1024]{1,0:T(8,128)(2,1)} %get-tuple-element.156), channel_id=1, source_target_pairs={{2,0},{6,4},{10,8},{14,12},{18,16},{22,20},{26,24},{30,28},{3,1},{... | collective-permute-start | bytes 1572872 | tf_op jit(solution)/shard_map/ppermute | solution.py:891
  434.5 1.3 copy-start.23
  435.8 0.8 copy-start.24
  450.4 4.2 collective-permute-start.14
  454.5 4.3 copy-start.5
  458.8 66.0 %all-gather.2.cloned.1.call-start = ((), (), s32[]{:S(2)}) async-start(), calls=%async_computation.10 | async-start | bytes 2064384 | tf_op jit(solution)/shard_map/all_gather | solution.py:743
  458.9 2.2 copy-start.3
  459.1 6.8 %copy-start.8 = (bf16[1,3,128,1024]{3,2,1,0:T(8,128)(2,1)S(1)}, bf16[1,3,128,1024]{3,2,1,0:T(8,128)(2,1)}, u32[]{:S(2)}) copy-start(bf16[1,3,128,1024]{3,2,1,0:T(8,128)(2,1)} %reduce-scatter.10.cloned.1.call-done) | copy-start | bytes 2359300
  459.1 6.8 %copy-start.9 = (bf16[1,3,128,1024]{3,2,1,0:T(8,128)(2,1)S(1)}, bf16[1,3,128,1024]{3,2,1,0:T(8,128)(2,1)}, u32[]{:S(2)}) copy-start(bf16[1,3,128,1024]{3,2,1,0:T(8,128)(2,1)} %reduce-scatter.12.cloned.1.call-done) | copy-start | bytes 2359300
  459.1 6.8 %copy-start.10 = (bf16[1,3,128,1024]{3,2,1,0:T(8,128)(2,1)S(1)}, bf16[1,3,128,1024]{3,2,1,0:T(8,128)(2,1)}, u32[]{:S(2)}) copy-start(bf16[1,3,128,1024]{3,2,1,0:T(8,128)(2,1)} %reduce-scatter.6.cloned.1.call-done) | copy-start | bytes 2359300
  459.1 6.8 %copy-start.11 = (bf16[1,3,128,1024]{3,2,1,0:T(8,128)(2,1)S(1)}, bf16[1,3,128,1024]{3,2,1,0:T(8,128)(2,1)}, u32[]{:S(2)}) copy-start(bf16[1,3,128,1024]{3,2,1,0:T(8,128)(2,1)} %reduce-scatter.8.cloned.1.call-done) | copy-start | bytes 2359300
  459.1 25.6 %collective-permute-start.15 = (bf16[512,1024]{1,0:T(8,128)(2,1)S(1)}, bf16[512,1024]{1,0:T(8,128)(2,1)}, u32[]{:S(2)}, u32[]{:S(2)}) collective-permute-start(bf16[512,1024]{1,0:T(8,128)(2,1)S(1)} %get-tuple-element.223), channel_id=1, source_target_pairs={{0,1},{1,0},{2,3},{3,2},{4,5},{5,4},{6,7},{7,6},{8,9},{9,8},{10,11... | collective-permute-start | bytes 3145736 | tf_op jit(solution)/shard_map/ppermute | solution.py:686
  491.8 22.0 %collective-permute-start.16 = (bf16[512,1024]{1,0:T(8,128)(2,1)S(1)}, bf16[512,1024]{1,0:T(8,128)(2,1)}, u32[]{:S(2)}, u32[]{:S(2)}) collective-permute-start(bf16[512,1024]{1,0:T(8,128)(2,1)S(1)} %get-tuple-element.222), channel_id=1, source_target_pairs={{0,1},{1,0},{2,3},{3,2},{4,5},{5,4},{6,7},{7,6},{8,9},{9,8},{10,11... | collective-permute-start | bytes 3145736 | tf_op jit(solution)/shard_map/ppermute | solution.py:686
  524.8 4.9 collective-permute-start.17
  524.8 2.8 copy-start.6
  527.7 2.1 copy-start.12
  530.0 3.2 copy-start.4
  531.7 14.3 %collective-permute-start.18 = (bf16[256,1024]{1,0:T(8,128)(2,1)S(1)}, bf16[256,1024]{1,0:T(8,128)(2,1)S(1)}, u32[]{:S(2)}, u32[]{:S(2)}) collective-permute-start(bf16[256,1024]{1,0:T(8,128)(2,1)S(1)} %get-tuple-element.224), channel_id=1, source_target_pairs={{0,1},{1,0},{2,3},{3,2},{4,5},{5,4},{6,7},{7,6},{8,9},{9,8},{10,11... | collective-permute-start | bytes 1572872 | tf_op jit(solution)/shard_map/ppermute | solution.py:686
Sparse Core Ops, SparseCore 0:
  159.6 69.6 reduce-scatter.9
  231.6 68.2 reduce-scatter.11
  302.2 68.3 reduce-scatter.5
  372.7 68.3 reduce-scatter.7
  458.9 32.7 reduce-scatter.13
  493.1 31.6 all-gather.1
